TPU v7x, 128 devices: a whole 4x4x4 slice. The times are simulated.
128 devices in a mesh: rows: 8 (over y, core), cols: 16 (over x, z).
Axes of the slice: x: 4, y: 4, z: 4, core: 2. Of those that a mesh axis runs over, the one named last changes fastest.
Arguments:
- position: float32 [2048, 3, 256], P(('rows', 'cols')), may hold values from 0 to 1
- velocity: float32 [2048, 3, 256], P(('rows', 'cols')), may hold values from -1.8 to 1.8
- mass: float32 [2048, 256], P(('rows', 'cols')), may hold values from 0.00025 to 0.001
- smoothing: float32 [2048, 256], P(('rows', 'cols')), may hold values from 0.1 to 0.25
- energy: float32 [2048, 256], P(('rows', 'cols')), may hold values from 0.05 to 0.5
- counts: int32 [2048], P(('rows', 'cols')), may hold values from 96 to 256
- proxy_cell: int32 [16384], P(('rows', 'cols')), may hold values from 0 to 15
- proxy_dest: int32 [16384, 1], P(('rows', 'cols')), may hold values from 0 to 127; in each aligned block of 128 rows (0 to 127, 128 to 255, ...) at most 2 rows name the same one
- proxy_target: int32 [16384], P(('rows', 'cols')), may hold values from 0 to 15
- pair_first: int32 [2048], P(('rows', 'cols')), may hold values from 0 to 15
- pair_offset: int32 [2048], P(('rows', 'cols')), may hold values from 1 to 15
- mig_cell: int32 [2048], P(('rows', 'cols')), may hold values from 0 to 15
- mig_dest: int32 [2048, 1], P(('rows', 'cols')), may hold values from 0 to 15; in each aligned block of 16 rows (0 to 15, 16 to 31, ...) at most 2 rows name the same one
Outputs:
- density: float32 [2048, 256], P(('rows', 'cols'))
- accel: float32 [2048, 4, 256], P(('rows', 'cols'))
- arrived: float32 [4096, 9, 256], P(('rows', 'cols'))
Inputs may be any that keep to these rules, and one draw needn't show every extreme that they name: `proxy_dest`: among the 128 entries of one domain no destination appears more than 2 times; in every draw some domain names some destination exactly 2 times. `mig_dest`: among the 16 entries of one domain no column appears more than 2 times; in every draw some domain names some column exactly 2 times.
All inputs are finite; a program needn't handle non-finite values.
Results may differ from a plain program's by a relative error of at most 0.0003.
Values sent between devices are 32-bit elements; how exact they have to be, the bound alone decides.
No kernel may reach another device: no remote copies, remote signals or barrier semaphores. Data moves between devices by JAX's collectives and lax.ppermute only.
A program may use at most 64 MiB of HBM per device.

v0:
```python
import jax
import jax.numpy as jnp
from jax import lax
from jax.sharding import PartitionSpec as P

CAP = 2
CAPM = 2


SIGMA = 0.3183098861837907
GAMMA = 5.0 / 3.0
ALPHA = 1.0
BETA = 2.0
STEP = 0.02
pair_block = 16


def spline(ratio):
    inner = 1.0 - 1.5 * ratio * ratio + 0.75 * ratio * ratio * ratio
    far = jnp.maximum(2.0 - ratio, 0.0)
    return jnp.where(ratio < 1.0, inner, 0.25 * far * far * far)


def slope(ratio):
    inner = -3.0 + 2.25 * ratio
    far = jnp.maximum(2.0 - ratio, 0.0)
    return jnp.where(ratio < 1.0, inner, -0.75 * far * far / jnp.maximum(ratio, 1.0))


def geometry(first, second):
    offsets = first[0:3, :, None] - second[0:3, None, :]
    dist_sq = jnp.sum(offsets * offsets, axis=0)
    pair_h = 0.5 * (first[7][:, None] + second[7][None, :])
    ratio = jnp.sqrt(dist_sq) / pair_h
    return (offsets, dist_sq, pair_h, ratio)


def density_pair(first, second, rho_first, rho_second):
    offsets, dist_sq, pair_h, ratio = geometry(first, second)
    kernel_val = SIGMA * spline(ratio) / (pair_h * pair_h * pair_h)
    return (
        jnp.sum(kernel_val * second[6][None, :], axis=1),
        jnp.sum(kernel_val * first[6][:, None], axis=0),
    )


def force_pair(first, second, rho_first, rho_second):
    offsets, dist_sq, pair_h, ratio = geometry(first, second)
    press_first = (GAMMA - 1.0) * first[8] / rho_first
    press_second = (GAMMA - 1.0) * second[8] / rho_second
    sound_first = jnp.sqrt(GAMMA * (GAMMA - 1.0) * first[8])
    sound_second = jnp.sqrt(GAMMA * (GAMMA - 1.0) * second[8])
    relative = first[3:6, :, None] - second[3:6, None, :]
    approach = jnp.sum(relative * offsets, axis=0)
    converge = pair_h * approach / (dist_sq + 0.01 * pair_h * pair_h)
    mean_sound = 0.5 * (sound_first[:, None] + sound_second[None, :])
    mean_rho = 0.5 * (rho_first[:, None] + rho_second[None, :])
    viscous = jnp.where(
        approach < 0.0,
        (-ALPHA * mean_sound * converge + BETA * converge * converge) / mean_rho,
        0.0,
    )
    scaled = (
        (press_first[:, None] + press_second[None, :] + viscous) * SIGMA * slope(ratio) / pair_h**5
    )
    weight_first = scaled * second[6][None, :]
    weight_second = scaled * first[6][:, None]
    accel_first = -jnp.sum(weight_first[None] * offsets, axis=2)
    accel_second = jnp.sum(weight_second[None] * offsets, axis=1)
    heat_first = 0.5 * jnp.sum(weight_first * approach, axis=1)
    heat_second = 0.5 * jnp.sum(weight_second * approach, axis=0)
    return (
        jnp.concatenate([accel_first, heat_first[None]], axis=0),
        jnp.concatenate([accel_second, heat_second[None]], axis=0),
    )


def run_pairs(kernel, first_cells, second_cells, first_rho, second_rho):

    def blocked(stacked):
        return stacked.reshape((-1, pair_block) + stacked.shape[1:])

    def one_block(block):
        return jax.vmap(kernel)(block[0], block[1], block[2], block[3])

    result = lax.map(
        one_block,
        (blocked(first_cells), blocked(second_cells), blocked(first_rho), blocked(second_rho)),
    )
    return jax.tree.map(lambda stacked: stacked.reshape((-1,) + stacked.shape[2:]), result)


def place_slots(target_dev, peer_count, room):
    hits = (
        target_dev[:, None] == lax.broadcasted_iota(jnp.int32, (target_dev.shape[0], peer_count), 1)
    ).astype(jnp.int32)
    earlier = jnp.cumsum(hits, axis=0) - hits
    return target_dev * room + jnp.sum(earlier * hits, axis=1)


def local(
    position,
    velocity,
    mass,
    smoothing,
    energy,
    counts,
    proxy_cell,
    proxy_dest,
    proxy_target,
    pair_first,
    pair_offset,
    mig_cell,
    mig_dest,
):
    cells_here = position.shape[0]
    particles = position.shape[2]
    all_devices = lax.axis_size(("rows", "cols"))
    col_count = lax.axis_size("cols")
    occupied = lax.broadcasted_iota(jnp.int32, (cells_here, particles), 1) < counts[:, None]
    live_mass = jnp.where(occupied, mass, 0.0)
    cells = jnp.concatenate(
        [position, velocity, live_mass[:, None], smoothing[:, None], energy[:, None]], axis=1
    )
    send_slot = place_slots(proxy_dest[:, 0], all_devices, CAP)
    outgoing = (
        jnp.zeros((all_devices * CAP, 9, particles), jnp.float32)
        .at[send_slot]
        .set(cells[proxy_cell])
    )
    aims = jnp.full((all_devices * CAP,), -1, jnp.int32).at[send_slot].set(proxy_target)
    visitors, goals = (
        lax.all_to_all(
            outgoing.reshape(all_devices, CAP, 9, particles),
            ("rows", "cols"),
            split_axis=0,
            concat_axis=0,
            tiled=True,
        ),
        lax.all_to_all(
            aims.reshape(all_devices, CAP),
            ("rows", "cols"),
            split_axis=0,
            concat_axis=0,
            tiled=True,
        ),
    )
    visitors = visitors.reshape(all_devices * CAP, 9, particles)
    goals = goals.reshape(all_devices * CAP)
    present = (goals >= 0).astype(jnp.float32)
    anchor = jnp.maximum(goals, 0)
    second_local = (pair_first + pair_offset) % cells_here
    local_count = pair_first.shape[0]
    split_at = cells_here + local_count
    first_cells = jnp.concatenate([cells, cells[pair_first], visitors], axis=0)
    second_cells = jnp.concatenate([cells, cells[second_local], cells[anchor]], axis=0)
    index_all = jnp.concatenate(
        [jnp.arange(cells_here, dtype=jnp.int32), pair_first, second_local, anchor]
    )
    keep_all = jnp.concatenate([jnp.ones((cells_here + 2 * local_count,), jnp.float32), present])
    fold = (
        lax.broadcasted_iota(jnp.int32, (cells_here, index_all.shape[0]), 0) == index_all[None, :]
    ).astype(jnp.float32) * keep_all[None, :]
    sender_fold = (
        lax.broadcasted_iota(jnp.int32, (cells_here, proxy_cell.shape[0]), 0) == proxy_cell[None, :]
    ).astype(jnp.float32)
    unit_rho = jnp.ones((first_cells.shape[0], particles), jnp.float32)
    rho_first, rho_second = run_pairs(density_pair, first_cells, second_cells, unit_rho, unit_rho)
    own_terms = jnp.concatenate([rho_first[:split_at], rho_second[cells_here:]], axis=0)
    partial_rho = jnp.dot(fold, own_terms, precision=lax.Precision.HIGHEST)
    returned_rho = lax.all_to_all(
        rho_first[split_at:].reshape(all_devices, CAP, particles),
        ("rows", "cols"),
        split_axis=0,
        concat_axis=0,
        tiled=True,
    )
    returned_rho = returned_rho.reshape(all_devices * CAP, particles)[send_slot]
    density_raw = partial_rho + jnp.dot(sender_fold, returned_rho, precision=lax.Precision.HIGHEST)
    rho = jnp.where(occupied, density_raw, 1.0)
    rho_out = (
        jnp.ones((all_devices * CAP, particles), jnp.float32).at[send_slot].set(rho[proxy_cell])
    )
    visitor_rho = lax.all_to_all(
        rho_out.reshape(all_devices, CAP, particles),
        ("rows", "cols"),
        split_axis=0,
        concat_axis=0,
        tiled=True,
    )
    visitor_rho = visitor_rho.reshape(all_devices * CAP, particles)
    first_rho = jnp.concatenate([rho, rho[pair_first], visitor_rho], axis=0)
    second_rho = jnp.concatenate([rho, rho[second_local], rho[anchor]], axis=0)
    force_first, force_second = run_pairs(
        force_pair, first_cells, second_cells, first_rho, second_rho
    )
    own_force = jnp.concatenate([force_first[:split_at], force_second[cells_here:]], axis=0)
    partial_force = jnp.einsum("cn,nkp->ckp", fold, own_force, precision=lax.Precision.HIGHEST)
    returned_force = lax.all_to_all(
        force_first[split_at:].reshape(all_devices, CAP, 4, particles),
        ("rows", "cols"),
        split_axis=0,
        concat_axis=0,
        tiled=True,
    )
    returned_force = returned_force.reshape(all_devices * CAP, 4, particles)[send_slot]
    total_force = partial_force + jnp.einsum(
        "cs,skp->ckp", sender_fold, returned_force, precision=lax.Precision.HIGHEST
    )
    accel = jnp.where(occupied[:, None, :], total_force, 0.0)
    density = jnp.where(occupied, density_raw, 0.0)
    new_vel = velocity + STEP * accel[:, 0:3]
    new_pos = position + STEP * new_vel
    new_energy = energy + STEP * accel[:, 3]
    kicked = jnp.concatenate(
        [new_pos, new_vel, live_mass[:, None], smoothing[:, None], new_energy[:, None]], axis=1
    )
    kicked = kicked * occupied[:, None, :].astype(jnp.float32)
    move_slot = place_slots(mig_dest[:, 0], col_count, CAPM)
    leaving = (
        jnp.zeros((col_count * CAPM, 9, particles), jnp.float32).at[move_slot].set(kicked[mig_cell])
    )
    arrived = lax.all_to_all(
        leaving.reshape(col_count, CAPM, 9, particles),
        "cols",
        split_axis=0,
        concat_axis=0,
        tiled=True,
    )
    return (density, accel, arrived.reshape(col_count * CAPM, 9, particles))


def solution(mesh):
    placed = (
        P(("rows", "cols"), None, None),
        P(("rows", "cols"), None, None),
        P(("rows", "cols"), None),
        P(("rows", "cols"), None),
        P(("rows", "cols"), None),
        P(("rows", "cols")),
        P(("rows", "cols")),
        P(("rows", "cols"), None),
        P(("rows", "cols")),
        P(("rows", "cols")),
        P(("rows", "cols")),
        P(("rows", "cols")),
        P(("rows", "cols"), None),
    )
    return jax.shard_map(
        local,
        mesh=mesh,
        in_specs=placed,
        out_specs=(
            P(("rows", "cols"), None),
            P(("rows", "cols"), None, None),
            P(("rows", "cols"), None, None),
        ),
        check_vma=False,
    )
```

profile of v0, /device:TPU:0, one launch (start us, length us, event | category | flops | bytes accessed | tf_op | source)
XLA Modules:
  0.0 758.3 jit_solution(18112888276579095713)
XLA Ops:
  4.9 11.1 %all-to-all-start = ((s32[128,1,2]{2,1,0:T(1,128)}), s32[128,1,2]{2,1,0:T(1,128)S(1)}, u32[]{:S(2)}, u32[]{:S(2)}) async-start(s32[128,1,2]{2,1,0:T(1,128)} %bitcast.27), calls=%async_computation | async-start | bytes 131072 | tf_op jit(solution)/shard_map/all_to_all | solution.py:140
  25.4 15.7 %scatter_fusion = f32[256,9,256]{2,1,0:T(8,128)} fusion(f32[256,9,256]{2,1,0:T(8,128)} %broadcast_in_dim.120, s32[128]{0:T(128)S(1)} %fusion.66, f32[128,9,256]{2,1,0:T(8,128)S(1)} %gather_fusion.1), kind=kCustom, calls=%fused_computation.12 | custom fusion | bytes 3539456 | tf_op jit(solution)/shard_map/scatter | solution.py:129
  41.1 5.9 copy.82
  47.0 9.9 %all-to-all-start.1 = ((f32[128,2,9,256]{3,1,2,0:T(2,128)}), f32[128,2,9,256]{3,1,2,0:T(2,128)S(1)}, u32[]{:S(2)}, u32[]{:S(2)}) async-start(f32[128,2,9,256]{3,1,2,0:T(2,128)} %copy.82), calls=%async_computation.1 | async-start | bytes 4718592 | tf_op jit(solution)/shard_map/all_to_all | solution.py:133
  69.2 20.1 %all-to-all-done.1 = f32[128,2,9,256]{3,1,2,0:T(2,128)S(1)} async-done(((f32[128,2,9,256]{3,1,2,0:T(2,128)}), f32[128,2,9,256]{3,1,2,0:T(2,128)S(1)}, u32[]{:S(2)}, u32[]{:S(2)}) %all-to-all-start.1) | async-done | bytes 2359328 | tf_op jit(solution)/shard_map/all_to_all | solution.py:133
  96.1 157.1 %while.26 = (s32[]{:T(128)}, f32[18,16,256]{2,1,0:T(8,128)S(1)}, f32[18,16,256]{2,1,0:T(8,128)S(1)}, f32[18,16,9,256]{3,1,2,0:T(8,128)S(1)}, f32[18,16,9,256]{3,1,2,0:T(8,128)}, /*index=5*/s32[]{:T(128)}) while((s32[]{:T(128)}, f32[18,16,256]{2,1,0:T(8,128)S(1)}, f32[18,16,256]{2,1,0:T(8,128)S(1)}, f32[18,16,9,256]{3,1,2,0:T(8,128)S(1)}, ...), condition=%wide.region_8.9_spmd, body=%wide.region_4.8_spmd.sunk | while | flops 34594816 | bytes 9764945 | solution.py:86
  99.3 5.4 multiply_reduce_fusion.9
  108.1 5.4 multiply_reduce_fusion.9
  116.8 5.4 multiply_reduce_fusion.9
  259.8 9.8 %all-to-all-done.2 = f32[128,2,256]{2,1,0:T(2,128)S(1)} async-done(((f32[128,2,256]{2,1,0:T(2,128)}), f32[128,2,256]{2,1,0:T(2,128)S(1)}, u32[]{:S(2)}, u32[]{:S(2)}) %all-to-all-start.2) | async-done | bytes 262176 | tf_op jit(solution)/shard_map/all_to_all | solution.py:171
  281.0 8.5 %all-to-all-done.3 = f32[128,2,256]{2,1,0:T(2,128)S(1)} async-done(((f32[128,2,256]{2,1,0:T(2,128)}), f32[128,2,256]{2,1,0:T(2,128)S(1)}, u32[]{:S(2)}, u32[]{:S(2)}) %all-to-all-start.3) | async-done | bytes 262176 | tf_op jit(solution)/shard_map/all_to_all | solution.py:184
  290.5 424.1 %while.27 = (s32[]{:T(128)}, f32[18,16,4,256]{3,2,1,0:T(4,128)}, f32[18,16,4,256]{3,2,1,0:T(4,128)}, f32[18,16,9,256]{3,1,2,0:T(8,128)S(1)}, f32[18,16,256]{2,1,...) while((s32[]{:T(128)}, f32[18,16,4,256]{3,2,1,0:T(4,128)}, ...), condition=%wide.region_17.18_spmd, body=%wide.region_10.17_spmd.sunk | while | flops 76591104 | bytes 36340836 | solution.py:86
  298.3 9.0 %multiply_reduce_fusion.10 = (f32[16,256]{1,0:T(8,128)S(1)}, f32[16,256]{1,0:T(8,128)S(1)}, f32[16,256,256]{2,1,0:T(8,128)S(1)}, f32[16,256,256]{2,1,0:T(8,128)S(1)}) fusion(f32[16,256,256]{2,1,0:T(8,128)S(1)} %get-tuple-element.373, f32[16,256]{1,0:T(8,128)S(1)} %get-tuple-element.374, f32[16,256]{1,0:T(8,128)S(1)} %get-tuple-element.375, ...), kind=kLoop, calls=%fused_computation.64.clone.1 | loop fusion | flops 44032000 | bytes 16973824 | tf_op jit(solution)/shard_map/while/body/eval_jaxpr/vmap()/reduce_sum | solution.py:71
  321.9 9.0 %multiply_reduce_fusion.10 = (f32[16,256]{1,0:T(8,128)S(1)}, f32[16,256]{1,0:T(8,128)S(1)}, f32[16,256,256]{2,1,0:T(8,128)S(1)}, f32[16,256,256]{2,1,0:T(8,128)S(1)}) fusion(f32[16,256,256]{2,1,0:T(8,128)S(1)} %get-tuple-element.373, f32[16,256]{1,0:T(8,128)S(1)} %get-tuple-element.374, f32[16,256]{1,0:T(8,128)S(1)} %get-tuple-element.375, ...), kind=kLoop, calls=%fused_computation.64.clone.1 | loop fusion | flops 44032000 | bytes 16973824 | tf_op jit(solution)/shard_map/while/body/eval_jaxpr/vmap()/reduce_sum | solution.py:71
  345.5 9.0 %multiply_reduce_fusion.10 = (f32[16,256]{1,0:T(8,128)S(1)}, f32[16,256]{1,0:T(8,128)S(1)}, f32[16,256,256]{2,1,0:T(8,128)S(1)}, f32[16,256,256]{2,1,0:T(8,128)S(1)}) fusion(f32[16,256,256]{2,1,0:T(8,128)S(1)} %get-tuple-element.373, f32[16,256]{1,0:T(8,128)S(1)} %get-tuple-element.374, f32[16,256]{1,0:T(8,128)S(1)} %get-tuple-element.375, ...), kind=kLoop, calls=%fused_computation.64.clone.1 | loop fusion | flops 44032000 | bytes 16973824 | tf_op jit(solution)/shard_map/while/body/eval_jaxpr/vmap()/reduce_sum | solution.py:71
  369.0 9.0 %multiply_reduce_fusion.10 = (f32[16,256]{1,0:T(8,128)S(1)}, f32[16,256]{1,0:T(8,128)S(1)}, f32[16,256,256]{2,1,0:T(8,128)S(1)}, f32[16,256,256]{2,1,0:T(8,128)S(1)}) fusion(f32[16,256,256]{2,1,0:T(8,128)S(1)} %get-tuple-element.373, f32[16,256]{1,0:T(8,128)S(1)} %get-tuple-element.374, f32[16,256]{1,0:T(8,128)S(1)} %get-tuple-element.375, ...), kind=kLoop, calls=%fused_computation.64.clone.1 | loop fusion | flops 44032000 | bytes 16973824 | tf_op jit(solution)/shard_map/while/body/eval_jaxpr/vmap()/reduce_sum | solution.py:71
  392.6 9.0 %multiply_reduce_fusion.10 = (f32[16,256]{1,0:T(8,128)S(1)}, f32[16,256]{1,0:T(8,128)S(1)}, f32[16,256,256]{2,1,0:T(8,128)S(1)}, f32[16,256,256]{2,1,0:T(8,128)S(1)}) fusion(f32[16,256,256]{2,1,0:T(8,128)S(1)} %get-tuple-element.373, f32[16,256]{1,0:T(8,128)S(1)} %get-tuple-element.374, f32[16,256]{1,0:T(8,128)S(1)} %get-tuple-element.375, ...), kind=kLoop, calls=%fused_computation.64.clone.1 | loop fusion | flops 44032000 | bytes 16973824 | tf_op jit(solution)/shard_map/while/body/eval_jaxpr/vmap()/reduce_sum | solution.py:71
  416.1 9.0 %multiply_reduce_fusion.10 = (f32[16,256]{1,0:T(8,128)S(1)}, f32[16,256]{1,0:T(8,128)S(1)}, f32[16,256,256]{2,1,0:T(8,128)S(1)}, f32[16,256,256]{2,1,0:T(8,128)S(1)}) fusion(f32[16,256,256]{2,1,0:T(8,128)S(1)} %get-tuple-element.373, f32[16,256]{1,0:T(8,128)S(1)} %get-tuple-element.374, f32[16,256]{1,0:T(8,128)S(1)} %get-tuple-element.375, ...), kind=kLoop, calls=%fused_computation.64.clone.1 | loop fusion | flops 44032000 | bytes 16973824 | tf_op jit(solution)/shard_map/while/body/eval_jaxpr/vmap()/reduce_sum | solution.py:71
  439.7 9.0 %multiply_reduce_fusion.10 = (f32[16,256]{1,0:T(8,128)S(1)}, f32[16,256]{1,0:T(8,128)S(1)}, f32[16,256,256]{2,1,0:T(8,128)S(1)}, f32[16,256,256]{2,1,0:T(8,128)S(1)}) fusion(f32[16,256,256]{2,1,0:T(8,128)S(1)} %get-tuple-element.373, f32[16,256]{1,0:T(8,128)S(1)} %get-tuple-element.374, f32[16,256]{1,0:T(8,128)S(1)} %get-tuple-element.375, ...), kind=kLoop, calls=%fused_computation.64.clone.1 | loop fusion | flops 44032000 | bytes 16973824 | tf_op jit(solution)/shard_map/while/body/eval_jaxpr/vmap()/reduce_sum | solution.py:71
  463.3 9.0 %multiply_reduce_fusion.10 = (f32[16,256]{1,0:T(8,128)S(1)}, f32[16,256]{1,0:T(8,128)S(1)}, f32[16,256,256]{2,1,0:T(8,128)S(1)}, f32[16,256,256]{2,1,0:T(8,128)S(1)}) fusion(f32[16,256,256]{2,1,0:T(8,128)S(1)} %get-tuple-element.373, f32[16,256]{1,0:T(8,128)S(1)} %get-tuple-element.374, f32[16,256]{1,0:T(8,128)S(1)} %get-tuple-element.375, ...), kind=kLoop, calls=%fused_computation.64.clone.1 | loop fusion | flops 44032000 | bytes 16973824 | tf_op jit(solution)/shard_map/while/body/eval_jaxpr/vmap()/reduce_sum | solution.py:71
  486.8 9.0 %multiply_reduce_fusion.10 = (f32[16,256]{1,0:T(8,128)S(1)}, f32[16,256]{1,0:T(8,128)S(1)}, f32[16,256,256]{2,1,0:T(8,128)S(1)}, f32[16,256,256]{2,1,0:T(8,128)S(1)}) fusion(f32[16,256,256]{2,1,0:T(8,128)S(1)} %get-tuple-element.373, f32[16,256]{1,0:T(8,128)S(1)} %get-tuple-element.374, f32[16,256]{1,0:T(8,128)S(1)} %get-tuple-element.375, ...), kind=kLoop, calls=%fused_computation.64.clone.1 | loop fusion | flops 44032000 | bytes 16973824 | tf_op jit(solution)/shard_map/while/body/eval_jaxpr/vmap()/reduce_sum | solution.py:71
  510.4 9.0 %multiply_reduce_fusion.10 = (f32[16,256]{1,0:T(8,128)S(1)}, f32[16,256]{1,0:T(8,128)S(1)}, f32[16,256,256]{2,1,0:T(8,128)S(1)}, f32[16,256,256]{2,1,0:T(8,128)S(1)}) fusion(f32[16,256,256]{2,1,0:T(8,128)S(1)} %get-tuple-element.373, f32[16,256]{1,0:T(8,128)S(1)} %get-tuple-element.374, f32[16,256]{1,0:T(8,128)S(1)} %get-tuple-element.375, ...), kind=kLoop, calls=%fused_computation.64.clone.1 | loop fusion | flops 44032000 | bytes 16973824 | tf_op jit(solution)/shard_map/while/body/eval_jaxpr/vmap()/reduce_sum | solution.py:71
  533.9 9.0 %multiply_reduce_fusion.10 = (f32[16,256]{1,0:T(8,128)S(1)}, f32[16,256]{1,0:T(8,128)S(1)}, f32[16,256,256]{2,1,0:T(8,128)S(1)}, f32[16,256,256]{2,1,0:T(8,128)S(1)}) fusion(f32[16,256,256]{2,1,0:T(8,128)S(1)} %get-tuple-element.373, f32[16,256]{1,0:T(8,128)S(1)} %get-tuple-element.374, f32[16,256]{1,0:T(8,128)S(1)} %get-tuple-element.375, ...), kind=kLoop, calls=%fused_computation.64.clone.1 | loop fusion | flops 44032000 | bytes 16973824 | tf_op jit(solution)/shard_map/while/body/eval_jaxpr/vmap()/reduce_sum | solution.py:71
  557.5 9.0 %multiply_reduce_fusion.10 = (f32[16,256]{1,0:T(8,128)S(1)}, f32[16,256]{1,0:T(8,128)S(1)}, f32[16,256,256]{2,1,0:T(8,128)S(1)}, f32[16,256,256]{2,1,0:T(8,128)S(1)}) fusion(f32[16,256,256]{2,1,0:T(8,128)S(1)} %get-tuple-element.373, f32[16,256]{1,0:T(8,128)S(1)} %get-tuple-element.374, f32[16,256]{1,0:T(8,128)S(1)} %get-tuple-element.375, ...), kind=kLoop, calls=%fused_computation.64.clone.1 | loop fusion | flops 44032000 | bytes 16973824 | tf_op jit(solution)/shard_map/while/body/eval_jaxpr/vmap()/reduce_sum | solution.py:71
  581.0 9.0 %multiply_reduce_fusion.10 = (f32[16,256]{1,0:T(8,128)S(1)}, f32[16,256]{1,0:T(8,128)S(1)}, f32[16,256,256]{2,1,0:T(8,128)S(1)}, f32[16,256,256]{2,1,0:T(8,128)S(1)}) fusion(f32[16,256,256]{2,1,0:T(8,128)S(1)} %get-tuple-element.373, f32[16,256]{1,0:T(8,128)S(1)} %get-tuple-element.374, f32[16,256]{1,0:T(8,128)S(1)} %get-tuple-element.375, ...), kind=kLoop, calls=%fused_computation.64.clone.1 | loop fusion | flops 44032000 | bytes 16973824 | tf_op jit(solution)/shard_map/while/body/eval_jaxpr/vmap()/reduce_sum | solution.py:71
  604.6 9.0 %multiply_reduce_fusion.10 = (f32[16,256]{1,0:T(8,128)S(1)}, f32[16,256]{1,0:T(8,128)S(1)}, f32[16,256,256]{2,1,0:T(8,128)S(1)}, f32[16,256,256]{2,1,0:T(8,128)S(1)}) fusion(f32[16,256,256]{2,1,0:T(8,128)S(1)} %get-tuple-element.373, f32[16,256]{1,0:T(8,128)S(1)} %get-tuple-element.374, f32[16,256]{1,0:T(8,128)S(1)} %get-tuple-element.375, ...), kind=kLoop, calls=%fused_computation.64.clone.1 | loop fusion | flops 44032000 | bytes 16973824 | tf_op jit(solution)/shard_map/while/body/eval_jaxpr/vmap()/reduce_sum | solution.py:71
  628.2 9.0 %multiply_reduce_fusion.10 = (f32[16,256]{1,0:T(8,128)S(1)}, f32[16,256]{1,0:T(8,128)S(1)}, f32[16,256,256]{2,1,0:T(8,128)S(1)}, f32[16,256,256]{2,1,0:T(8,128)S(1)}) fusion(f32[16,256,256]{2,1,0:T(8,128)S(1)} %get-tuple-element.373, f32[16,256]{1,0:T(8,128)S(1)} %get-tuple-element.374, f32[16,256]{1,0:T(8,128)S(1)} %get-tuple-element.375, ...), kind=kLoop, calls=%fused_computation.64.clone.1 | loop fusion | flops 44032000 | bytes 16973824 | tf_op jit(solution)/shard_map/while/body/eval_jaxpr/vmap()/reduce_sum | solution.py:71
  651.7 9.0 %multiply_reduce_fusion.10 = (f32[16,256]{1,0:T(8,128)S(1)}, f32[16,256]{1,0:T(8,128)S(1)}, f32[16,256,256]{2,1,0:T(8,128)S(1)}, f32[16,256,256]{2,1,0:T(8,128)S(1)}) fusion(f32[16,256,256]{2,1,0:T(8,128)S(1)} %get-tuple-element.373, f32[16,256]{1,0:T(8,128)S(1)} %get-tuple-element.374, f32[16,256]{1,0:T(8,128)S(1)} %get-tuple-element.375, ...), kind=kLoop, calls=%fused_computation.64.clone.1 | loop fusion | flops 44032000 | bytes 16973824 | tf_op jit(solution)/shard_map/while/body/eval_jaxpr/vmap()/reduce_sum | solution.py:71
  675.3 9.0 %multiply_reduce_fusion.10 = (f32[16,256]{1,0:T(8,128)S(1)}, f32[16,256]{1,0:T(8,128)S(1)}, f32[16,256,256]{2,1,0:T(8,128)S(1)}, f32[16,256,256]{2,1,0:T(8,128)S(1)}) fusion(f32[16,256,256]{2,1,0:T(8,128)S(1)} %get-tuple-element.373, f32[16,256]{1,0:T(8,128)S(1)} %get-tuple-element.374, f32[16,256]{1,0:T(8,128)S(1)} %get-tuple-element.375, ...), kind=kLoop, calls=%fused_computation.64.clone.1 | loop fusion | flops 44032000 | bytes 16973824 | tf_op jit(solution)/shard_map/while/body/eval_jaxpr/vmap()/reduce_sum | solution.py:71
  698.8 9.0 %multiply_reduce_fusion.10 = (f32[16,256]{1,0:T(8,128)S(1)}, f32[16,256]{1,0:T(8,128)S(1)}, f32[16,256,256]{2,1,0:T(8,128)S(1)}, f32[16,256,256]{2,1,0:T(8,128)S(1)}) fusion(f32[16,256,256]{2,1,0:T(8,128)S(1)} %get-tuple-element.373, f32[16,256]{1,0:T(8,128)S(1)} %get-tuple-element.374, f32[16,256]{1,0:T(8,128)S(1)} %get-tuple-element.375, ...), kind=kLoop, calls=%fused_computation.64.clone.1 | loop fusion | flops 44032000 | bytes 16973824 | tf_op jit(solution)/shard_map/while/body/eval_jaxpr/vmap()/reduce_sum | solution.py:71
  724.4 16.4 %all-to-all-done.4 = f32[128,2,4,256]{3,2,1,0:T(4,128)S(1)} async-done(((f32[128,2,4,256]{3,2,1,0:T(4,128)}), f32[128,2,4,256]{3,2,1,0:T(4,128)S(1)}, u32[]{:S(2)}, u32[]{:S(2)}) %all-to-all-start.4) | async-done | bytes 1048608 | tf_op jit(solution)/shard_map/all_to_all | solution.py:199
  749.3 7.9 %all-to-all-done.5 = f32[16,2,9,256]{3,1,2,0:T(2,128)S(1)} async-done(((f32[16,2,9,256]{3,1,2,0:T(2,128)}), f32[16,2,9,256]{3,1,2,0:T(2,128)S(1)}, u32[]{:S(2)}, u32[]{:S(2)}) %all-to-all-start.5) | async-done | bytes 294944 | tf_op jit(solution)/shard_map/all_to_all | solution.py:223
  (684 shorter events, 470.2 us)
Async XLA Ops:
  3.0 55.3 %copy-start.13 = (s32[128]{0:T(128)}, s32[128]{0:T(128)S(1)}, u32[]{:S(2)}) copy-start(s32[128]{0:T(128)S(1)} %fusion.66) | copy-start | bytes 1540
  4.9 42.1 %all-to-all-start = ((s32[128,1,2]{2,1,0:T(1,128)}), s32[128,1,2]{2,1,0:T(1,128)S(1)}, u32[]{:S(2)}, u32[]{:S(2)}) async-start(s32[128,1,2]{2,1,0:T(1,128)} %bitcast.27), calls=%async_computation | async-start | bytes 131072 | tf_op jit(solution)/shard_map/all_to_all | solution.py:140
  18.8 6.6 copy-start.12
  18.8 38.3 %copy-start.10 = (s32[1024]{0:T(1024)}, s32[1024]{0:T(1024)S(1)}, u32[]{:S(2)}) copy-start(s32[1024]{0:T(1024)S(1)} %get-tuple-element.252) | copy-start | bytes 12292
  47.0 11.4 %copy-start.18 = (s32[16]{0:T(128)S(1)}, s32[16]{0:T(128)}, u32[]{:S(2)}) copy-start(s32[16]{0:T(128)} %param.28) | copy-start | bytes 196
  47.0 42.3 %all-to-all-start.1 = ((f32[128,2,9,256]{3,1,2,0:T(2,128)}), f32[128,2,9,256]{3,1,2,0:T(2,128)S(1)}, u32[]{:S(2)}, u32[]{:S(2)}) async-start(f32[128,2,9,256]{3,1,2,0:T(2,128)} %copy.82), calls=%async_computation.1 | async-start | bytes 4718592 | tf_op jit(solution)/shard_map/all_to_all | solution.py:133
  57.7 4.6 copy-start.11
  94.8 1.0 copy-start.2
  95.1 1.0 copy-start.4
  96.0 162.7 %copy-start.14 = (s32[16]{0:T(128)S(1)}, s32[16]{0:T(128)}, u32[]{:S(2)}) copy-start(s32[16]{0:T(128)} %param.26) | copy-start | bytes 196
  96.0 162.7 %copy-start.16 = (s32[16]{0:T(128)S(1)}, s32[16]{0:T(128)}, u32[]{:S(2)}) copy-start(s32[16]{0:T(128)} %get-tuple-element.223) | copy-start | bytes 196
  253.2 0.9 copy-start.3
  253.2 17.4 %copy-start.9 = (s32[16]{0:T(128)S(1)}, s32[16]{0:T(128)}, u32[]{:S(2)}) copy-start(s32[16]{0:T(128)} %param.22) | copy-start | bytes 196
  253.2 17.4 %copy-start.17 = (s32[128]{0:T(128)S(1)}, s32[128]{0:T(128)}, u32[]{:S(2)}) copy-start(s32[128]{0:T(128)} %param.23) | copy-start | bytes 1540
  254.1 15.5 %all-to-all-start.2 = ((f32[128,2,256]{2,1,0:T(2,128)}), f32[128,2,256]{2,1,0:T(2,128)S(1)}, u32[]{:S(2)}, u32[]{:S(2)}) async-start(f32[128,2,256]{2,1,0:T(2,128)} %reshape.249), calls=%async_computation.2 | async-start | bytes 524288 | tf_op jit(solution)/shard_map/all_to_all | solution.py:171
  273.8 15.7 %all-to-all-start.3 = ((f32[128,2,256]{2,1,0:T(2,128)}), f32[128,2,256]{2,1,0:T(2,128)S(1)}, u32[]{:S(2)}, u32[]{:S(2)}) async-start(f32[128,2,256]{2,1,0:T(2,128)} %reshape.251), calls=%async_computation.3 | async-start | bytes 524288 | tf_op jit(solution)/shard_map/all_to_all | solution.py:184
  714.6 7.2 copy-start.15
  714.6 8.5 %copy-start = (f32[18,16,4,256]{3,2,1,0:T(4,128)S(1)}, f32[18,16,4,256]{3,2,1,0:T(4,128)}, u32[]{:S(2)}) copy-start(f32[18,16,4,256]{3,2,1,0:T(4,128)} %get-tuple-element.125) | copy-start | bytes 3538948
  717.2 23.7 %all-to-all-start.4 = ((f32[128,2,4,256]{3,2,1,0:T(4,128)}), f32[128,2,4,256]{3,2,1,0:T(4,128)S(1)}, u32[]{:S(2)}, u32[]{:S(2)}) async-start(f32[128,2,4,256]{3,2,1,0:T(4,128)} %bitcast.41), calls=%async_computation.4 | async-start | bytes 2097152 | tf_op jit(solution)/shard_map/all_to_all | solution.py:199
  721.8 20.3 %copy-start.1 = (f32[16,3,256]{2,0,1:T(8,128)S(1)}, f32[16,3,256]{2,0,1:T(8,128)}, u32[]{:S(2)}) copy-start(f32[16,3,256]{2,0,1:T(8,128)} %param.18) | copy-start | bytes 147460
  721.8 20.3 %copy-start.5 = (f32[16,3,256]{2,0,1:T(8,128)S(1)}, f32[16,3,256]{2,0,1:T(8,128)}, u32[]{:S(2)}) copy-start(f32[16,3,256]{2,0,1:T(8,128)} %param.17) | copy-start | bytes 147460
  721.9 20.2 %copy-start.7 = (f32[16,256]{1,0:T(8,128)S(1)}, f32[16,256]{1,0:T(8,128)}, u32[]{:S(2)}) copy-start(f32[16,256]{1,0:T(8,128)} %param.19) | copy-start | bytes 49156
  722.2 20.0 %copy-start.8 = (f32[16,256]{1,0:T(8,128)S(1)}, f32[16,256]{1,0:T(8,128)}, u32[]{:S(2)}) copy-start(f32[16,256]{1,0:T(8,128)} %param.20) | copy-start | bytes 49156
  722.2 20.0 %copy-start.6 = (f32[16,256]{1,0:T(8,128)S(1)}, f32[16,256]{1,0:T(8,128)}, u32[]{:S(2)}) copy-start(f32[16,256]{1,0:T(8,128)} %param.21) | copy-start | bytes 49156
  745.1 12.2 %all-to-all-start.5 = ((f32[16,2,9,256]{3,1,2,0:T(2,128)}), f32[16,2,9,256]{3,1,2,0:T(2,128)S(1)}, u32[]{:S(2)}, u32[]{:S(2)}) async-start(f32[16,2,9,256]{3,1,2,0:T(2,128)} %copy.94), calls=%async_computation.5 | async-start | bytes 589824 | tf_op jit(solution)/shard_map/all_to_all | solution.py:223
where the time goes:
time: 765 us; the launch traced here: 758 us
  other arithmetic  536 us (70%)
  local copies, waits for them, and re-layouts  114 us (15%)
  waiting for transfers between devices  62.8 us (8%)
  starting transfers between devices  38.7 us (5%)
    reduce_sum x18, other arithmetic, force_pair(): heat_second = 0.5 * jnp.sum(weight_second * approach, axis=0)  161 us
    reduce_sum x18, other arithmetic, density_pair(): jnp.sum(kernel_val * first[6][:, None], axis=0)  97 us
    reduce_sum x18, other arithmetic, force_pair(): accel_second = jnp.sum(weight_second[None] * offsets, axis=1)  97 us
    reduce_sum x18, other arithmetic, force_pair(): approach = jnp.sum(relative * offsets, axis=0)  79.6 us
    reduce_sum x18, other arithmetic, geometry(): dist_sq = jnp.sum(offsets * offsets, axis=0)  39.6 us
    squeeze x36, local copies, waits for them, and re-layouts, run_pairs(): lax.map(one_block, (blocked(first_cells), blocked(second_cells), blocked(...  33.5 us
    dynamic_update_slice x36, other arithmetic, run_pairs(): lax.map(one_block, (blocked(first_cells), blocked(second_cells), blocked(...  23.6 us
    all_to_all x1, waiting for transfers between devices, local(): lax.all_to_all(outgoing.reshape(all_devices, CAP, 9, particles), ('rows',...  20.1 us
  transfers between devices with their start and end apart: 6, of which 5 were waited for; matrix products, arithmetic and copies ran while one was open for 7% of the time, Pallas kernels for 0%

commit v1 on v0

v1 whole, which is shorter than its diff:
```python
import jax
import jax.numpy as jnp
from jax import lax
from jax.experimental import pallas as pl
from jax.experimental.pallas import tpu as pltpu
from jax.sharding import PartitionSpec as P

CAP = 2
CAPM = 2
CELLS = 16
SEND = 128
PAIRS = 16
PART = 256

GAMMA = 5.0 / 3.0
STEP = 0.02
PI = 3.141592653589793
W_SCALE = 2.0 / PI
K_SCALE = -24.0 / PI
TINY = 1e-12
CHUNK = 32

f32, bf16, i32 = jnp.float32, jnp.bfloat16, jnp.int32
VMEM = pl.BlockSpec(memory_space=pltpu.VMEM)
SMEM = pl.BlockSpec(memory_space=pltpu.SMEM)
LIMIT = 56 * 2**20


def shape(*dims, dtype=f32):
    return jax.ShapeDtypeStruct(dims, dtype)


def kernel_call(body, out_shape, in_specs, out_specs, scratch=(), flops=0, moved=0):
    return pl.pallas_call(
        body,
        out_shape=out_shape,
        in_specs=in_specs,
        out_specs=out_specs,
        scratch_shapes=list(scratch),
        compiler_params=pltpu.CompilerParams(vmem_limit_bytes=LIMIT),
        cost_estimate=pl.CostEstimate(flops=flops, bytes_accessed=moved, transcendentals=0),
    )


def sublane():
    return lax.broadcasted_iota(i32, (8, PART), 0)


def split3(x):
    a = x.astype(bf16).astype(f32)
    b = (x - a).astype(bf16).astype(f32)
    return a, b, x - a - b


def left_parts(x):
    a, b, c = split3(x)
    return [a, a, b, b, a, c]


def right_parts(x):
    a, b, c = split3(x)
    return [a, b, a, b, c, a]


def stack16(parts):
    return jnp.concatenate(parts, axis=0).astype(bf16)


def basis(rows):
    row = sublane()
    place = jnp.where(row < 3, 2.0 * rows - 1.0, rows)
    first = place[0:3]
    norm = jnp.sum(first * first, axis=0, keepdims=True)
    cross = jnp.sum(first * place[3:6], axis=0, keepdims=True)
    full = jnp.where(row < 6, place, jnp.where(row == 6, cross, 1.0))
    return full, norm, cross


def right_distance(full, norm):
    row = sublane()
    return jnp.where(
        row < 3, full, jnp.where(row == 3, norm, jnp.where(row == 4, 1.0, 0.0))
    )


def left_distance(full, norm):
    row = sublane()
    return jnp.where(
        row < 3, -2.0 * full, jnp.where(row == 3, 1.0, jnp.where(row == 4, norm, 0.0))
    )


def left_approach(full, cross):
    return 4.0 * jnp.concatenate(
        [-full[3:6], -full[0:3], jnp.ones((1, PART), f32), cross], axis=0
    )


def columns(parts):
    fill = 128 - 8 * len(parts)
    return jnp.concatenate(parts + [jnp.zeros((fill, PART), f32)], axis=0).T


def mass_rows(mass):
    a, b, c = split3(mass)
    return jnp.concatenate([a, b, c, jnp.zeros((13, PART), f32)], axis=0).astype(bf16)


def halves(w):
    hi = w.astype(bf16)
    return hi, (w - hi.astype(f32)).astype(bf16)


def request_kernel(pos, vel, mass, smooth, counts, dest, target, state, req, slot, used):
    lane = lax.broadcasted_iota(i32, (1, PART), 1)

    def cell(c, _):
        live = jnp.where(lane < counts[c], mass[pl.ds(c, 1), :], 0.0)
        state[c] = jnp.concatenate([pos[c], vel[c], smooth[pl.ds(c, 1), :], live], axis=0)
        return 0

    lax.fori_loop(0, CELLS, cell, 0)
    req[...] = jnp.full_like(req, -1)

    def clear(d, _):
        used[d] = 0
        return 0

    lax.fori_loop(0, req.shape[0], clear, 0)
    short = lax.broadcasted_iota(i32, (1, 128), 1)

    def entry(e, _):
        d = dest[e]
        k = used[d]
        used[d] = k + 1
        slot[e] = d * CAP + k
        req[d] = jnp.where(short == k, target[e], req[d])
        return 0

    lax.fori_loop(0, SEND, entry, 0)


def respond_kernel(state, goals, out):
    def one(s, _):
        goal = jnp.maximum(goals[s], 0)
        out[s] = state[goal]
        return 0

    lax.fori_loop(0, out.shape[0], one, 0, unroll=4)


def pipeline(count, load, combine, store, work):
    load(0)

    def body(p, _):
        sums = combine(jnp.maximum(p - 1, 0))
        work(p)
        load(jnp.minimum(p + 1, count - 1))
        store(jnp.maximum(p - 1, 0), sums, p > 0)
        return 0

    lax.fori_loop(0, count, body, 0)
    store(count - 1, combine(count - 1), True)


def own_lists(pair_first, pair_offset, pa, po, ps, dummy):
    def one(e, _):
        pa[e] = e
        po[e] = e
        ps[e] = dummy
        a = pair_first[e]
        b = lax.rem(a + pair_offset[e], CELLS)
        pa[CELLS + e] = a
        po[CELLS + e] = b
        ps[CELLS + e] = b
        return 0

    lax.fori_loop(0, CELLS, one, 0)


def nn(a, b):
    return jnp.dot(a, b, preferred_element_type=f32)


def nt(a, b):
    return lax.dot_general(a, b, (((1,), (1,)), ((), ())), preferred_element_type=f32)


def density_weights(r2, total_h):
    inv = pltpu.reciprocal(total_h, approx=True)
    inv2 = inv * inv
    q2 = jnp.maximum(r2, TINY) * inv2
    q = q2 * lax.rsqrt(q2)
    u = 2.0 - q
    t = jnp.maximum(u, 0.0)
    return jnp.minimum(t * t * t, 4.0 - 3.0 * (q2 * u)) * (inv2 * inv)


def density_pairs(count, pa, po, ps, bf, cj, hj, at, bh, dist, ws, acc1, acc2):
    def load(p):
        dist[...] = nn(at[pa[p]], bf[po[p]])

    def work(p):
        a = pa[p]
        h_j = hj[po[p]]
        for c in range(0, PART, CHUNK):
            h_i = bh[a, c : c + CHUNK, :]
            w = density_weights(
                dist[c : c + CHUNK, :], jnp.concatenate([h_i, h_i], axis=1) + h_j
            )
            hi, lo = halves(w)
            ws[c : c + CHUNK, :] = hi
            ws[PART + c : PART + c + CHUNK, :] = lo

    def combine(p):
        own = cj[pa[p]]
        second = nn(jnp.concatenate([own, own], axis=1), ws[...])
        first = nt(cj[po[p]], ws[...])
        return first[0:8, 0:PART] + first[0:8, PART:], second[0:8]

    def store(p, sums, valid):
        if valid is True:
            acc1[pa[p]] += sums[0]
            acc2[ps[p]] += sums[1]
        else:
            keep = jnp.where(valid, 1.0, 0.0)
            acc1[pa[p]] += sums[0] * keep
            acc2[ps[p]] += sums[1] * keep

    ws[...] = jnp.zeros_like(ws)
    pipeline(count, load, combine, store, work)


def density_prepare_own(c, state, bf, cj, hj, at, bh):
    rows = state[c]
    full, norm, _ = basis(rows)
    bf[c] = stack16(right_parts(right_distance(full, norm)))
    cj[c] = mass_rows(rows[7:8])
    hj[c] = rows[6:7]
    t = columns(
        left_parts(left_distance(full, norm)) + [jnp.broadcast_to(rows[6:7], (8, PART))]
    )
    at[c] = t[:, 0:48].astype(bf16)
    bh[c] = jnp.broadcast_to(t[:, 48:49], (PART, 128))


def density_prepare_other(o, rows, bf, cj, hj):
    full, norm, _ = basis(rows)
    bf[o] = stack16(right_parts(right_distance(full, norm)))
    cj[o] = mass_rows(rows[7:8])
    hj[o] = rows[6:7]


def own_density_kernel(
    state, pair_first, pair_offset, total, acc1, acc2, bf, cj, hj, at, bh, dist, ws, pa, po, ps
):
    lax.fori_loop(
        0, CELLS, lambda c, _: density_prepare_own(c, state, bf, cj, hj, at, bh) or 0, 0
    )
    own_lists(pair_first, pair_offset, pa, po, ps, CELLS)
    acc1[...] = jnp.zeros_like(acc1)
    acc2[...] = jnp.zeros_like(acc2)
    density_pairs(CELLS + PAIRS, pa, po, ps, bf, cj, hj, at, bh, dist, ws, acc1, acc2)
    total[...] = acc1[...] + acc2[0:CELLS]


def far_density_kernel(
    state, far, slot, proxy_cell, acc1, ret, acc2, bf, cj, hj, at, bh, dist, ws, pa, po, ps
):
    lax.fori_loop(
        0, CELLS, lambda c, _: density_prepare_own(c, state, bf, cj, hj, at, bh) or 0, 0
    )

    def other(e, _):
        density_prepare_other(CELLS + e, far[slot[e]], bf, cj, hj)
        pa[e] = proxy_cell[e]
        po[e] = CELLS + e
        ps[e] = e
        return 0

    lax.fori_loop(0, SEND, other, 0, unroll=4)
    acc1[...] = jnp.zeros_like(acc1)
    acc2[...] = jnp.zeros_like(acc2)
    density_pairs(SEND, pa, po, ps, bf, cj, hj, at, bh, dist, ws, acc1, acc2)

    def back(e, _):
        ret[slot[e]] = jnp.sum(acc2[e][0:3], axis=0, keepdims=True)
        return 0

    lax.fori_loop(0, SEND, back, 0, unroll=4)


def combine_density_kernel(
    back, goals, near, far, energy, counts, density, fluid, answer, sums
):
    sums[...] = jnp.zeros_like(sums)

    def one(s, _):
        goal = goals[s]
        sums[jnp.where(goal < 0, CELLS, goal)] += back[s]
        return 0

    lax.fori_loop(0, back.shape[0], one, 0, unroll=2)
    lane = lax.broadcasted_iota(i32, (1, PART), 1)

    def cell(c, _):
        both = near[c] + far[c]
        raw = W_SCALE * (jnp.sum(both[0:3], axis=0, keepdims=True) + sums[c])
        here = lane < counts[c]
        density[pl.ds(c, 1), :] = jnp.where(here, raw, 0.0)
        fluid[c] = jnp.concatenate(
            [jnp.where(here, raw, 1.0), energy[pl.ds(c, 1), :]], axis=0
        )
        return 0

    lax.fori_loop(0, CELLS, cell, 0)

    def send(s, _):
        answer[s] = fluid[jnp.maximum(goals[s], 0)]
        return 0

    lax.fori_loop(0, answer.shape[0], send, 0, unroll=4)


def force_weights(r2, s, total_h, total_c, total_p, total_r):
    inv = pltpu.reciprocal(total_h, approx=True)
    inv2 = inv * inv
    q2 = jnp.maximum(r2, TINY) * inv2
    rs = lax.rsqrt(q2)
    q = q2 * rs
    u = 2.0 - q
    t = jnp.maximum(u, 0.0)
    grad = jnp.where(q < 1.0, 3.0 * u - 2.0, t * t * rs)
    m = jnp.minimum(s, 0.0) * (inv * pltpu.reciprocal(q2 + 0.01, approx=True))
    visc = m * (m - total_c) * pltpu.reciprocal(total_r, approx=True)
    return (total_p + visc) * (grad * (inv2 * inv2 * inv))


def force_fluid(fluid):
    rho, u = fluid[0:1], fluid[1:2]
    pressure = (GAMMA - 1.0) * u / rho
    sound = jnp.sqrt(GAMMA * (GAMMA - 1.0) * u)
    return pressure, sound, 4.0 * rho


def force_pairs(count, pa, po, ps, refs, acc1, acc2):
    bd, bs, cf, ad, as_, row, col, dist, appr, ws = refs

    def load(p):
        a, o = pa[p], po[p]
        dist[...] = nn(ad[a], bd[o])
        appr[...] = nn(as_[a], bs[o])

    def work(p):
        a, o = pa[p], po[p]
        side = row[o]

        def total(k, c):
            v = col[a, k, c : c + CHUNK, :]
            return jnp.concatenate([v, v], axis=1) + side[k : k + 1]

        for c in range(0, PART, CHUNK):
            w = force_weights(
                dist[c : c + CHUNK, :],
                appr[c : c + CHUNK, :],
                total(0, c),
                total(1, c),
                total(2, c),
                total(3, c),
            )
            hi, lo = halves(w)
            ws[c : c + CHUNK, :] = hi
            ws[PART + c : PART + c + CHUNK, :] = lo

    def fold(x):
        return x[0:8] + x[8:16] + x[16:24]

    def combine(p):
        own = cf[pa[p]]
        second = fold(nn(jnp.concatenate([own, own], axis=1), ws[...]))
        first = fold(nt(cf[po[p]], ws[...]))
        return first[:, 0:PART] + first[:, PART:], second

    def store(p, sums, valid):
        if valid is True:
            acc1[pa[p]] += sums[0]
            acc2[ps[p]] += sums[1]
        else:
            keep = jnp.where(valid, 1.0, 0.0)
            acc1[pa[p]] += sums[0] * keep
            acc2[ps[p]] += sums[1] * keep

    ws[...] = jnp.zeros_like(ws)
    pipeline(count, load, combine, store, work)


def force_prepare_other(o, rows, fluid, bd, bs, cf, row):
    full, norm, cross = basis(rows)
    bd[o] = stack16(right_parts(right_distance(full, norm)))
    bs[o] = stack16(right_parts(full))
    cf[o] = stack16(list(split3(rows[7:8] * full)))
    pressure, sound, rho4 = force_fluid(fluid)
    row[o] = jnp.concatenate(
        [rows[6:7], sound, pressure, rho4, jnp.zeros((4, PART), f32)], axis=0
    )
    return full, norm, cross


def force_prepare_own(c, rows, fluid, bd, bs, cf, row, ad, as_, col):
    full, norm, cross = force_prepare_other(c, rows, fluid, bd, bs, cf, row)
    t = columns(left_parts(left_distance(full, norm)) + [row[c]])
    ad[c] = t[:, 0:48].astype(bf16)
    for k in range(4):
        col[c, k] = jnp.broadcast_to(t[:, 48 + k : 49 + k], (PART, 128))
    as_[c] = columns(left_parts(left_approach(full, cross)))[:, 0:48].astype(bf16)


def force_sums(rows, sums):
    full, _, cross = basis(rows)
    count = sums[7:8]
    accel = (-0.5 * K_SCALE) * (full[0:3] * count - sums[0:3])
    mixed = jnp.sum(full[3:6] * sums[0:3] + full[0:3] * sums[3:6], axis=0, keepdims=True)
    heat = (0.25 * K_SCALE) * (cross * count - mixed + sums[6:7])
    return jnp.concatenate([accel, heat], axis=0)


def own_force_kernel(
    state, fluid, pair_first, pair_offset, total, acc1, acc2,
    bd, bs, cf, ad, as_, row, col, dist, appr, ws, pa, po, ps,
):
    def mine(c, _):
        force_prepare_own(c, state[c], fluid[c], bd, bs, cf, row, ad, as_, col)
        return 0

    lax.fori_loop(0, CELLS, mine, 0)
    own_lists(pair_first, pair_offset, pa, po, ps, CELLS)
    acc1[...] = jnp.zeros_like(acc1)
    acc2[...] = jnp.zeros_like(acc2)
    refs = (bd, bs, cf, ad, as_, row, col, dist, appr, ws)
    force_pairs(CELLS + PAIRS, pa, po, ps, refs, acc1, acc2)
    total[...] = acc1[...] + acc2[0:CELLS]


def far_force_kernel(
    state, fluid, far, far_fluid, slot, proxy_cell, acc1, ret, acc2,
    bd, bs, cf, ad, as_, row, col, dist, appr, ws, pa, po, ps,
):
    def mine(c, _):
        force_prepare_own(c, state[c], fluid[c], bd, bs, cf, row, ad, as_, col)
        return 0

    lax.fori_loop(0, CELLS, mine, 0)

    def other(e, _):
        s = slot[e]
        force_prepare_other(CELLS + e, far[s], far_fluid[s], bd, bs, cf, row)
        pa[e] = proxy_cell[e]
        po[e] = CELLS + e
        ps[e] = e
        return 0

    lax.fori_loop(0, SEND, other, 0, unroll=2)
    acc1[...] = jnp.zeros_like(acc1)
    acc2[...] = jnp.zeros_like(acc2)
    refs = (bd, bs, cf, ad, as_, row, col, dist, appr, ws)
    force_pairs(SEND, pa, po, ps, refs, acc1, acc2)

    def back(e, _):
        s = slot[e]
        ret[s] = force_sums(far[s], acc2[e])
        return 0

    lax.fori_loop(0, SEND, back, 0, unroll=2)


def finish_kernel(
    back, goals, near, far, state, energy, counts, mig_cell, mig_dest, accel, leave, sums, moved, used
):
    sums[...] = jnp.zeros_like(sums)

    def one(s, _):
        goal = goals[s]
        sums[jnp.where(goal < 0, CELLS, goal)] += back[s]
        return 0

    lax.fori_loop(0, back.shape[0], one, 0, unroll=2)
    lane = lax.broadcasted_iota(i32, (1, PART), 1)

    def cell(c, _):
        rows = state[c]
        here = lane < counts[c]
        total = jnp.where(here, force_sums(rows, near[c] + far[c]) + sums[c], 0.0)
        accel[c] = total
        new_vel = rows[3:6] + STEP * total[0:3]
        new_pos = rows[0:3] + STEP * new_vel
        new_energy = energy[pl.ds(c, 1), :] + STEP * total[3:4]
        kicked = jnp.concatenate(
            [new_pos, new_vel, rows[7:8], rows[6:7], new_energy], axis=0
        )
        moved[c] = jnp.where(here, kicked, 0.0)
        return 0

    lax.fori_loop(0, CELLS, cell, 0)
    leave[...] = jnp.zeros_like(leave)

    def clear(d, _):
        used[d] = 0
        return 0

    lax.fori_loop(0, leave.shape[0] // CAPM, clear, 0)

    def entry(e, _):
        d = mig_dest[e]
        k = used[d]
        used[d] = k + 1
        leave[d * CAPM + k] = moved[mig_cell[e]]
        return 0

    lax.fori_loop(0, mig_cell.shape[0], entry, 0)


def density_scratch(others):
    return [
        pltpu.VMEM((others, 48, PART), bf16),
        pltpu.VMEM((others, 16, PART), bf16),
        pltpu.VMEM((others, 1, PART), f32),
        pltpu.VMEM((CELLS, PART, 48), bf16),
        pltpu.VMEM((CELLS, PART, 128), f32),
        pltpu.VMEM((PART, PART), f32),
        pltpu.VMEM((2 * PART, PART), bf16),
    ] + [pltpu.SMEM((SEND,), i32)] * 3


def force_scratch(others):
    return [
        pltpu.VMEM((others, 48, PART), bf16),
        pltpu.VMEM((others, 48, PART), bf16),
        pltpu.VMEM((others, 24, PART), bf16),
        pltpu.VMEM((CELLS, PART, 48), bf16),
        pltpu.VMEM((CELLS, PART, 48), bf16),
        pltpu.VMEM((others, 8, PART), f32),
        pltpu.VMEM((CELLS, 4, PART, 128), f32),
        pltpu.VMEM((PART, PART), f32),
        pltpu.VMEM((PART, PART), f32),
        pltpu.VMEM((2 * PART, PART), bf16),
    ] + [pltpu.SMEM((SEND,), i32)] * 3


def exchange(x, axes):
    return lax.all_to_all(x, axes, split_axis=0, concat_axis=0, tiled=True)


def local(
    position, velocity, mass, smoothing, energy, counts, proxy_cell, proxy_dest,
    proxy_target, pair_first, pair_offset, mig_cell, mig_dest,
):
    devices = lax.axis_size(("rows", "cols"))
    col_count = lax.axis_size("cols")
    slots = devices * CAP
    both = ("rows", "cols")
    state, req, slot = kernel_call(
        request_kernel,
        (shape(CELLS, 8, PART), shape(devices, 1, 128, dtype=i32), shape(SEND, dtype=i32)),
        [VMEM] * 4 + [SMEM] * 3,
        (VMEM, VMEM, SMEM),
        [pltpu.SMEM((devices,), i32)],
        moved=2**20,
    )(position, velocity, mass, smoothing, counts, proxy_dest[:, 0], proxy_target)
    goals = exchange(req, both)[:, 0, 0:CAP].reshape(slots)
    near = kernel_call(
        own_density_kernel,
        shape(CELLS, 8, PART),
        [VMEM] + [SMEM] * 2,
        VMEM,
        [pltpu.VMEM((CELLS, 8, PART), f32), pltpu.VMEM((CELLS + 1, 8, PART), f32)]
        + density_scratch(CELLS),
        flops=32 * PART * PART * 300,
        moved=2**20,
    )(state, pair_first, pair_offset)
    answer = kernel_call(
        respond_kernel, shape(slots, 8, PART), [VMEM, SMEM], VMEM, moved=4 * 2**20
    )(state, goals)
    far = exchange(answer, both)
    far_sums, ret = kernel_call(
        far_density_kernel,
        (shape(CELLS, 8, PART), shape(slots, 1, PART)),
        [VMEM] * 2 + [SMEM] * 2,
        (VMEM, VMEM),
        [pltpu.VMEM((SEND, 8, PART), f32)] + density_scratch(CELLS + SEND),
        flops=128 * PART * PART * 300,
        moved=2**20,
    )(state, far, slot, proxy_cell)
    back = exchange(ret, both)
    density, fluid, answer2 = kernel_call(
        combine_density_kernel,
        (shape(CELLS, PART), shape(CELLS, 2, PART), shape(slots, 2, PART)),
        [VMEM, SMEM] + [VMEM] * 3 + [SMEM],
        (VMEM, VMEM, VMEM),
        [pltpu.VMEM((CELLS + 1, 1, PART), f32)],
        moved=2**20,
    )(back, goals, near, far_sums, energy, counts)
    far_fluid = exchange(answer2, both)
    near_force = kernel_call(
        own_force_kernel,
        shape(CELLS, 8, PART),
        [VMEM] * 2 + [SMEM] * 2,
        VMEM,
        [pltpu.VMEM((CELLS, 8, PART), f32), pltpu.VMEM((CELLS + 1, 8, PART), f32)]
        + force_scratch(CELLS),
        flops=32 * PART * PART * 600,
        moved=2**20,
    )(state, fluid, pair_first, pair_offset)
    far_force, ret4 = kernel_call(
        far_force_kernel,
        (shape(CELLS, 8, PART), shape(slots, 4, PART)),
        [VMEM] * 4 + [SMEM] * 2,
        (VMEM, VMEM),
        [pltpu.VMEM((SEND, 8, PART), f32)] + force_scratch(CELLS + SEND),
        flops=128 * PART * PART * 600,
        moved=2**20,
    )(state, fluid, far, far_fluid, slot, proxy_cell)
    back4 = exchange(ret4, both)
    accel, leave = kernel_call(
        finish_kernel,
        (shape(CELLS, 4, PART), shape(col_count * CAPM, 9, PART)),
        [VMEM, SMEM] + [VMEM] * 4 + [SMEM] * 3,
        (VMEM, VMEM),
        [
            pltpu.VMEM((CELLS + 1, 4, PART), f32),
            pltpu.VMEM((CELLS, 9, PART), f32),
            pltpu.SMEM((col_count,), i32),
        ],
        moved=2**20,
    )(back4, goals, near_force, far_force, state, energy, counts, mig_cell, mig_dest[:, 0])
    arrived = exchange(leave, "cols")
    return (density, accel, arrived)


def solution(mesh):
    lead = ("rows", "cols")
    one, two, three = P(lead), P(lead, None), P(lead, None, None)
    return jax.shard_map(
        local,
        mesh=mesh,
        in_specs=(three, three, two, two, two, one, one, two, one, one, one, one, two),
        out_specs=(two, three, three),
        check_vma=False,
    )
```

time: 765 us -> 283 us (0.37)
  other arithmetic: 536 us -> 0 us
  Pallas kernels: 0 us -> 168 us
  local copies, waits for them, and re-layouts: 114 us -> 6.39 us
  blocking collectives: 0 us -> 97.9 us
  waiting for transfers between devices: 62.8 us -> 0.01 us
  starting transfers between devices: 38.7 us -> 9.24 us
    reduce_sum x92 -> x0, other arithmetic: 476 us -> none  [the longest x18 161 us: force_pair(): heat_second = 0.5 * jnp.sum(weight_second * approach, axis=0)]
    pallas_call x0 -> x8, Pallas kernels: none -> 168 us  [the longest x1 67.9 us: local(): kernel_call(far_force_kernel, (shape(CELLS, 8, PART), shape(slots, 4, PAR...]
    all_to_all x0 -> x4, blocking collectives: none -> 97.9 us  [exchange(): return lax.all_to_all(x, axes, split_axis=0, concat_axis=0, tiled=True)]
    all_to_all x6 -> x2, waiting for transfers between devices: 62.8 us -> 0.01 us  [exchange(): return lax.all_to_all(x, axes, split_axis=0, concat_axis=0, tiled=True)]
    squeeze x36 -> x0, local copies, waits for them, and re-layouts: 33.5 us -> none  [run_pairs(): lax.map(one_block, (blocked(first_cells), blocked(second_cells), blocked(...]
    all_to_all x6 -> x2, starting transfers between devices: 38.7 us -> 9.24 us  [exchange(): return lax.all_to_all(x, axes, split_axis=0, concat_axis=0, tiled=True)]
    dynamic_update_slice x36 -> x0, other arithmetic: 23.6 us -> none  [run_pairs(): lax.map(one_block, (blocked(first_cells), blocked(second_cells), blocked(...]
    scatter x4 -> x0, local copies, waits for them, and re-layouts: 19.5 us -> none  [the longest x1 15.7 us: local(): outgoing = jnp.zeros((all_devices * CAP, 9, particles), jnp.float32).at[s...]
  transfers between devices with their start and end apart: 6 -> 2, of which waited for: 5 -> 0; matrix products, arithmetic and copies ran while one was open for 7% -> 0% of each run, Pallas kernels for 0% -> 13%
where the time goes in v1:
time: 283 us
  Pallas kernels  168 us (59%)
  blocking collectives  97.9 us (35%)
  starting transfers between devices  9.24 us (3%)
  local copies, waits for them, and re-layouts  6.39 us (2%)
    all_to_all x4, blocking collectives, exchange(): return lax.all_to_all(x, axes, split_axis=0, concat_axis=0, tiled=True)  97.9 us
    pallas_call x1, Pallas kernels, local(): kernel_call(far_force_kernel, (shape(CELLS, 8, PART), shape(slots, 4, PAR...  67.9 us
    pallas_call x1, Pallas kernels, local(): kernel_call(far_density_kernel, (shape(CELLS, 8, PART), shape(slots, 1, P...  48.1 us
    pallas_call x1, Pallas kernels, local(): kernel_call(own_force_kernel, shape(CELLS, 8, PART), [VMEM] * 2 + [SMEM]...  21.7 us
    pallas_call x1, Pallas kernels, local(): kernel_call(own_density_kernel, shape(CELLS, 8, PART), [VMEM] + [SMEM] *...  15.1 us
    all_to_all x2, starting transfers between devices, exchange(): return lax.all_to_all(x, axes, split_axis=0, concat_axis=0, tiled=True)  9.24 us
  transfers between devices with their start and end apart: 2, of which 0 were waited for; matrix products, arithmetic and copies ran while one was open for 0% of the time, Pallas kernels for 13%

profile of v1, /device:TPU:0, one launch (start us, length us, event | category | flops | bytes accessed | tf_op | source)
XLA Modules:
  0.0 282.5 jit_solution(9781832609516448565)
XLA Ops:
  0.6 1.5 copy.19.pos
  2.1 1.5 copy.20.vel
  3.6 3.7 %shard_map.148 = (f32[16,8,256]{2,1,0:T(8,128)}, s32[128,1,128]{2,1,0:T(1,128)}, s32[128]{0:T(128)}) custom-call(f32[16,3,256]{2,1,0:T(4,128)} %copy.19.pos, f32[16,3,256]{2,1,0:T(4,128)} %copy.20.vel, f32[16,256]{1,0:T(8,128)} %mass.1, f32[16,256]{1,0:T(8,128)} %smooth.1, s32[16]{0:T(128)} %counts.5, s32[128]{0:T(128)} %bitcast.2, s32[128]{0:T(128)} %target.1), custom_call_target="tpu_custom_call" | custom-call | bytes 1048576 | tf_op jit(solution)/shard_map/pallas_call | solution.py:561
  7.3 20.6 %all_to_all.30 = s32[128,1,128]{2,1,0:T(1,128)S(1)} all-to-all(s32[128,1,128]{2,1,0:T(1,128)} %get-tuple-element.16), channel_id=1, replica_groups=mesh['rows'=8,'cols'=16] {'rows','cols'}, dimensions={0} | all-to-all | bytes 131072 | tf_op jit(solution)/shard_map/all_to_all | solution.py:550
  27.9 0.2 slice_reduce_fusion
  28.1 0.7 reshape_squeeze.3.goals
  28.8 3.0 %shard_map.149 = f32[256,8,256]{2,1,0:T(8,128)} custom-call(f32[16,8,256]{2,1,0:T(8,128)} %get-tuple-element.15.state, s32[256]{0:T(256)} %reshape_squeeze.3.goals), custom_call_target="tpu_custom_call" | custom-call | bytes 4194304 | tf_op jit(solution)/shard_map/pallas_call | solution.py:580
  31.8 35.3 %all_to_all.31.far = f32[256,8,256]{2,1,0:T(8,128)} all-to-all(f32[256,8,256]{2,1,0:T(8,128)} %shard_map.149), channel_id=1, replica_groups=mesh['rows'=8,'cols'=16] {'rows','cols'}, dimensions={0} | all-to-all | bytes 4194304 | tf_op jit(solution)/shard_map/all_to_all | solution.py:550
  67.1 48.1 %shard_map.150 = (f32[16,8,256]{2,1,0:T(8,128)}, f32[256,1,256]{2,1,0:T(1,128)}) custom-call(f32[16,8,256]{2,1,0:T(8,128)} %get-tuple-element.15.state, f32[256,8,256]{2,1,0:T(8,128)} %all_to_all.31.far, s32[128]{0:T(128)} %get-tuple-element.17.slot, s32[128]{0:T(128)} %proxy_cell.3), custom_call_target="tpu_custom_call" | custom-call | flops 2516582400 | bytes 1048576 | tf_op jit(solution)/shard_map/pallas_call | solution.py:584
  115.2 4.6 %all-to-all-start.2 = ((f32[256,1,256]{2,1,0:T(1,128)}), f32[256,1,256]{2,1,0:T(1,128)S(1)}, u32[]{:S(2)}, u32[]{:S(2)}) async-start(f32[256,1,256]{2,1,0:T(1,128)} %get-tuple-element.18), calls=%async_computation.2 | async-start | bytes 524288 | tf_op jit(solution)/shard_map/all_to_all | solution.py:550
  119.8 15.1 %shard_map.151.near = f32[16,8,256]{2,1,0:T(8,128)} custom-call(f32[16,8,256]{2,1,0:T(8,128)} %get-tuple-element.15.state, s32[16]{0:T(128)} %pair_first.3, s32[16]{0:T(128)} %pair_offset.3), custom_call_target="tpu_custom_call" | custom-call | flops 629145600 | bytes 1048576 | tf_op jit(solution)/shard_map/pallas_call | solution.py:570
  134.9 0.0 all-to-all-done.2.back
  134.9 0.0 copy-start.1
  134.9 0.7 copy-done.1
  135.6 4.3 %shard_map.152 = (f32[16,256]{1,0:T(8,128)}, f32[16,2,256]{2,1,0:T(2,128)}, f32[256,2,256]{2,1,0:T(2,128)}) custom-call(f32[256,1,256]{2,1,0:T(1,128)} %copy-done.1, s32[256]{0:T(256)} %reshape_squeeze.3.goals, f32[16,8,256]{2,1,0:T(8,128)} %shard_map.151.near, f32[16,8,256]{2,1,0:T(8,128)} %get-tuple-element.19.far, f32[16,256]{1,0:T(8,128)} %energy.3, ...), custom_call_target="tpu_custom_call" | custom-call | bytes 1048576 | tf_op jit(solution)/shard_map/pallas_call | solution.py:594
  139.9 23.5 %all_to_all.32.far_fluid = f32[256,2,256]{2,1,0:T(2,128)} all-to-all(f32[256,2,256]{2,1,0:T(2,128)} %get-tuple-element.22), channel_id=1, replica_groups=mesh['rows'=8,'cols'=16] {'rows','cols'}, dimensions={0} | all-to-all | bytes 1048576 | tf_op jit(solution)/shard_map/all_to_all | solution.py:550
  163.4 67.9 %shard_map.153 = (f32[16,8,256]{2,1,0:T(8,128)}, f32[256,4,256]{2,1,0:T(4,128)}) custom-call(f32[16,8,256]{2,1,0:T(8,128)} %get-tuple-element.15.state, f32[16,2,256]{2,1,0:T(2,128)} %get-tuple-element.21.fluid, f32[256,8,256]{2,1,0:T(8,128)} %all_to_all.31.far, f32[256,2,256]{2,1,0:T(2,128)} %all_to_all.32.far_fluid, s32[128]{0:T(128)} %get-tuple-element.17.slot, ...), custom_call_target="tpu_custom_call" | custom-call | flops 5033164800 | bytes 1048576 | tf_op jit(solution)/shard_map/pallas_call | solution.py:613
  231.3 4.6 %all-to-all-start.4 = ((f32[256,4,256]{2,1,0:T(4,128)}), f32[256,4,256]{2,1,0:T(4,128)S(1)}, u32[]{:S(2)}, u32[]{:S(2)}) async-start(f32[256,4,256]{2,1,0:T(4,128)} %get-tuple-element.23), calls=%async_computation.4 | async-start | bytes 2097152 | tf_op jit(solution)/shard_map/all_to_all | solution.py:550
  235.9 21.7 %shard_map.154.near = f32[16,8,256]{2,1,0:T(8,128)} custom-call(f32[16,8,256]{2,1,0:T(8,128)} %get-tuple-element.15.state, f32[16,2,256]{2,1,0:T(2,128)} %get-tuple-element.21.fluid, s32[16]{0:T(128)} %pair_first.3, s32[16]{0:T(128)} %pair_offset.3), custom_call_target="tpu_custom_call" | custom-call | flops 1258291200 | bytes 1048576 | tf_op jit(solution)/shard_map/pallas_call | solution.py:603
  257.6 0.0 all-to-all-done.4.back
  257.6 0.0 copy-start
  257.6 1.0 copy-done
  258.6 4.5 %shard_map.155 = (f32[16,4,256]{2,1,0:T(4,128)}, f32[32,9,256]{2,1,0:T(8,128)}) custom-call(f32[256,4,256]{2,1,0:T(4,128)} %copy-done, s32[256]{0:T(256)} %reshape_squeeze.3.goals, f32[16,8,256]{2,1,0:T(8,128)} %shard_map.154.near, f32[16,8,256]{2,1,0:T(8,128)} %get-tuple-element.24.far, f32[16,8,256]{2,1,0:T(8,128)} %get-tuple-element.15.state, ...), custom_call_target="tpu_custom_call" | custom-call | bytes 1048576 | tf_op jit(solution)/shard_map/pallas_call | solution.py:623
  263.1 18.5 %all_to_all.33 = f32[32,9,256]{2,1,0:T(8,128)S(1)} all-to-all(f32[32,9,256]{2,1,0:T(8,128)} %get-tuple-element.26), channel_id=1, replica_groups=mesh['rows'=8,'cols'=16] {'cols'}, dimensions={0} | all-to-all | bytes 589824 | tf_op jit(solution)/shard_map/all_to_all | solution.py:550
  281.6 0.9 copy.21
Async XLA Ops:
  115.2 19.7 %all-to-all-start.2 = ((f32[256,1,256]{2,1,0:T(1,128)}), f32[256,1,256]{2,1,0:T(1,128)S(1)}, u32[]{:S(2)}, u32[]{:S(2)}) async-start(f32[256,1,256]{2,1,0:T(1,128)} %get-tuple-element.18), calls=%async_computation.2 | async-start | bytes 524288 | tf_op jit(solution)/shard_map/all_to_all | solution.py:550
  134.9 0.7 copy-start.1
  231.3 26.3 %all-to-all-start.4 = ((f32[256,4,256]{2,1,0:T(4,128)}), f32[256,4,256]{2,1,0:T(4,128)S(1)}, u32[]{:S(2)}, u32[]{:S(2)}) async-start(f32[256,4,256]{2,1,0:T(4,128)} %get-tuple-element.23), calls=%async_computation.4 | async-start | bytes 2097152 | tf_op jit(solution)/shard_map/all_to_all | solution.py:550
  257.6 1.0 copy-start

commit v2 on v1

--- a/solution.py
+++ b/solution.py
@@ -19,6 +19,8 @@
 K_SCALE = -24.0 / PI
 TINY = 1e-12
 CHUNK = 32
+ROWS = (128, 160, 192, 224, 256)
+BLOCKS = SEND + CELLS
 
 f32, bf16, i32 = jnp.float32, jnp.bfloat16, jnp.int32
 VMEM = pl.BlockSpec(memory_space=pltpu.VMEM)
@@ -149,18 +151,81 @@
     lax.fori_loop(0, out.shape[0], one, 0, unroll=4)
 
 
-def pipeline(count, load, combine, store, work):
+def pipeline(count, rows_of, load, combine, store, work):
     load(0)
 
     def body(p, _):
-        sums = combine(jnp.maximum(p - 1, 0))
-        work(p)
-        load(jnp.minimum(p + 1, count - 1))
-        store(jnp.maximum(p - 1, 0), sums, p > 0)
+        need = rows_of(p)
+        low = 0
+        for rows in ROWS:
+            @pl.when((need > low) & (need <= rows))
+            def _():
+                sums = combine(jnp.maximum(p - 1, 0))
+                work(p, rows)
+                load(jnp.minimum(p + 1, count - 1))
+                store(jnp.maximum(p - 1, 0), sums, p > 0)
+
+            low = rows
         return 0
 
     lax.fori_loop(0, count, body, 0)
     store(count - 1, combine(count - 1), True)
+
+
+def pack_plan(far, slot, proxy_cell, offset, block_own, live, filled):
+    def clear(c, _):
+        filled[c] = 0
+        return 0
+
+    lax.fori_loop(0, CELLS, clear, 0)
+
+    def measure(e, _):
+        mass = far[slot[e]][7:8]
+        n = jnp.sum(jnp.where(mass > 0.0, 1.0, 0.0)).astype(i32)
+        live[e] = n
+        a = proxy_cell[e]
+        offset[e] = filled[a]
+        filled[a] = filled[a] + n
+        return 0
+
+    lax.fori_loop(0, SEND, measure, 0, unroll=8)
+
+    def place(c, total):
+        blocks = (filled[c] + PART - 1) // PART
+        filled[c] = total * PART
+
+        def name(t, _):
+            block_own[total + t] = c
+            return 0
+
+        lax.fori_loop(0, blocks, name, 0)
+        return total + blocks
+
+    total = lax.fori_loop(0, CELLS, place, 0)
+
+    def shift(e, _):
+        offset[e] = offset[e] + filled[proxy_cell[e]]
+        return 0
+
+    lax.fori_loop(0, SEND, shift, 0, unroll=8)
+    return total
+
+
+def pack(target, rows, offset, n):
+    t = offset // PART
+    lane0 = offset - t * PART
+    lane = lax.broadcasted_iota(i32, rows.shape, 1)
+    turned = pltpu.roll(rows, lane0, 1)
+    target[t] = jnp.where((lane >= lane0) & (lane < lane0 + n), turned, target[t])
+    target[t + 1] = jnp.where(lane < lane0 + n - PART, turned, target[t + 1])
+
+
+def unpack(source, offset):
+    t = offset // PART
+    lane0 = offset - t * PART
+    first, second = source[t], source[t + 1]
+    lane = lax.broadcasted_iota(i32, first.shape, 1)
+    return pltpu.roll(jnp.where(lane >= lane0, first, second), lax.rem(PART - lane0, PART), 1)
 
 
 def own_lists(pair_first, pair_offset, pa, po, ps, dummy):
@@ -196,14 +261,14 @@
     return jnp.minimum(t * t * t, 4.0 - 3.0 * (q2 * u)) * (inv2 * inv)
 
 
-def density_pairs(count, pa, po, ps, bf, cj, hj, at, bh, dist, ws, acc1, acc2):
+def density_pairs(count, counts, pa, po, ps, bf, cj, hj, at, bh, dist, ws, acc1, acc2):
     def load(p):
         dist[...] = nn(at[pa[p]], bf[po[p]])
 
-    def work(p):
+    def work(p, rows):
         a = pa[p]
         h_j = hj[po[p]]
-        for c in range(0, PART, CHUNK):
+        for c in range(0, rows, CHUNK):
             h_i = bh[a, c : c + CHUNK, :]
             w = density_weights(
                 dist[c : c + CHUNK, :], jnp.concatenate([h_i, h_i], axis=1) + h_j
@@ -228,7 +293,7 @@
             acc2[ps[p]] += sums[1] * keep
 
     ws[...] = jnp.zeros_like(ws)
-    pipeline(count, load, combine, store, work)
+    pipeline(count, lambda p: counts[pa[p]], load, combine, store, work)
 
 
 def density_prepare_own(c, state, bf, cj, hj, at, bh):
@@ -252,7 +317,7 @@
 
 
 def own_density_kernel(
-    state, pair_first, pair_offset, total, acc1, acc2, bf, cj, hj, at, bh, dist, ws, pa, po, ps
+    state, counts, pair_first, pair_offset, total, acc1, acc2, bf, cj, hj, at, bh, dist, ws, pa, po, ps
 ):
     lax.fori_loop(
         0, CELLS, lambda c, _: density_prepare_own(c, state, bf, cj, hj, at, bh) or 0, 0
@@ -260,31 +325,41 @@
     own_lists(pair_first, pair_offset, pa, po, ps, CELLS)
     acc1[...] = jnp.zeros_like(acc1)
     acc2[...] = jnp.zeros_like(acc2)
-    density_pairs(CELLS + PAIRS, pa, po, ps, bf, cj, hj, at, bh, dist, ws, acc1, acc2)
+    density_pairs(CELLS + PAIRS, counts, pa, po, ps, bf, cj, hj, at, bh, dist, ws, acc1, acc2)
     total[...] = acc1[...] + acc2[0:CELLS]
 
 
 def far_density_kernel(
-    state, far, slot, proxy_cell, acc1, ret, acc2, bf, cj, hj, at, bh, dist, ws, pa, po, ps
+    state, far, counts, slot, proxy_cell, acc1, ret, blocks, offset, block_own, live, size, acc2,
+    bf, cj, hj, at, bh, dist, ws, pa, po, ps, filled,
 ):
     lax.fori_loop(
         0, CELLS, lambda c, _: density_prepare_own(c, state, bf, cj, hj, at, bh) or 0, 0
     )
-
-    def other(e, _):
-        density_prepare_other(CELLS + e, far[slot[e]], bf, cj, hj)
-        pa[e] = proxy_cell[e]
-        po[e] = CELLS + e
-        ps[e] = e
-        return 0
-
-    lax.fori_loop(0, SEND, other, 0, unroll=4)
+    total = pack_plan(far, slot, proxy_cell, offset, block_own, live, filled)
+    size[0] = total
+    blocks[...] = jnp.zeros_like(blocks)
+
+    def fill(e, _):
+        pack(blocks, far[slot[e]], offset[e], live[e])
+        return 0
+
+    lax.fori_loop(0, SEND, fill, 0, unroll=4)
+
+    def other(t, _):
+        density_prepare_other(CELLS + t, blocks[t], bf, cj, hj)
+        pa[t] = block_own[t]
+        po[t] = CELLS + t
+        ps[t] = t
+        acc2[t] = jnp.zeros((8, PART), f32)
+        return 0
+
+    lax.fori_loop(0, total, other, 0)
     acc1[...] = jnp.zeros_like(acc1)
-    acc2[...] = jnp.zeros_like(acc2)
-    density_pairs(SEND, pa, po, ps, bf, cj, hj, at, bh, dist, ws, acc1, acc2)
+    density_pairs(total, counts, pa, po, ps, bf, cj, hj, at, bh, dist, ws, acc1, acc2)
 
     def back(e, _):
-        ret[slot[e]] = jnp.sum(acc2[e][0:3], axis=0, keepdims=True)
+        ret[slot[e]] = jnp.sum(unpack(acc2, offset[e])[0:3], axis=0, keepdims=True)
         return 0
 
     lax.fori_loop(0, SEND, back, 0, unroll=4)
@@ -343,7 +418,7 @@
     return pressure, sound, 4.0 * rho
 
 
-def force_pairs(count, pa, po, ps, refs, acc1, acc2):
+def force_pairs(count, counts, pa, po, ps, refs, acc1, acc2):
     bd, bs, cf, ad, as_, row, col, dist, appr, ws = refs
 
     def load(p):
@@ -351,7 +426,7 @@
         dist[...] = nn(ad[a], bd[o])
         appr[...] = nn(as_[a], bs[o])
 
-    def work(p):
+    def work(p, rows):
         a, o = pa[p], po[p]
         side = row[o]
 
@@ -359,7 +434,7 @@
             v = col[a, k, c : c + CHUNK, :]
             return jnp.concatenate([v, v], axis=1) + side[k : k + 1]
 
-        for c in range(0, PART, CHUNK):
+        for c in range(0, rows, CHUNK):
             w = force_weights(
                 dist[c : c + CHUNK, :],
                 appr[c : c + CHUNK, :],
@@ -391,7 +466,7 @@
             acc2[ps[p]] += sums[1] * keep
 
     ws[...] = jnp.zeros_like(ws)
-    pipeline(count, load, combine, store, work)
+    pipeline(count, lambda p: counts[pa[p]], load, combine, store, work)
 
 
 def force_prepare_other(o, rows, fluid, bd, bs, cf, row):
@@ -425,7 +500,7 @@
 
 
 def own_force_kernel(
-    state, fluid, pair_first, pair_offset, total, acc1, acc2,
+    state, fluid, counts, pair_first, pair_offset, total, acc1, acc2,
     bd, bs, cf, ad, as_, row, col, dist, appr, ws, pa, po, ps,
 ):
     def mine(c, _):
@@ -437,40 +512,52 @@
     acc1[...] = jnp.zeros_like(acc1)
     acc2[...] = jnp.zeros_like(acc2)
     refs = (bd, bs, cf, ad, as_, row, col, dist, appr, ws)
-    force_pairs(CELLS + PAIRS, pa, po, ps, refs, acc1, acc2)
+    force_pairs(CELLS + PAIRS, counts, pa, po, ps, refs, acc1, acc2)
     total[...] = acc1[...] + acc2[0:CELLS]
 
 
 def far_force_kernel(
-    state, fluid, far, far_fluid, slot, proxy_cell, acc1, ret, acc2,
-    bd, bs, cf, ad, as_, row, col, dist, appr, ws, pa, po, ps,
+    state, fluid, blocks, far_fluid, counts, slot, offset, block_own, live, size, acc1, ret, acc2,
+    fluids, bd, bs, cf, ad, as_, row, col, dist, appr, ws, pa, po, ps,
 ):
     def mine(c, _):
         force_prepare_own(c, state[c], fluid[c], bd, bs, cf, row, ad, as_, col)
         return 0
 
     lax.fori_loop(0, CELLS, mine, 0)
-
-    def other(e, _):
-        s = slot[e]
-        force_prepare_other(CELLS + e, far[s], far_fluid[s], bd, bs, cf, row)
-        pa[e] = proxy_cell[e]
-        po[e] = CELLS + e
-        ps[e] = e
-        return 0
-
-    lax.fori_loop(0, SEND, other, 0, unroll=2)
+    fluids[...] = jnp.ones_like(fluids)
+
+    def fill(e, _):
+        pack(fluids, far_fluid[slot[e]], offset[e], live[e])
+        return 0
+
+    lax.fori_loop(0, SEND, fill, 0, unroll=4)
+    total = size[0]
+
+    def other(t, _):
+        force_prepare_other(CELLS + t, blocks[t], fluids[t], bd, bs, cf, row)
+        pa[t] = block_own[t]
+        po[t] = CELLS + t
+        ps[t] = t
+        return 0
+
+    lax.fori_loop(0, total, other, 0)
     acc1[...] = jnp.zeros_like(acc1)
     acc2[...] = jnp.zeros_like(acc2)
     refs = (bd, bs, cf, ad, as_, row, col, dist, appr, ws)
-    force_pairs(SEND, pa, po, ps, refs, acc1, acc2)
+    force_pairs(total, counts, pa, po, ps, refs, acc1, acc2)
+
+    def turn(t, _):
+        acc2[t, 0:4] = force_sums(blocks[t], acc2[t])
+        return 0
+
+    lax.fori_loop(0, total, turn, 0)
 
     def back(e, _):
-        s = slot[e]
-        ret[s] = force_sums(far[s], acc2[e])
-        return 0
-
-    lax.fori_loop(0, SEND, back, 0, unroll=2)
+        ret[slot[e]] = unpack(acc2, offset[e])[0:4]
+        return 0
+
+    lax.fori_loop(0, SEND, back, 0, unroll=4)
 
 
 def finish_kernel(
@@ -528,7 +615,7 @@
         pltpu.VMEM((CELLS, PART, 128), f32),
         pltpu.VMEM((PART, PART), f32),
         pltpu.VMEM((2 * PART, PART), bf16),
-    ] + [pltpu.SMEM((SEND,), i32)] * 3
+    ] + [pltpu.SMEM((BLOCKS,), i32)] * 3
 
 
 def force_scratch(others):
@@ -543,7 +630,7 @@
         pltpu.VMEM((PART, PART), f32),
         pltpu.VMEM((PART, PART), f32),
         pltpu.VMEM((2 * PART, PART), bf16),
-    ] + [pltpu.SMEM((SEND,), i32)] * 3
+    ] + [pltpu.SMEM((BLOCKS,), i32)] * 3
 
 
 def exchange(x, axes):
@@ -570,26 +657,36 @@
     near = kernel_call(
         own_density_kernel,
         shape(CELLS, 8, PART),
-        [VMEM] + [SMEM] * 2,
+        [VMEM] + [SMEM] * 3,
         VMEM,
         [pltpu.VMEM((CELLS, 8, PART), f32), pltpu.VMEM((CELLS + 1, 8, PART), f32)]
         + density_scratch(CELLS),
         flops=32 * PART * PART * 300,
         moved=2**20,
-    )(state, pair_first, pair_offset)
+    )(state, counts, pair_first, pair_offset)
     answer = kernel_call(
         respond_kernel, shape(slots, 8, PART), [VMEM, SMEM], VMEM, moved=4 * 2**20
     )(state, goals)
     far = exchange(answer, both)
-    far_sums, ret = kernel_call(
+    far_sums, ret, blocks, offset, block_own, live, size = kernel_call(
         far_density_kernel,
-        (shape(CELLS, 8, PART), shape(slots, 1, PART)),
-        [VMEM] * 2 + [SMEM] * 2,
-        (VMEM, VMEM),
-        [pltpu.VMEM((SEND, 8, PART), f32)] + density_scratch(CELLS + SEND),
+        (
+            shape(CELLS, 8, PART),
+            shape(slots, 1, PART),
+            shape(BLOCKS + 1, 8, PART),
+            shape(SEND, dtype=i32),
+            shape(BLOCKS, dtype=i32),
+            shape(SEND, dtype=i32),
+            shape(1, dtype=i32),
+        ),
+        [VMEM] * 2 + [SMEM] * 3,
+        (VMEM,) * 3 + (SMEM,) * 4,
+        [pltpu.VMEM((BLOCKS + 1, 8, PART), f32)]
+        + density_scratch(CELLS + BLOCKS)
+        + [pltpu.SMEM((CELLS,), i32)],
         flops=128 * PART * PART * 300,
         moved=2**20,
-    )(state, far, slot, proxy_cell)
+    )(state, far, counts, slot, proxy_cell)
     back = exchange(ret, both)
     density, fluid, answer2 = kernel_call(
         combine_density_kernel,
@@ -603,22 +700,23 @@
     near_force = kernel_call(
         own_force_kernel,
         shape(CELLS, 8, PART),
-        [VMEM] * 2 + [SMEM] * 2,
+        [VMEM] * 2 + [SMEM] * 3,
         VMEM,
         [pltpu.VMEM((CELLS, 8, PART), f32), pltpu.VMEM((CELLS + 1, 8, PART), f32)]
         + force_scratch(CELLS),
         flops=32 * PART * PART * 600,
         moved=2**20,
-    )(state, fluid, pair_first, pair_offset)
+    )(state, fluid, counts, pair_first, pair_offset)
     far_force, ret4 = kernel_call(
         far_force_kernel,
         (shape(CELLS, 8, PART), shape(slots, 4, PART)),
-        [VMEM] * 4 + [SMEM] * 2,
+        [VMEM] * 4 + [SMEM] * 6,
         (VMEM, VMEM),
-        [pltpu.VMEM((SEND, 8, PART), f32)] + force_scratch(CELLS + SEND),
+        [pltpu.VMEM((BLOCKS + 1, 8, PART), f32), pltpu.VMEM((BLOCKS + 1, 2, PART), f32)]
+        + force_scratch(CELLS + BLOCKS),
         flops=128 * PART * PART * 600,
         moved=2**20,
-    )(state, fluid, far, far_fluid, slot, proxy_cell)
+    )(state, fluid, blocks, far_fluid, counts, slot, offset, block_own, live, size)
     back4 = exchange(ret4, both)
     accel, leave = kernel_call(
         finish_kernel,

time: 283 us -> 277 us (0.979)
  Pallas kernels: 168 us -> 154 us
  starting transfers between devices: 9.24 us -> 15.7 us
    pallas_call x1, Pallas kernels: 67.9 us -> 56.2 us  [local(): kernel_call(far_force_kernel, (shape(CELLS, 8, PART), shape(slots, 4, PAR...]
    all_to_all x2, starting transfers between devices: 9.24 us -> 15.7 us  [exchange(): return lax.all_to_all(x, axes, split_axis=0, concat_axis=0, tiled=True)]
where the time goes in v2:
time: 277 us; the launch traced here: 276 us
  Pallas kernels  154 us (56%)
  blocking collectives  99.2 us (36%)
  starting transfers between devices  15.7 us (6%)
  local copies, waits for them, and re-layouts  6.39 us (2%)
    all_to_all x4, blocking collectives, exchange(): return lax.all_to_all(x, axes, split_axis=0, concat_axis=0, tiled=True)  99.2 us
    pallas_call x1, Pallas kernels, local(): kernel_call(far_force_kernel, (shape(CELLS, 8, PART), shape(slots, 4, PAR...  56.2 us
    pallas_call x1, Pallas kernels, local(): kernel_call(far_density_kernel, (shape(CELLS, 8, PART), shape(slots, 1, P...  47.3 us
    pallas_call x1, Pallas kernels, local(): kernel_call(own_force_kernel, shape(CELLS, 8, PART), [VMEM] * 2 + [SMEM]...  19.8 us
    all_to_all x2, starting transfers between devices, exchange(): return lax.all_to_all(x, axes, split_axis=0, concat_axis=0, tiled=True)  15.7 us
    pallas_call x1, Pallas kernels, local(): kernel_call(own_density_kernel, shape(CELLS, 8, PART), [VMEM] + [SMEM] *...  14.8 us
  transfers between devices with their start and end apart: 2, of which 0 were waited for; matrix products, arithmetic and copies ran while one was open for 0% of the time, Pallas kernels for 13%

profile of v2, /device:TPU:0, one launch (start us, length us, event | category | flops | bytes accessed | tf_op | source)
XLA Modules:
  0.0 275.5 jit_solution(809822510031198856)
XLA Ops:
  0.6 1.5 copy.19.pos
  2.1 1.5 copy.20.vel
  3.6 3.7 %shard_map.148 = (f32[16,8,256]{2,1,0:T(8,128)}, s32[128,1,128]{2,1,0:T(1,128)}, s32[128]{0:T(128)}) custom-call(f32[16,3,256]{2,1,0:T(4,128)} %copy.19.pos, f32[16,3,256]{2,1,0:T(4,128)} %copy.20.vel, f32[16,256]{1,0:T(8,128)} %mass.1, f32[16,256]{1,0:T(8,128)} %smooth.1, s32[16]{0:T(128)} %counts.13, s32[128]{0:T(128)} %bitcast.2, s32[128]{0:T(128)} %target.1), custom_call_target="tpu_custom_call" | custom-call | bytes 1048576 | tf_op jit(solution)/shard_map/pallas_call | solution.py:648
  7.3 20.6 %all_to_all.30 = s32[128,1,128]{2,1,0:T(1,128)S(1)} all-to-all(s32[128,1,128]{2,1,0:T(1,128)} %get-tuple-element.21), channel_id=1, replica_groups=mesh['rows'=8,'cols'=16] {'rows','cols'}, dimensions={0} | all-to-all | bytes 131072 | tf_op jit(solution)/shard_map/all_to_all | solution.py:637
  27.9 0.2 slice_reduce_fusion
  28.1 0.7 reshape_squeeze.3.goals
  28.8 3.0 %shard_map.149 = f32[256,8,256]{2,1,0:T(8,128)} custom-call(f32[16,8,256]{2,1,0:T(8,128)} %get-tuple-element.20.state, s32[256]{0:T(256)} %reshape_squeeze.3.goals), custom_call_target="tpu_custom_call" | custom-call | bytes 4194304 | tf_op jit(solution)/shard_map/pallas_call | solution.py:667
  31.8 35.3 %all_to_all.31.far = f32[256,8,256]{2,1,0:T(8,128)} all-to-all(f32[256,8,256]{2,1,0:T(8,128)} %shard_map.149), channel_id=1, replica_groups=mesh['rows'=8,'cols'=16] {'rows','cols'}, dimensions={0} | all-to-all | bytes 4194304 | tf_op jit(solution)/shard_map/all_to_all | solution.py:637
  67.1 47.3 %shard_map.150 = (f32[16,8,256]{2,1,0:T(8,128)}, f32[256,1,256]{2,1,0:T(1,128)}, f32[145,8,256]{2,1,0:T(8,128)}, s32[128]{0:T(128)}, s32[144]{0:T(256)}, /*index=5*/s32[128]{0:T(128)}, s32[1]{0:T(128)}) custom-call(f32[16,8,256]{2,1,0:T(8,128)} %get-tuple-element.20.state, f32[256,8,256]{2,1,0:T(8,128)} %all_to_all.31.far, s32[16]{0:T(128)} %counts.13, ...), custom_call_target="tpu_custom_call" | custom-call | flops 2516582400 | bytes 1048576 | tf_op jit(solution)/shard_map/pallas_call | solution.py:671
  114.4 6.7 %all-to-all-start.2 = ((f32[256,1,256]{2,1,0:T(1,128)}), f32[256,1,256]{2,1,0:T(1,128)S(1)}, u32[]{:S(2)}, u32[]{:S(2)}) async-start(f32[256,1,256]{2,1,0:T(1,128)} %get-tuple-element.23), calls=%async_computation.2 | async-start | bytes 524288 | tf_op jit(solution)/shard_map/all_to_all | solution.py:637
  121.1 14.8 %shard_map.151.near = f32[16,8,256]{2,1,0:T(8,128)} custom-call(f32[16,8,256]{2,1,0:T(8,128)} %get-tuple-element.20.state, s32[16]{0:T(128)} %counts.13, s32[16]{0:T(128)} %pair_first.3, s32[16]{0:T(128)} %pair_offset.3), custom_call_target="tpu_custom_call" | custom-call | flops 629145600 | bytes 1048576 | tf_op jit(solution)/shard_map/pallas_call | solution.py:657
  135.8 0.0 all-to-all-done.2.back
  135.8 0.0 copy-start.1
  135.8 0.7 copy-done.1
  136.5 4.3 %shard_map.152 = (f32[16,256]{1,0:T(8,128)}, f32[16,2,256]{2,1,0:T(2,128)}, f32[256,2,256]{2,1,0:T(2,128)}) custom-call(f32[256,1,256]{2,1,0:T(1,128)} %copy-done.1, s32[256]{0:T(256)} %reshape_squeeze.3.goals, f32[16,8,256]{2,1,0:T(8,128)} %shard_map.151.near, f32[16,8,256]{2,1,0:T(8,128)} %get-tuple-element.24.far, f32[16,256]{1,0:T(8,128)} %energy.3, ...), custom_call_target="tpu_custom_call" | custom-call | bytes 1048576 | tf_op jit(solution)/shard_map/pallas_call | solution.py:691
  140.8 24.1 %all_to_all.32.far_fluid = f32[256,2,256]{2,1,0:T(2,128)} all-to-all(f32[256,2,256]{2,1,0:T(2,128)} %get-tuple-element.28), channel_id=1, replica_groups=mesh['rows'=8,'cols'=16] {'rows','cols'}, dimensions={0} | all-to-all | bytes 1048576 | tf_op jit(solution)/shard_map/all_to_all | solution.py:637
  164.9 56.2 %shard_map.153 = (f32[16,8,256]{2,1,0:T(8,128)}, f32[256,4,256]{2,1,0:T(4,128)}) custom-call(f32[16,8,256]{2,1,0:T(8,128)} %get-tuple-element.20.state, f32[16,2,256]{2,1,0:T(2,128)} %get-tuple-element.26.fluid, f32[145,8,256]{2,1,0:T(8,128)} %get-tuple-element.27.blocks, f32[256,2,256]{2,1,0:T(2,128)} %all_to_all.32.far_fluid, s32[16]{0:T(128)} %counts.13, ...), custom_call_target="tpu_custom_call" | custom-call | flops 5033164800 | bytes 1048576 | tf_op jit(solution)/shard_map/pallas_call | solution.py:710
  221.1 9.1 %all-to-all-start.4 = ((f32[256,4,256]{2,1,0:T(4,128)}), f32[256,4,256]{2,1,0:T(4,128)S(1)}, u32[]{:S(2)}, u32[]{:S(2)}) async-start(f32[256,4,256]{2,1,0:T(4,128)} %get-tuple-element.33), calls=%async_computation.4 | async-start | bytes 2097152 | tf_op jit(solution)/shard_map/all_to_all | solution.py:637
  230.2 19.8 %shard_map.154.near = f32[16,8,256]{2,1,0:T(8,128)} custom-call(f32[16,8,256]{2,1,0:T(8,128)} %get-tuple-element.20.state, f32[16,2,256]{2,1,0:T(2,128)} %get-tuple-element.26.fluid, s32[16]{0:T(128)} %counts.13, s32[16]{0:T(128)} %pair_first.3, s32[16]{0:T(128)} %pair_offset.3), custom_call_target="tpu_custom_call" | custom-call | flops 1258291200 | bytes 1048576 | tf_op jit(solution)/shard_map/pallas_call | solution.py:700
  249.9 0.0 all-to-all-done.4.back
  249.9 0.0 copy-start
  249.9 1.0 copy-done
  250.9 4.5 %shard_map.155 = (f32[16,4,256]{2,1,0:T(4,128)}, f32[32,9,256]{2,1,0:T(8,128)}) custom-call(f32[256,4,256]{2,1,0:T(4,128)} %copy-done, s32[256]{0:T(256)} %reshape_squeeze.3.goals, f32[16,8,256]{2,1,0:T(8,128)} %shard_map.154.near, f32[16,8,256]{2,1,0:T(8,128)} %get-tuple-element.34.far, f32[16,8,256]{2,1,0:T(8,128)} %get-tuple-element.20.state, ...), custom_call_target="tpu_custom_call" | custom-call | bytes 1048576 | tf_op jit(solution)/shard_map/pallas_call | solution.py:721
  255.5 19.2 %all_to_all.33 = f32[32,9,256]{2,1,0:T(8,128)S(1)} all-to-all(f32[32,9,256]{2,1,0:T(8,128)} %get-tuple-element.36), channel_id=1, replica_groups=mesh['rows'=8,'cols'=16] {'cols'}, dimensions={0} | all-to-all | bytes 589824 | tf_op jit(solution)/shard_map/all_to_all | solution.py:637
  274.6 0.9 copy.21
Async XLA Ops:
  114.4 21.4 %all-to-all-start.2 = ((f32[256,1,256]{2,1,0:T(1,128)}), f32[256,1,256]{2,1,0:T(1,128)S(1)}, u32[]{:S(2)}, u32[]{:S(2)}) async-start(f32[256,1,256]{2,1,0:T(1,128)} %get-tuple-element.23), calls=%async_computation.2 | async-start | bytes 524288 | tf_op jit(solution)/shard_map/all_to_all | solution.py:637
  135.8 0.7 copy-start.1
  221.1 28.8 %all-to-all-start.4 = ((f32[256,4,256]{2,1,0:T(4,128)}), f32[256,4,256]{2,1,0:T(4,128)S(1)}, u32[]{:S(2)}, u32[]{:S(2)}) async-start(f32[256,4,256]{2,1,0:T(4,128)} %get-tuple-element.33), calls=%async_computation.4 | async-start | bytes 2097152 | tf_op jit(solution)/shard_map/all_to_all | solution.py:637
  249.9 1.0 copy-start

commit v3 on v2

v3 whole, which is shorter than its diff:
```python
import jax
import jax.numpy as jnp
from jax import lax
from jax.experimental import pallas as pl
from jax.experimental.pallas import tpu as pltpu
from jax.sharding import PartitionSpec as P

CAP = 2
CAPM = 2
CELLS = 16
SEND = 128
PAIRS = 16
PART = 256

GAMMA = 5.0 / 3.0
STEP = 0.02
PI = 3.141592653589793
W_SCALE = 2.0 / PI
K_SCALE = -24.0 / PI
TINY = 1e-12
CHUNK = 32
ROWS = (128, 160, 192, 224, 256)
BLOCKS = SEND + CELLS
EARLY, LATE = 42, 48
DEPTH = 4

f32, bf16, i32 = jnp.float32, jnp.bfloat16, jnp.int32
VMEM = pl.BlockSpec(memory_space=pltpu.VMEM)
ANY = pl.BlockSpec(memory_space=pl.ANY)
SMEM = pl.BlockSpec(memory_space=pltpu.SMEM)
LIMIT = 56 * 2**20


def shape(*dims, dtype=f32):
    return jax.ShapeDtypeStruct(dims, dtype)


def kernel_call(body, out_shape, in_specs, out_specs, scratch=(), flops=0, moved=0):
    return pl.pallas_call(
        body,
        out_shape=out_shape,
        in_specs=in_specs,
        out_specs=out_specs,
        scratch_shapes=list(scratch),
        compiler_params=pltpu.CompilerParams(vmem_limit_bytes=LIMIT),
        cost_estimate=pl.CostEstimate(flops=flops, bytes_accessed=moved, transcendentals=0),
    )


def sublane():
    return lax.broadcasted_iota(i32, (8, PART), 0)


def split3(x):
    a = x.astype(bf16).astype(f32)
    b = (x - a).astype(bf16).astype(f32)
    return a, b, x - a - b


def left_parts(x):
    a, b, c = split3(x)
    return [a, a, b, b, a, c]


def right_parts(x):
    a, b, c = split3(x)
    return [a, b, a, b, c, a]


def stack16(parts):
    return jnp.concatenate(parts, axis=0).astype(bf16)


def basis(rows):
    row = sublane()
    place = jnp.where(row < 3, 2.0 * rows - 1.0, rows)
    first = place[0:3]
    norm = jnp.sum(first * first, axis=0, keepdims=True)
    cross = jnp.sum(first * place[3:6], axis=0, keepdims=True)
    full = jnp.where(row < 6, place, jnp.where(row == 6, cross, 1.0))
    return full, norm, cross


def right_distance(full, norm):
    row = sublane()
    return jnp.where(
        row < 3, full, jnp.where(row == 3, norm, jnp.where(row == 4, 1.0, 0.0))
    )


def left_distance(full, norm):
    row = sublane()
    return jnp.where(
        row < 3, -2.0 * full, jnp.where(row == 3, 1.0, jnp.where(row == 4, norm, 0.0))
    )


def left_approach(full, cross):
    return 4.0 * jnp.concatenate(
        [-full[3:6], -full[0:3], jnp.ones((1, PART), f32), cross], axis=0
    )


def columns(parts):
    fill = 128 - 8 * len(parts)
    return jnp.concatenate(parts + [jnp.zeros((fill, PART), f32)], axis=0).T


def mass_rows(mass):
    a, b, c = split3(mass)
    return jnp.concatenate([a, b, c, jnp.zeros((13, PART), f32)], axis=0).astype(bf16)


def halves(w):
    hi = w.astype(bf16)
    return hi, (w - hi.astype(f32)).astype(bf16)


def request_kernel(pos, vel, mass, smooth, counts, dest, target, state, req, slot, used):
    lane = lax.broadcasted_iota(i32, (1, PART), 1)

    def cell(c, _):
        live = jnp.where(lane < counts[c], mass[pl.ds(c, 1), :], 0.0)
        state[c] = jnp.concatenate([pos[c], vel[c], smooth[pl.ds(c, 1), :], live], axis=0)
        return 0

    lax.fori_loop(0, CELLS, cell, 0)
    req[...] = jnp.full_like(req, -1)

    def clear(d, _):
        used[d] = 0
        return 0

    lax.fori_loop(0, req.shape[0], clear, 0)
    short = lax.broadcasted_iota(i32, (1, 128), 1)

    def entry(e, _):
        d = dest[e]
        k = used[d]
        used[d] = k + 1
        slot[e] = d * CAP + k
        req[d] = jnp.where(short == k, target[e], req[d])
        return 0

    lax.fori_loop(0, SEND, entry, 0)


def respond_kernel(state, goals, out):
    def one(s, _):
        goal = jnp.maximum(goals[s], 0)
        out[s] = state[goal]
        return 0

    lax.fori_loop(0, out.shape[0], one, 0, unroll=4)


def by_rows(need, step):
    low = 0
    for rows in ROWS:
        pl.when((need > low) & (need <= rows))(lambda rows=rows: step(rows))
        low = rows


def pipeline(first, count, rows_of, prepare, load, combine, store, work):
    last = first + count - 1

    def clamp(p):
        return jnp.minimum(p, last)

    for k in range(3):
        prepare(clamp(first + k))
    load(first, 0)

    def body(t, _):
        p = first + 2 * t

        def step(rows):
            before = jnp.maximum(p - 1, first)
            sums = combine(before, 1)
            work(p, 0, rows)
            load(p + 1, 1)
            sums0 = combine(p, 0)
            work(p + 1, 1, rows)
            load(clamp(p + 2), 0)
            store(before, sums, t > 0)
            store(p, sums0, True)
            prepare(clamp(p + 3))
            prepare(clamp(p + 4))

        by_rows(jnp.maximum(rows_of(p), rows_of(p + 1)), step)
        return 0

    lax.fori_loop(0, count // 2, body, 0)
    store(last, combine(last, 1), True)


def keep_sums(acc1, acc2, a, s, sums, valid):
    if valid is not True:
        keep = jnp.where(valid, 1.0, 0.0)
        sums = (sums[0] * keep, sums[1] * keep)
    acc1[a] += sums[0]
    acc2[s] += sums[1]


def pack_plan(far, slot, proxy_cell, offset, block_own, live, filled):
    def clear(c, _):
        filled[c] = 0
        return 0

    lax.fori_loop(0, CELLS, clear, 0)

    def measure(e, _):
        mass = far[slot[e]][7:8]
        n = jnp.sum(jnp.where(mass > 0.0, 1.0, 0.0)).astype(i32)
        live[e] = n
        a = proxy_cell[e]
        offset[e] = filled[a]
        filled[a] = filled[a] + n
        return 0

    lax.fori_loop(0, SEND, measure, 0, unroll=16)

    def place(c, total):
        blocks = (filled[c] + PART - 1) // PART
        filled[c] = total * PART

        def name(t, _):
            block_own[total + t] = c
            return 0

        lax.fori_loop(0, blocks, name, 0)
        return total + blocks

    total = lax.fori_loop(0, CELLS, place, 0)

    def shift(e, _):
        offset[e] = offset[e] + filled[proxy_cell[e]]
        return 0

    lax.fori_loop(0, SEND, shift, 0, unroll=8)
    block_own[total] = block_own[total - 1]
    return total + lax.rem(total, 2)


def pack(target, rows, offset, n):
    t = offset // PART
    lane0 = offset - t * PART
    lane = lax.broadcasted_iota(i32, rows.shape, 1)
    turned = pltpu.roll(rows, lane0, 1)
    target[t] = jnp.where((lane >= lane0) & (lane < lane0 + n), turned, target[t])
    target[t + 1] = jnp.where(lane < lane0 + n - PART, turned, target[t + 1])


def unpack(source, offset):
    t = offset // PART
    lane0 = offset - t * PART
    first, second = source[t], source[t + 1]
    lane = lax.broadcasted_iota(i32, first.shape, 1)
    return pltpu.roll(jnp.where(lane >= lane0, first, second), lax.rem(PART - lane0, PART), 1)


def own_lists(pair_first, pair_offset, pa, po, ps, dummy):
    def one(e, _):
        pa[e] = e
        po[e] = e
        ps[e] = dummy
        a = pair_first[e]
        b = lax.rem(a + pair_offset[e], CELLS)
        pa[CELLS + e] = a
        po[CELLS + e] = b
        ps[CELLS + e] = b
        return 0

    lax.fori_loop(0, CELLS, one, 0)


def nn(a, b):
    return jnp.dot(a, b, preferred_element_type=f32)


def nt(a, b):
    return lax.dot_general(a, b, (((1,), (1,)), ((), ())), preferred_element_type=f32)


def density_weights(r2, total_h):
    inv = pltpu.reciprocal(total_h, approx=True)
    inv2 = inv * inv
    q2 = jnp.maximum(r2, TINY) * inv2
    q = q2 * lax.rsqrt(q2)
    u = 2.0 - q
    t = jnp.maximum(u, 0.0)
    return jnp.minimum(t * t * t, 4.0 - 3.0 * (q2 * u)) * (inv2 * inv)


def density_pairs(count, counts, pa, po, ps, refs, prepare, acc1, acc2):
    bf, own_m, other_m, hj, at, bh, dist, ws = refs

    def load(p, side):
        dist[side][...] = nn(at[pa(p)], bf[po(p)])

    def work(p, side, rows):
        a = pa(p)
        h_j = hj[po(p)]
        for c in range(0, rows, CHUNK):
            h_i = bh[a, c : c + CHUNK, :]
            w = density_weights(
                dist[side][c : c + CHUNK, :], jnp.concatenate([h_i, h_i], axis=1) + h_j
            )
            hi, lo = halves(w)
            ws[side][c : c + CHUNK, :] = hi
            ws[side][PART + c : PART + c + CHUNK, :] = lo

    def combine(p, side):
        own = own_m[pa(p)]
        second = nn(jnp.concatenate([own, own], axis=1), ws[side][...])
        first = nt(other_m[po(p)], ws[side][...])
        return first[0:8, 0:PART] + first[0:8, PART:], second[0:8]

    def store(p, sums, valid):
        keep_sums(acc1, acc2, pa(p), ps(p), sums, valid)

    for side in range(2):
        ws[side][...] = jnp.zeros_like(ws[side])
    pipeline(0, count, lambda p: counts[pa(p)], prepare, load, combine, store, work)


def density_prepare(o, rows, bf, cj, hj):
    full, norm, cross = basis(rows)
    bf[o] = stack16(right_parts(right_distance(full, norm)))
    cj[o] = mass_rows(rows[7:8])
    hj[o] = rows[6:7]
    return full, norm, cross


def own_density_kernel(
    state, counts, pair_first, pair_offset, total, at, as_, bh, cj,
    acc1, acc2, bf, hj, dist0, dist1, ws0, ws1, pa, po, ps,
):
    def mine(c, _):
        rows = state[c]
        full, norm, cross = density_prepare(c, rows, bf, cj, hj)
        t = columns(
            left_parts(left_distance(full, norm))
            + [jnp.broadcast_to(rows[6:7], (8, PART))]
            + left_parts(left_approach(full, cross))
        )
        at[c] = t[:, 0:48].astype(bf16)
        as_[c] = t[:, 56:104].astype(bf16)
        bh[c] = jnp.broadcast_to(t[:, 48:49], (PART, 128))
        return 0

    lax.fori_loop(0, CELLS, mine, 0, unroll=2)
    own_lists(pair_first, pair_offset, pa, po, ps, CELLS)
    acc1[...] = jnp.zeros_like(acc1)
    acc2[...] = jnp.zeros_like(acc2)
    refs = (bf, cj, cj, hj, at, bh, (dist0, dist1), (ws0, ws1))
    density_pairs(
        CELLS + PAIRS, counts, lambda p: pa[p], lambda p: po[p], lambda p: ps[p], refs,
        lambda p: None, acc1, acc2,
    )
    total[...] = acc1[...] + acc2[0:CELLS]


def far_density_kernel(
    state, far, counts, slot, proxy_cell, at, bh, own_m,
    acc1, ret, blocks, offset, block_own, live, size,
    acc2, bf, cj, hj, dist0, dist1, ws0, ws1, filled,
):
    total = pack_plan(far, slot, proxy_cell, offset, block_own, live, filled)
    size[0] = total
    blocks[...] = jnp.zeros_like(blocks)

    def fill(e, _):
        pack(blocks, far[slot[e]], offset[e], live[e])
        return 0

    lax.fori_loop(0, SEND, fill, 0, unroll=8)
    acc2[...] = jnp.zeros_like(acc2)
    acc1[...] = jnp.zeros_like(acc1)
    refs = (bf, own_m, cj, hj, at, bh, (dist0, dist1), (ws0, ws1))
    same = lambda p: p
    density_pairs(
        total, counts, lambda p: block_own[p], same, same, refs,
        lambda p: density_prepare(p, blocks[p], bf, cj, hj), acc1, acc2,
    )

    def back(e, _):
        ret[slot[e]] = jnp.sum(unpack(acc2, offset[e])[0:3], axis=0, keepdims=True)
        return 0

    lax.fori_loop(0, SEND, back, 0, unroll=8)


def combine_density_kernel(
    back, goals, near, far, energy, counts, density, fluid, answer, sums
):
    sums[...] = jnp.zeros_like(sums)

    def one(s, _):
        goal = goals[s]
        sums[jnp.where(goal < 0, CELLS, goal)] += back[s]
        return 0

    lax.fori_loop(0, back.shape[0], one, 0, unroll=2)
    lane = lax.broadcasted_iota(i32, (1, PART), 1)

    def cell(c, _):
        both = near[c] + far[c]
        raw = W_SCALE * (jnp.sum(both[0:3], axis=0, keepdims=True) + sums[c])
        here = lane < counts[c]
        density[pl.ds(c, 1), :] = jnp.where(here, raw, 0.0)
        fluid[c] = jnp.concatenate(
            [jnp.where(here, raw, 1.0), energy[pl.ds(c, 1), :]], axis=0
        )
        return 0

    lax.fori_loop(0, CELLS, cell, 0)

    def send(s, _):
        answer[s] = fluid[jnp.maximum(goals[s], 0)]
        return 0

    lax.fori_loop(0, answer.shape[0], send, 0, unroll=4)


def slope_weights(r2, s, total_h):
    inv = pltpu.reciprocal(total_h, approx=True)
    inv2 = inv * inv
    q2 = jnp.maximum(r2, TINY) * inv2
    rs = lax.rsqrt(q2)
    q = q2 * rs
    u = 2.0 - q
    t = jnp.maximum(u, 0.0)
    grad = jnp.where(q < 1.0, 3.0 * u - 2.0, t * t * rs)
    m = jnp.minimum(s, 0.0) * (inv * pltpu.reciprocal(q2 + 0.01, approx=True))
    return grad * (inv2 * inv2 * inv), m


def fluid_weights(grad, m, total_c, total_p, total_r):
    return (total_p + m * (m - total_c) * pltpu.reciprocal(total_r, approx=True)) * grad


def force_fluid(fluid):
    rho, u = fluid[0:1], fluid[1:2]
    pressure = (GAMMA - 1.0) * u / rho
    sound = jnp.sqrt(GAMMA * (GAMMA - 1.0) * u)
    return pressure, sound, 4.0 * rho


def two_wide(col, row):
    return jnp.concatenate([col, col], axis=1) + row


def put_halves(ws, c, w):
    hi, lo = halves(w)
    ws[c : c + CHUNK, :] = hi
    ws[PART + c : PART + c + CHUNK, :] = lo


def fluid_work(ws, col, side_row, a, rows, grads):
    for c in range(0, rows, CHUNK):
        grad, m = grads(c)
        total = [
            two_wide(col[a, k, c : c + CHUNK, :], side_row[k + 1 : k + 2]) for k in range(3)
        ]
        put_halves(ws, c, fluid_weights(grad, m, *total))


def fold(x):
    return x[0:8] + x[8:16] + x[16:24]


def force_combine(own, other, ws):
    second = fold(nn(jnp.concatenate([own, own], axis=1), ws[...]))
    first = fold(nt(other, ws[...]))
    return first[:, 0:PART] + first[:, PART:], second


def full_force(first, count, counts, pa, po, ps, refs, prepare, acc1, acc2):
    bd, bs, own_cf, other_cf, at, as_, bh, row, col, dist, appr, ws = refs

    def load(p, side):
        a, o = pa(p), po(p)
        dist[side][...] = nn(at[a], bd[o])
        appr[side][...] = nn(as_[a], bs[o])

    def work(p, side, rows):
        a = pa(p)
        side_row = row[po(p)]

        def grads(c):
            return slope_weights(
                dist[side][c : c + CHUNK, :],
                appr[side][c : c + CHUNK, :],
                two_wide(bh[a, c : c + CHUNK, :], side_row[0:1]),
            )

        fluid_work(ws[side], col, side_row, a, rows, grads)

    def combine(p, side):
        return force_combine(own_cf[pa(p)], other_cf[po(p)], ws[side])

    def store(p, sums, valid):
        keep_sums(acc1, acc2, pa(p), ps(p), sums, valid)

    pipeline(first, count, lambda p: counts[pa(p)], prepare, load, combine, store, work)


def geometry_prepare(o, rows, bd, bs):
    full, norm, cross = basis(rows)
    bd[o] = stack16(right_parts(right_distance(full, norm)))
    bs[o] = stack16(right_parts(full))
    return full


def fluid_prepare(o, rows, full, fluid, cf, row):
    cf[o] = stack16(list(split3(rows[7:8] * full)))
    pressure, sound, rho4 = force_fluid(fluid)
    row[o] = jnp.concatenate(
        [rows[6:7], sound, pressure, rho4, jnp.zeros((4, PART), f32)], axis=0
    )


def own_fluid_columns(c, row, col):
    t = columns([row[c]])
    for k in range(3):
        col[c, k] = jnp.broadcast_to(t[:, k + 1 : k + 2], (PART, 128))


def slope_kernel(
    state_after, blocks, counts, block_own, size, at, as_, bh, out,
    bd, bs, hj, dist0, dist1, appr0, appr1, buf, sems, *, first,
):
    del state_after
    dist, appr = (dist0, dist1), (appr0, appr1)
    count = jnp.clip(size[0] - first, 0, out.shape[0])
    last = first + count - 1

    def clamp(p):
        return jnp.minimum(p, last)

    def prepare(p):
        rows = blocks[p]
        geometry_prepare(p - first, rows, bd, bs)
        hj[p - first] = rows[6:7]

    def load(p, side):
        a = block_own[p]
        dist[side][...] = nn(at[a], bd[p - first])
        appr[side][...] = nn(as_[a], bs[p - first])

    def copy(t):
        k = lax.rem(t, DEPTH)
        return pltpu.make_async_copy(buf.at[k], out.at[pl.ds(2 * t, 2)], sems.at[k])

    def work(p, side, rows, k):
        a = block_own[p]
        h_j = hj[p - first]
        for c in range(0, rows, CHUNK):
            grad, m = slope_weights(
                dist[side][c : c + CHUNK, :],
                appr[side][c : c + CHUNK, :],
                two_wide(bh[a, c : c + CHUNK, :], h_j),
            )
            buf[k, side, 0, c : c + CHUNK, :] = grad
            buf[k, side, 1, c : c + CHUNK, :] = m

    @pl.when(count > 0)
    def _():
        for k in range(3):
            prepare(clamp(first + k))
        load(first, 0)

    def body(t, _):
        p = first + 2 * t
        k = lax.rem(t, DEPTH)
        pl.when(t >= DEPTH)(lambda: copy(t - DEPTH).wait())

        def step(rows):
            load(p + 1, 1)
            work(p, 0, rows, k)
            work(p + 1, 1, rows, k)
            load(clamp(p + 2), 0)
            prepare(clamp(p + 3))
            prepare(clamp(p + 4))

        by_rows(jnp.maximum(counts[block_own[p]], counts[block_own[p + 1]]), step)
        copy(t).start()
        return 0

    steps = count // 2
    lax.fori_loop(0, steps, body, 0)

    def drain(t, _):
        copy(t).wait()
        return 0

    lax.fori_loop(jnp.maximum(steps - DEPTH, 0), steps, drain, 0)


def force_sums(rows, sums):
    full, _, cross = basis(rows)
    count = sums[7:8]
    accel = (-0.5 * K_SCALE) * (full[0:3] * count - sums[0:3])
    mixed = jnp.sum(full[3:6] * sums[0:3] + full[0:3] * sums[3:6], axis=0, keepdims=True)
    heat = (0.25 * K_SCALE) * (cross * count - mixed + sums[6:7])
    return jnp.concatenate([accel, heat], axis=0)


def own_force_kernel(
    after, state, fluid, counts, pair_first, pair_offset, at, as_, bh, total,
    acc1, acc2, bd, bs, cf, row, col, dist0, dist1, appr0, appr1, ws0, ws1, pa, po, ps,
):
    del after

    def mine(c, _):
        rows = state[c]
        fluid_prepare(c, rows, geometry_prepare(c, rows, bd, bs), fluid[c], cf, row)
        own_fluid_columns(c, row, col)
        return 0

    lax.fori_loop(0, CELLS, mine, 0, unroll=2)
    own_lists(pair_first, pair_offset, pa, po, ps, CELLS)
    acc1[...] = jnp.zeros_like(acc1)
    acc2[...] = jnp.zeros_like(acc2)
    ws0[...] = jnp.zeros_like(ws0)
    ws1[...] = jnp.zeros_like(ws1)
    refs = (bd, bs, cf, cf, at, as_, bh, row, col, (dist0, dist1), (appr0, appr1), (ws0, ws1))
    full_force(
        0, CELLS + PAIRS, counts, lambda p: pa[p], lambda p: po[p], lambda p: ps[p], refs,
        lambda p: None, acc1, acc2,
    )
    total[...] = acc1[...] + acc2[0:CELLS]


def far_force_kernel(
    state, fluid, blocks, far_fluid, counts, slot, offset, block_own, live, size, at, as_, bh,
    ready0, ready1, acc1, ret,
    acc2, fluids, bd, bs, own_cf, own_row, cf, row, col,
    dist0, dist1, appr0, appr1, ws0, ws1, buf, sems,
):
    total = size[0]
    half = ready0.shape[0] // 2
    steps = jnp.minimum(total, ready0.shape[0] + ready1.shape[0]) // 2

    def start(t):
        k = lax.rem(t, DEPTH)

        @pl.when(t < half)
        def _():
            pltpu.make_async_copy(ready0.at[pl.ds(2 * t, 2)], buf.at[k], sems.at[k]).start()

        @pl.when(t >= half)
        def _():
            pltpu.make_async_copy(
                ready1.at[pl.ds(2 * (t - half), 2)], buf.at[k], sems.at[k]
            ).start()

    def wait(t):
        k = lax.rem(t, DEPTH)
        pltpu.make_async_copy(ready0.at[pl.ds(0, 2)], buf.at[k], sems.at[k]).wait()

    for t in range(DEPTH - 1):
        pl.when(t < steps)(lambda t=t: start(t))

    def mine(c, _):
        rows = state[c]
        fluid_prepare(c, rows, basis(rows)[0], fluid[c], own_cf, own_row)
        own_fluid_columns(c, own_row, col)
        return 0

    lax.fori_loop(0, CELLS, mine, 0, unroll=2)
    fluids[...] = jnp.ones_like(fluids)

    def fill(e, _):
        pack(fluids, far_fluid[slot[e]], offset[e], live[e])
        return 0

    lax.fori_loop(0, SEND, fill, 0, unroll=8)
    acc1[...] = jnp.zeros_like(acc1)
    acc2[...] = jnp.zeros_like(acc2)
    ws0[...] = jnp.zeros_like(ws0)
    ws1[...] = jnp.zeros_like(ws1)
    ws = (ws0, ws1)

    def prepare(p):
        rows = blocks[p]
        fluid_prepare(p, rows, basis(rows)[0], fluids[p], cf, row)

    last = 2 * steps - 1
    for k in range(2):
        prepare(jnp.int32(k))

    def combine(p, side):
        return force_combine(own_cf[block_own[p]], cf[p], ws[side])

    def store(p, sums, valid):
        keep_sums(acc1, acc2, block_own[p], p, sums, valid)

    def body(t, _):
        p = 2 * t
        k = lax.rem(t, DEPTH)
        pl.when(t + DEPTH - 1 < steps)(lambda: start(t + DEPTH - 1))
        wait(t)

        def work(p, side, rows):
            def grads(c):
                return buf[k, side, 0, c : c + CHUNK, :], buf[k, side, 1, c : c + CHUNK, :]

            fluid_work(ws[side], col, row[p], block_own[p], rows, grads)

        def step(rows):
            before = jnp.maximum(p - 1, 0)
            sums = combine(before, 1)
            work(p, 0, rows)
            sums0 = combine(p, 0)
            work(p + 1, 1, rows)
            store(before, sums, t > 0)
            store(p, sums0, True)
            prepare(jnp.minimum(p + 2, last))
            prepare(jnp.minimum(p + 3, last))

        by_rows(jnp.maximum(counts[block_own[p]], counts[block_own[p + 1]]), step)
        return 0

    lax.fori_loop(0, steps, body, 0)
    store(last, combine(last, 1), True)

    @pl.when(total > 2 * steps)
    def _():
        def rest(p):
            rows = blocks[p]
            fluid_prepare(p, rows, geometry_prepare(p, rows, bd, bs), fluids[p], cf, row)

        refs = (
            bd, bs, own_cf, cf, at, as_, bh, row, col, (dist0, dist1), (appr0, appr1), ws,
        )
        same = lambda p: p
        full_force(
            2 * steps, total - 2 * steps, counts, lambda p: block_own[p], same, same, refs,
            rest, acc1, acc2,
        )

    def turn(t, _):
        acc2[t, 0:4] = force_sums(blocks[t], acc2[t])
        return 0

    lax.fori_loop(0, total // 2, lambda t, _: turn(2 * t, 0) + turn(2 * t + 1, 0), 0)

    def back(e, _):
        ret[slot[e]] = unpack(acc2, offset[e])[0:4]
        return 0

    lax.fori_loop(0, SEND, back, 0, unroll=8)


def finish_kernel(
    back, goals, near, far, state, energy, counts, mig_cell, mig_dest, accel, leave, sums, moved, used
):
    sums[...] = jnp.zeros_like(sums)

    def one(s, _):
        goal = goals[s]
        sums[jnp.where(goal < 0, CELLS, goal)] += back[s]
        return 0

    lax.fori_loop(0, back.shape[0], one, 0, unroll=2)
    lane = lax.broadcasted_iota(i32, (1, PART), 1)

    def cell(c, _):
        rows = state[c]
        here = lane < counts[c]
        total = jnp.where(here, force_sums(rows, near[c] + far[c]) + sums[c], 0.0)
        accel[c] = total
        new_vel = rows[3:6] + STEP * total[0:3]
        new_pos = rows[0:3] + STEP * new_vel
        new_energy = energy[pl.ds(c, 1), :] + STEP * total[3:4]
        kicked = jnp.concatenate(
            [new_pos, new_vel, rows[7:8], rows[6:7], new_energy], axis=0
        )
        moved[c] = jnp.where(here, kicked, 0.0)
        return 0

    lax.fori_loop(0, CELLS, cell, 0)
    leave[...] = jnp.zeros_like(leave)

    def clear(d, _):
        used[d] = 0
        return 0

    lax.fori_loop(0, leave.shape[0] // CAPM, clear, 0)

    def entry(e, _):
        d = mig_dest[e]
        k = used[d]
        used[d] = k + 1
        leave[d * CAPM + k] = moved[mig_cell[e]]
        return 0

    lax.fori_loop(0, mig_cell.shape[0], entry, 0)


def vmem(*dims, dtype=f32):
    return pltpu.VMEM(dims, dtype)


def smem(*dims):
    return pltpu.SMEM(dims, i32)


WS = [vmem(2 * PART, PART, dtype=bf16)] * 2
SQUARE = [vmem(PART, PART)] * 2


def own_density(state, counts, pair_first, pair_offset):
    return kernel_call(
        own_density_kernel,
        (
            shape(CELLS, 8, PART),
            shape(CELLS, PART, 48, dtype=bf16),
            shape(CELLS, PART, 48, dtype=bf16),
            shape(CELLS, PART, 128),
            shape(CELLS, 16, PART, dtype=bf16),
        ),
        [VMEM] + [SMEM] * 3,
        (VMEM,) * 5,
        [
            vmem(CELLS, 8, PART),
            vmem(CELLS + 1, 8, PART),
            vmem(CELLS, 48, PART, dtype=bf16),
            vmem(CELLS, 1, PART),
        ]
        + SQUARE
        + WS
        + [smem(CELLS + PAIRS)] * 3,
        flops=32 * PART * PART * 300,
        moved=2**20,
    )(state, counts, pair_first, pair_offset)


def far_density(state, far, counts, slot, proxy_cell, at, bh, own_m):
    return kernel_call(
        far_density_kernel,
        (
            shape(CELLS, 8, PART),
            shape(far.shape[0], 1, PART),
            shape(BLOCKS + 1, 8, PART),
            shape(SEND, dtype=i32),
            shape(BLOCKS, dtype=i32),
            shape(SEND, dtype=i32),
            shape(1, dtype=i32),
        ),
        [VMEM] * 2 + [SMEM] * 3 + [VMEM] * 3,
        (VMEM,) * 3 + (SMEM,) * 4,
        [
            vmem(BLOCKS + 1, 8, PART),
            vmem(BLOCKS, 48, PART, dtype=bf16),
            vmem(BLOCKS, 16, PART, dtype=bf16),
            vmem(BLOCKS, 1, PART),
        ]
        + SQUARE
        + WS
        + [smem(CELLS)],
        flops=128 * PART * PART * 300,
        moved=2**20,
    )(state, far, counts, slot, proxy_cell, at, bh, own_m)


def slopes(after, first, count, blocks, counts, block_own, size, at, as_, bh):
    def body(*refs):
        slope_kernel(*refs, first=first)

    return kernel_call(
        body,
        shape(count, 2, PART, PART),
        [ANY, VMEM] + [SMEM] * 3 + [VMEM] * 3,
        ANY,
        [
            vmem(count, 48, PART, dtype=bf16),
            vmem(count, 48, PART, dtype=bf16),
            vmem(count, 1, PART),
        ]
        + SQUARE * 2
        + [vmem(DEPTH, 2, 2, PART, PART), pltpu.SemaphoreType.DMA((DEPTH,))],
        flops=count * PART * PART * 400,
        moved=count * 2**19,
    )(after, blocks, counts, block_own, size, at, as_, bh)


def far_force(
    state, fluid, far_fluid, counts, slot, blocks, offset, block_own, live, size, at, as_, bh,
    ready0, ready1,
):
    return kernel_call(
        far_force_kernel,
        (shape(CELLS, 8, PART), shape(far_fluid.shape[0], 4, PART)),
        [VMEM] * 4 + [SMEM] * 6 + [VMEM] * 3 + [ANY] * 2,
        (VMEM, VMEM),
        [
            vmem(BLOCKS + 1, 8, PART),
            vmem(BLOCKS + 1, 2, PART),
            vmem(BLOCKS, 48, PART, dtype=bf16),
            vmem(BLOCKS, 48, PART, dtype=bf16),
            vmem(CELLS, 24, PART, dtype=bf16),
            vmem(CELLS, 8, PART),
            vmem(BLOCKS, 24, PART, dtype=bf16),
            vmem(BLOCKS, 8, PART),
            vmem(CELLS, 3, PART, 128),
        ]
        + SQUARE * 2
        + WS
        + [vmem(DEPTH, 2, 2, PART, PART), pltpu.SemaphoreType.DMA((DEPTH,))],
        flops=128 * PART * PART * 300,
        moved=2**20,
    )(
        state, fluid, blocks, far_fluid, counts, slot, offset, block_own, live, size,
        at, as_, bh, ready0, ready1,
    )


def own_force(after, state, fluid, counts, pair_first, pair_offset, at, as_, bh):
    return kernel_call(
        own_force_kernel,
        shape(CELLS, 8, PART),
        [ANY] + [VMEM] * 2 + [SMEM] * 3 + [VMEM] * 3,
        VMEM,
        [
            vmem(CELLS, 8, PART),
            vmem(CELLS + 1, 8, PART),
            vmem(CELLS, 48, PART, dtype=bf16),
            vmem(CELLS, 48, PART, dtype=bf16),
            vmem(CELLS, 24, PART, dtype=bf16),
            vmem(CELLS, 8, PART),
            vmem(CELLS, 3, PART, 128),
        ]
        + SQUARE * 2
        + WS
        + [smem(CELLS + PAIRS)] * 3,
        flops=32 * PART * PART * 600,
        moved=2**20,
    )(after, state, fluid, counts, pair_first, pair_offset, at, as_, bh)


def exchange(x, axes):
    return lax.all_to_all(x, axes, split_axis=0, concat_axis=0, tiled=True)


def local(
    position, velocity, mass, smoothing, energy, counts, proxy_cell, proxy_dest,
    proxy_target, pair_first, pair_offset, mig_cell, mig_dest,
):
    devices = lax.axis_size(("rows", "cols"))
    col_count = lax.axis_size("cols")
    slots = devices * CAP
    both = ("rows", "cols")
    state, req, slot = kernel_call(
        request_kernel,
        (shape(CELLS, 8, PART), shape(devices, 1, 128, dtype=i32), shape(SEND, dtype=i32)),
        [VMEM] * 4 + [SMEM] * 3,
        (VMEM, VMEM, SMEM),
        [pltpu.SMEM((devices,), i32)],
        moved=2**20,
    )(position, velocity, mass, smoothing, counts, proxy_dest[:, 0], proxy_target)
    goals = exchange(req, both)[:, 0, 0:CAP].reshape(slots)
    near, at, as_, bh, own_m = own_density(state, counts, pair_first, pair_offset)
    answer = kernel_call(
        respond_kernel, shape(slots, 8, PART), [VMEM, SMEM], VMEM, moved=4 * 2**20
    )(state, goals)
    far = exchange(answer, both)
    far_sums, ret, *plan = far_density(state, far, counts, slot, proxy_cell, at, bh, own_m)
    blocks, offset, block_own, live, size = plan
    ready0 = slopes(far_sums, 0, EARLY, blocks, counts, block_own, size, at, as_, bh)
    back = exchange(ret, both)
    density, fluid, answer2 = kernel_call(
        combine_density_kernel,
        (shape(CELLS, PART), shape(CELLS, 2, PART), shape(slots, 2, PART)),
        [VMEM, SMEM] + [VMEM] * 3 + [SMEM],
        (VMEM, VMEM, VMEM),
        [pltpu.VMEM((CELLS + 1, 1, PART), f32)],
        moved=2**20,
    )(back, goals, near, far_sums, energy, counts)
    far_fluid = exchange(answer2, both)
    ready1 = slopes(fluid, EARLY, LATE, blocks, counts, block_own, size, at, as_, bh)
    far_force_sums, ret4 = far_force(
        state, fluid, far_fluid, counts, slot, *plan, at, as_, bh, ready0, ready1
    )
    near_force = own_force(
        far_force_sums, state, fluid, counts, pair_first, pair_offset, at, as_, bh
    )
    back4 = exchange(ret4, both)
    accel, leave = kernel_call(
        finish_kernel,
        (shape(CELLS, 4, PART), shape(col_count * CAPM, 9, PART)),
        [VMEM, SMEM] + [VMEM] * 4 + [SMEM] * 3,
        (VMEM, VMEM),
        [
            pltpu.VMEM((CELLS + 1, 4, PART), f32),
            pltpu.VMEM((CELLS, 9, PART), f32),
            pltpu.SMEM((col_count,), i32),
        ],
        moved=2**20,
    )(back4, goals, near_force, far_force_sums, state, energy, counts, mig_cell, mig_dest[:, 0])
    arrived = exchange(leave, "cols")
    return (density, accel, arrived)


def solution(mesh):
    lead = ("rows", "cols")
    one, two, three = P(lead), P(lead, None), P(lead, None, None)
    return jax.shard_map(
        local,
        mesh=mesh,
        in_specs=(three, three, two, two, two, one, one, two, one, one, one, one, two),
        out_specs=(two, three, three),
        check_vma=False,
    )
```

time: 277 us -> 254 us (0.917)
  blocking collectives: 99.2 us -> 55.5 us
  waiting for transfers between devices: 0.01 us -> 16.1 us
  starting transfers between devices: 15.7 us -> 20.5 us
    all_to_all x4 -> x3, blocking collectives: 99.2 us -> 55.5 us  [exchange(): return lax.all_to_all(x, axes, split_axis=0, concat_axis=0, tiled=True)]
    all_to_all x2 -> x3, waiting for transfers between devices: 0.01 us -> 16.1 us  [exchange(): return lax.all_to_all(x, axes, split_axis=0, concat_axis=0, tiled=True)]
    all_to_all x2 -> x3, starting transfers between devices: 15.7 us -> 20.5 us  [exchange(): return lax.all_to_all(x, axes, split_axis=0, concat_axis=0, tiled=True)]
    pallas_call x4 -> x6, Pallas kernels: 138 us -> 136 us  [the longest x1 37.3 us: far_force(): kernel_call(far_force_kernel, (shape(CELLS, 8, PART), shape(far_fluid.sha...]
    unnamed x7 -> x9, local copies, waits for them, and re-layouts: 5.48 us -> 6.92 us
  transfers between devices with their start and end apart: 2 -> 3, of which waited for: 0 -> 1; matrix products, arithmetic and copies ran while one was open for 0% -> 0% of each run, Pallas kernels for 13% -> 26%
where the time goes in v3:
time: 254 us; the launch traced here: 252 us
  Pallas kernels  152 us (60%)
  blocking collectives  55.5 us (22%)
  starting transfers between devices  20.5 us (8%)
  waiting for transfers between devices  16.1 us (6%)
  local copies, waits for them, and re-layouts  7.81 us (3%)
    all_to_all x3, blocking collectives, exchange(): return lax.all_to_all(x, axes, split_axis=0, concat_axis=0, tiled=True)  55.5 us
    pallas_call x1, Pallas kernels, far_force(): kernel_call(far_force_kernel, (shape(CELLS, 8, PART), shape(far_fluid.sha...  37.3 us
    pallas_call x1, Pallas kernels, far_density(): kernel_call(far_density_kernel, (shape(CELLS, 8, PART), shape(far.shape[0...  34.3 us
    pallas_call x2, Pallas kernels, slopes(): kernel_call(body, shape(count, 2, PART, PART), [ANY, VMEM] + [SMEM] * 3 +...  31.8 us
    all_to_all x3, starting transfers between devices, exchange(): return lax.all_to_all(x, axes, split_axis=0, concat_axis=0, tiled=True)  20.5 us
    pallas_call x1, Pallas kernels, own_force(): kernel_call(own_force_kernel, shape(CELLS, 8, PART), [ANY] + [VMEM] * 2 +...  19.2 us
    all_to_all x3, waiting for transfers between devices, exchange(): return lax.all_to_all(x, axes, split_axis=0, concat_axis=0, tiled=True)  16.1 us
    pallas_call x1, Pallas kernels, own_density(): kernel_call(own_density_kernel, (shape(CELLS, 8, PART), shape(CELLS, PART...  13.6 us
  transfers between devices with their start and end apart: 3, of which 1 were waited for; matrix products, arithmetic and copies ran while one was open for 0% of the time, Pallas kernels for 26%

profile of v3, /device:TPU:0, one launch (start us, length us, event | category | flops | bytes accessed | tf_op | source)
XLA Modules:
  0.0 252.3 jit_solution(4005754841511979324)
XLA Ops:
  0.6 1.5 copy.19.pos
  2.1 1.5 copy.20.vel
  3.6 3.7 %shard_map.148 = (f32[16,8,256]{2,1,0:T(8,128)}, s32[128,1,128]{2,1,0:T(1,128)}, s32[128]{0:T(128)}) custom-call(f32[16,3,256]{2,1,0:T(4,128)} %copy.19.pos, f32[16,3,256]{2,1,0:T(4,128)} %copy.20.vel, f32[16,256]{1,0:T(8,128)} %mass.1, f32[16,256]{1,0:T(8,128)} %smooth.1, s32[16]{0:T(128)} %counts.13, s32[128]{0:T(128)} %bitcast.2, s32[128]{0:T(128)} %target.1), custom_call_target="tpu_custom_call" | custom-call | bytes 1048576 | tf_op jit(solution)/shard_map/pallas_call | solution.py:956
  7.3 20.6 %all_to_all.30 = s32[128,1,128]{2,1,0:T(1,128)S(1)} all-to-all(s32[128,1,128]{2,1,0:T(1,128)} %get-tuple-element.26), channel_id=1, replica_groups=mesh['rows'=8,'cols'=16] {'rows','cols'}, dimensions={0} | all-to-all | bytes 131072 | tf_op jit(solution)/shard_map/all_to_all | solution.py:945
  27.9 0.2 slice_reduce_fusion
  28.1 0.7 reshape_squeeze.3.goals
  28.8 3.0 %shard_map.149 = f32[256,8,256]{2,1,0:T(8,128)} custom-call(f32[16,8,256]{2,1,0:T(8,128)} %get-tuple-element.25.state, s32[256]{0:T(256)} %reshape_squeeze.3.goals), custom_call_target="tpu_custom_call" | custom-call | bytes 4194304 | tf_op jit(solution)/shard_map/pallas_call | solution.py:966
  31.8 4.6 %all-to-all-start.1 = ((f32[256,8,256]{2,1,0:T(8,128)}), f32[256,8,256]{2,1,0:T(8,128)S(1)}, u32[]{:S(2)}, u32[]{:S(2)}) async-start(f32[256,8,256]{2,1,0:T(8,128)} %shard_map.149), calls=%async_computation.1 | async-start | bytes 4194304 | tf_op jit(solution)/shard_map/all_to_all | solution.py:945
  36.4 13.6 %shard_map.150 = (f32[16,8,256]{2,1,0:T(8,128)}, bf16[16,256,48]{2,1,0:T(8,128)(2,1)}, bf16[16,256,48]{2,1,0:T(8,128)(2,1)}, f32[16,256,128]{2,1,0:T(8,128)}, bf16[16,16,256]{2,1,0:T(8,128)(2,1)}) custom-call(f32[16,8,256]{2,1,0:T(8,128)} %get-tuple-element.25.state, s32[16]{0:T(128)} %counts.13, s32[16]{0:T(128)} %pair_first.3, s32[16]{0:T(128)} %pair_offset.3), custom_call_target="tpu_custom_call" | custom-call | flops 629145600 | bytes 1048576 | tf_op jit(solution)/shard_map/pallas_call | solution.py:816
  50.0 16.1 %all-to-all-done.1.far = f32[256,8,256]{2,1,0:T(8,128)S(1)} async-done(((f32[256,8,256]{2,1,0:T(8,128)}), f32[256,8,256]{2,1,0:T(8,128)S(1)}, u32[]{:S(2)}, u32[]{:S(2)}) %all-to-all-start.1) | async-done | bytes 2097184 | tf_op jit(solution)/shard_map/all_to_all | solution.py:945
  66.1 0.0 copy-start.2
  66.1 1.3 copy-done.2
  67.5 34.3 %shard_map.151 = (f32[16,8,256]{2,1,0:T(8,128)}, f32[256,1,256]{2,1,0:T(1,128)}, f32[145,8,256]{2,1,0:T(8,128)}, s32[128]{0:T(128)}, s32[144]{0:T(256)}, /*index=5*/s32[128]{0:T(128)}, s32[1]{0:T(128)}) custom-call(f32[16,8,256]{2,1,0:T(8,128)} %get-tuple-element.25.state, f32[256,8,256]{2,1,0:T(8,128)} %copy-done.2, s32[16]{0:T(128)} %counts.13, ...), custom_call_target="tpu_custom_call" | custom-call | flops 2516582400 | bytes 1048576 | tf_op jit(solution)/shard_map/pallas_call | solution.py:842
  101.8 16.6 %all_to_all.31.back = f32[256,1,256]{2,1,0:T(1,128)} all-to-all(f32[256,1,256]{2,1,0:T(1,128)} %get-tuple-element.31), channel_id=1, replica_groups=mesh['rows'=8,'cols'=16] {'rows','cols'}, dimensions={0} | all-to-all | bytes 524288 | tf_op jit(solution)/shard_map/all_to_all | solution.py:945
  118.4 4.3 %shard_map.152 = (f32[16,256]{1,0:T(8,128)}, f32[16,2,256]{2,1,0:T(2,128)}, f32[256,2,256]{2,1,0:T(2,128)}) custom-call(f32[256,1,256]{2,1,0:T(1,128)} %all_to_all.31.back, s32[256]{0:T(256)} %reshape_squeeze.3.goals, f32[16,8,256]{2,1,0:T(8,128)} %get-tuple-element.32.near, f32[16,8,256]{2,1,0:T(8,128)} %get-tuple-element.33.far.refs_0_, f32[16,256]{1,0:T(8,128)} %energy.3, ...), custom_call_target="tpu_custom_call" | custom-call | bytes 1048576 | tf_op jit(solution)/shard_map/pallas_call | solution.py:974
  122.7 4.6 %all-to-all-start.3 = ((f32[256,2,256]{2,1,0:T(2,128)}), f32[256,2,256]{2,1,0:T(2,128)S(1)}, u32[]{:S(2)}, u32[]{:S(2)}) async-start(f32[256,2,256]{2,1,0:T(2,128)} %get-tuple-element.37), calls=%async_computation.3 | async-start | bytes 1048576 | tf_op jit(solution)/shard_map/all_to_all | solution.py:945
  127.3 15.1 %shard_map.153.ready0 = f32[42,2,256,256]{3,2,1,0:T(8,128)} custom-call(f32[16,8,256]{2,1,0:T(8,128)} %get-tuple-element.33.far.refs_0_, f32[145,8,256]{2,1,0:T(8,128)} %get-tuple-element.36.refs_1_.blocks, s32[16]{0:T(128)} %counts.13, s32[144]{0:T(256)} %get-tuple-element.39.refs_3_.block_own, s32[1]{0:T(128)} %get-tuple-element.41.refs_4_.size, ...), custom_call_target="tpu_custom_call" | custom-call | flops 1101004800 | bytes 22020096 | tf_op jit(solution)/shard_map/pallas_call | solution.py:873
  142.4 16.7 %shard_map.154.ready1 = f32[48,2,256,256]{3,2,1,0:T(8,128)} custom-call(f32[16,2,256]{2,1,0:T(2,128)} %get-tuple-element.35.refs_0_.fluid, f32[145,8,256]{2,1,0:T(8,128)} %get-tuple-element.36.refs_1_.blocks, s32[16]{0:T(128)} %counts.13, s32[144]{0:T(256)} %get-tuple-element.39.refs_3_.block_own, s32[1]{0:T(128)} %get-tuple-element.41.refs_4_.size, ...), custom_call_target="tpu_custom_call" | custom-call | flops 1258291200 | bytes 25165824 | tf_op jit(solution)/shard_map/pallas_call | solution.py:873
  159.1 0.0 all-to-all-done.3.far_fluid
  159.1 0.0 copy-start.1
  159.1 0.8 copy-done.1
  159.9 37.3 %shard_map.155 = (f32[16,8,256]{2,1,0:T(8,128)}, f32[256,4,256]{2,1,0:T(4,128)}) custom-call(f32[16,8,256]{2,1,0:T(8,128)} %get-tuple-element.25.state, f32[16,2,256]{2,1,0:T(2,128)} %get-tuple-element.35.refs_0_.fluid, f32[145,8,256]{2,1,0:T(8,128)} %get-tuple-element.36.refs_1_.blocks, f32[256,2,256]{2,1,0:T(2,128)} %copy-done.1, s32[16]{0:T(128)} %counts.13, ...), custom_call_target="tpu_custom_call" | custom-call | flops 2516582400 | bytes 1048576 | tf_op jit(solution)/shard_map/pallas_call | solution.py:894
  197.2 11.3 %all-to-all-start.4 = ((f32[256,4,256]{2,1,0:T(4,128)}), f32[256,4,256]{2,1,0:T(4,128)S(1)}, u32[]{:S(2)}, u32[]{:S(2)}) async-start(f32[256,4,256]{2,1,0:T(4,128)} %get-tuple-element.43), calls=%async_computation.4 | async-start | bytes 2097152 | tf_op jit(solution)/shard_map/all_to_all | solution.py:945
  208.5 19.2 %shard_map.156.near = f32[16,8,256]{2,1,0:T(8,128)} custom-call(f32[16,8,256]{2,1,0:T(8,128)} %get-tuple-element.44.after.far, f32[16,8,256]{2,1,0:T(8,128)} %get-tuple-element.25.state, f32[16,2,256]{2,1,0:T(2,128)} %get-tuple-element.35.refs_0_.fluid, s32[16]{0:T(128)} %counts.13, s32[16]{0:T(128)} %pair_first.3, s32[16]{0:T(128)} %pair_offset.3, ...), custom_call_target="tpu_custom_call" | custom-call | flops 1258291200 | bytes 1048576 | tf_op jit(solution)/shard_map/pallas_call | solution.py:922
  227.7 0.0 all-to-all-done.4.back
  227.7 0.0 copy-start
  227.7 1.0 copy-done
  228.7 4.6 %shard_map.157 = (f32[16,4,256]{2,1,0:T(4,128)}, f32[32,9,256]{2,1,0:T(8,128)}) custom-call(f32[256,4,256]{2,1,0:T(4,128)} %copy-done, s32[256]{0:T(256)} %reshape_squeeze.3.goals, f32[16,8,256]{2,1,0:T(8,128)} %shard_map.156.near, f32[16,8,256]{2,1,0:T(8,128)} %get-tuple-element.44.after.far, f32[16,8,256]{2,1,0:T(8,128)} %get-tuple-element.25.state, ...), custom_call_target="tpu_custom_call" | custom-call | bytes 1048576 | tf_op jit(solution)/shard_map/pallas_call | solution.py:991
  233.2 18.2 %all_to_all.32 = f32[32,9,256]{2,1,0:T(8,128)S(1)} all-to-all(f32[32,9,256]{2,1,0:T(8,128)} %get-tuple-element.46), channel_id=1, replica_groups=mesh['rows'=8,'cols'=16] {'cols'}, dimensions={0} | all-to-all | bytes 589824 | tf_op jit(solution)/shard_map/all_to_all | solution.py:945
  251.4 0.9 copy.21
Async XLA Ops:
  31.8 34.4 %all-to-all-start.1 = ((f32[256,8,256]{2,1,0:T(8,128)}), f32[256,8,256]{2,1,0:T(8,128)S(1)}, u32[]{:S(2)}, u32[]{:S(2)}) async-start(f32[256,8,256]{2,1,0:T(8,128)} %shard_map.149), calls=%async_computation.1 | async-start | bytes 4194304 | tf_op jit(solution)/shard_map/all_to_all | solution.py:945
  66.1 1.3 copy-start.2
  122.7 36.4 %all-to-all-start.3 = ((f32[256,2,256]{2,1,0:T(2,128)}), f32[256,2,256]{2,1,0:T(2,128)S(1)}, u32[]{:S(2)}, u32[]{:S(2)}) async-start(f32[256,2,256]{2,1,0:T(2,128)} %get-tuple-element.37), calls=%async_computation.3 | async-start | bytes 1048576 | tf_op jit(solution)/shard_map/all_to_all | solution.py:945
  159.1 0.8 copy-start.1
  197.2 30.5 %all-to-all-start.4 = ((f32[256,4,256]{2,1,0:T(4,128)}), f32[256,4,256]{2,1,0:T(4,128)S(1)}, u32[]{:S(2)}, u32[]{:S(2)}) async-start(f32[256,4,256]{2,1,0:T(4,128)} %get-tuple-element.43), calls=%async_computation.4 | async-start | bytes 2097152 | tf_op jit(solution)/shard_map/all_to_all | solution.py:945
  227.7 1.0 copy-start

commit v4 on v3

--- a/solution.py
+++ b/solution.py
@@ -21,7 +21,7 @@
 CHUNK = 32
 ROWS = (128, 160, 192, 224, 256)
 BLOCKS = SEND + CELLS
-EARLY, LATE = 42, 48
+EARLY, LATE = 42, 50
 DEPTH = 4
 
 f32, bf16, i32 = jnp.float32, jnp.bfloat16, jnp.int32
@@ -106,32 +106,19 @@
     return jnp.concatenate(parts + [jnp.zeros((fill, PART), f32)], axis=0).T
 
 
-def mass_rows(mass):
-    a, b, c = split3(mass)
-    return jnp.concatenate([a, b, c, jnp.zeros((13, PART), f32)], axis=0).astype(bf16)
-
-
 def halves(w):
     hi = w.astype(bf16)
     return hi, (w - hi.astype(f32)).astype(bf16)
 
 
-def request_kernel(pos, vel, mass, smooth, counts, dest, target, state, req, slot, used):
-    lane = lax.broadcasted_iota(i32, (1, PART), 1)
-
-    def cell(c, _):
-        live = jnp.where(lane < counts[c], mass[pl.ds(c, 1), :], 0.0)
-        state[c] = jnp.concatenate([pos[c], vel[c], smooth[pl.ds(c, 1), :], live], axis=0)
-        return 0
-
-    lax.fori_loop(0, CELLS, cell, 0)
+def request_kernel(dest, target, req, slot, used):
     req[...] = jnp.full_like(req, -1)
 
     def clear(d, _):
         used[d] = 0
         return 0
 
-    lax.fori_loop(0, req.shape[0], clear, 0)
+    lax.fori_loop(0, req.shape[0], clear, 0, unroll=8)
     short = lax.broadcasted_iota(i32, (1, 128), 1)
 
     def entry(e, _):
@@ -142,7 +129,7 @@
         req[d] = jnp.where(short == k, target[e], req[d])
         return 0
 
-    lax.fori_loop(0, SEND, entry, 0)
+    lax.fori_loop(0, SEND, entry, 0, unroll=4)
 
 
 def respond_kernel(state, goals, out):
@@ -247,8 +234,8 @@
     lane0 = offset - t * PART
     lane = lax.broadcasted_iota(i32, rows.shape, 1)
     turned = pltpu.roll(rows, lane0, 1)
-    target[t] = jnp.where((lane >= lane0) & (lane < lane0 + n), turned, target[t])
-    target[t + 1] = jnp.where(lane < lane0 + n - PART, turned, target[t + 1])
+    pltpu.store(target.at[t], turned, mask=(lane >= lane0) & (lane < lane0 + n))
+    pltpu.store(target.at[t + 1], turned, mask=lane < lane0 + n - PART)
 
 
 def unpack(source, offset):
@@ -292,82 +279,127 @@
     return jnp.minimum(t * t * t, 4.0 - 3.0 * (q2 * u)) * (inv2 * inv)
 
 
+def two_wide(col, row):
+    return jnp.concatenate([col, col], axis=1) + row
+
+
 def density_pairs(count, counts, pa, po, ps, refs, prepare, acc1, acc2):
-    bf, own_m, other_m, hj, at, bh, dist, ws = refs
+    bf, hj, mj, at, bh, bm, dist = refs
 
     def load(p, side):
         dist[side][...] = nn(at[pa(p)], bf[po(p)])
 
     def work(p, side, rows):
-        a = pa(p)
-        h_j = hj[po(p)]
+        a, o = pa(p), po(p)
+        h_j, m_j = hj[o], mj[o]
+        second = jnp.zeros((8, PART), f32)
         for c in range(0, rows, CHUNK):
-            h_i = bh[a, c : c + CHUNK, :]
             w = density_weights(
-                dist[side][c : c + CHUNK, :], jnp.concatenate([h_i, h_i], axis=1) + h_j
+                dist[side][c : c + CHUNK, :], two_wide(bh[a, c : c + CHUNK, :], h_j)
             )
-            hi, lo = halves(w)
-            ws[side][c : c + CHUNK, :] = hi
-            ws[side][PART + c : PART + c + CHUNK, :] = lo
-
-    def combine(p, side):
-        own = own_m[pa(p)]
-        second = nn(jnp.concatenate([own, own], axis=1), ws[side][...])
-        first = nt(other_m[po(p)], ws[side][...])
-        return first[0:8, 0:PART] + first[0:8, PART:], second[0:8]
-
-    def store(p, sums, valid):
-        keep_sums(acc1, acc2, pa(p), ps(p), sums, valid)
-
-    for side in range(2):
-        ws[side][...] = jnp.zeros_like(ws[side])
-    pipeline(0, count, lambda p: counts[pa(p)], prepare, load, combine, store, work)
-
-
-def density_prepare(o, rows, bf, cj, hj):
+            first = w * m_j
+            acc1[a, c : c + CHUNK, :] += first[:, 0:128] + first[:, 128:256]
+            m_i = bm[a, c : c + CHUNK, :]
+            other = w * jnp.concatenate([m_i, m_i], axis=1)
+            second += jnp.sum(other.reshape(CHUNK // 8, 8, PART), axis=0)
+        acc2[ps(p)] += jnp.sum(second, axis=0, keepdims=True)
+
+    last = count - 1
+
+    def clamp(p):
+        return jnp.minimum(p, last)
+
+    for k in range(3):
+        prepare(clamp(k))
+    load(0, 0)
+
+    def body(t, _):
+        p = 2 * t
+
+        def step(rows):
+            load(p + 1, 1)
+            work(p, 0, rows)
+            work(p + 1, 1, rows)
+            load(clamp(p + 2), 0)
+            prepare(clamp(p + 3))
+            prepare(clamp(p + 4))
+
+        by_rows(jnp.maximum(counts[pa(p)], counts[pa(p + 1)]), step)
+        return 0
+
+    lax.fori_loop(0, count // 2, body, 0)
+
+
+def column_sums(x):
+    return jnp.sum(x.T, axis=0, keepdims=True)
+
+
+def expand(cols, at, as_, bh, bm):
+    def one(c, _):
+        t = cols[c]
+        at[c] = t[:, 0:48].astype(bf16)
+        if as_ is not None:
+            as_[c] = t[:, 56:104].astype(bf16)
+        bh[c] = jnp.broadcast_to(t[:, 54:55], (PART, 128))
+        if bm is not None:
+            bm[c] = jnp.broadcast_to(t[:, 55:56], (PART, 128))
+        return 0
+
+    lax.fori_loop(0, CELLS, one, 0, unroll=2)
+
+
+def density_prepare(o, rows, bf, hj, mj):
     full, norm, cross = basis(rows)
     bf[o] = stack16(right_parts(right_distance(full, norm)))
-    cj[o] = mass_rows(rows[7:8])
     hj[o] = rows[6:7]
+    mj[o] = rows[7:8]
     return full, norm, cross
 
 
 def own_density_kernel(
-    state, counts, pair_first, pair_offset, total, at, as_, bh, cj,
-    acc1, acc2, bf, hj, dist0, dist1, ws0, ws1, pa, po, ps,
+    pos, vel, mass, smooth, counts, pair_first, pair_offset, near, state, cols,
+    acc1, acc2, at, bh, bm, bf, hj, mj, dist0, dist1, pa, po, ps,
 ):
+    lane = lax.broadcasted_iota(i32, (1, PART), 1)
+
     def mine(c, _):
-        rows = state[c]
-        full, norm, cross = density_prepare(c, rows, bf, cj, hj)
-        t = columns(
+        live = jnp.where(lane < counts[c], mass[pl.ds(c, 1), :], 0.0)
+        rows = jnp.concatenate([pos[c], vel[c], smooth[pl.ds(c, 1), :], live], axis=0)
+        state[c] = rows
+        full, norm, cross = density_prepare(c, rows, bf, hj, mj)
+        cols[c] = columns(
             left_parts(left_distance(full, norm))
-            + [jnp.broadcast_to(rows[6:7], (8, PART))]
+            + [rows]
             + left_parts(left_approach(full, cross))
         )
-        at[c] = t[:, 0:48].astype(bf16)
-        as_[c] = t[:, 56:104].astype(bf16)
-        bh[c] = jnp.broadcast_to(t[:, 48:49], (PART, 128))
         return 0
 
     lax.fori_loop(0, CELLS, mine, 0, unroll=2)
+    expand(cols, at, None, bh, bm)
     own_lists(pair_first, pair_offset, pa, po, ps, CELLS)
     acc1[...] = jnp.zeros_like(acc1)
     acc2[...] = jnp.zeros_like(acc2)
-    refs = (bf, cj, cj, hj, at, bh, (dist0, dist1), (ws0, ws1))
+    refs = (bf, hj, mj, at, bh, bm, (dist0, dist1))
     density_pairs(
         CELLS + PAIRS, counts, lambda p: pa[p], lambda p: po[p], lambda p: ps[p], refs,
         lambda p: None, acc1, acc2,
     )
-    total[...] = acc1[...] + acc2[0:CELLS]
+
+    def total(c, _):
+        near[c] = column_sums(acc1[c]) + acc2[c]
+        return 0
+
+    lax.fori_loop(0, CELLS, total, 0, unroll=2)
 
 
 def far_density_kernel(
-    state, far, counts, slot, proxy_cell, at, bh, own_m,
+    far, counts, slot, proxy_cell, cols,
     acc1, ret, blocks, offset, block_own, live, size,
-    acc2, bf, cj, hj, dist0, dist1, ws0, ws1, filled,
+    acc2, at, bh, bm, bf, hj, mj, dist0, dist1, filled,
 ):
     total = pack_plan(far, slot, proxy_cell, offset, block_own, live, filled)
     size[0] = total
+    expand(cols, at, None, bh, bm)
     blocks[...] = jnp.zeros_like(blocks)
 
     def fill(e, _):
@@ -377,36 +409,43 @@
     lax.fori_loop(0, SEND, fill, 0, unroll=8)
     acc2[...] = jnp.zeros_like(acc2)
     acc1[...] = jnp.zeros_like(acc1)
-    refs = (bf, own_m, cj, hj, at, bh, (dist0, dist1), (ws0, ws1))
+    refs = (bf, hj, mj, at, bh, bm, (dist0, dist1))
     same = lambda p: p
     density_pairs(
         total, counts, lambda p: block_own[p], same, same, refs,
-        lambda p: density_prepare(p, blocks[p], bf, cj, hj), acc1, acc2,
+        lambda p: density_prepare(p, blocks[p], bf, hj, mj), acc1, acc2,
     )
 
     def back(e, _):
-        ret[slot[e]] = jnp.sum(unpack(acc2, offset[e])[0:3], axis=0, keepdims=True)
+        ret[slot[e]] = unpack(acc2, offset[e])
         return 0
 
     lax.fori_loop(0, SEND, back, 0, unroll=8)
 
 
+def add_by_goal(back, goals, sums):
+    for part in sums:
+        part[...] = jnp.zeros_like(part)
+
+    def one(t, _):
+        for k, part in enumerate(sums):
+            s = t * len(sums) + k
+            goal = goals[s]
+            part[jnp.where(goal < 0, CELLS, goal)] += back[s]
+        return 0
+
+    lax.fori_loop(0, back.shape[0] // len(sums), one, 0, unroll=2)
+
+
 def combine_density_kernel(
-    back, goals, near, far, energy, counts, density, fluid, answer, sums
+    after, back, goals, near, far, energy, counts, density, fluid, answer, *sums
 ):
-    sums[...] = jnp.zeros_like(sums)
-
-    def one(s, _):
-        goal = goals[s]
-        sums[jnp.where(goal < 0, CELLS, goal)] += back[s]
-        return 0
-
-    lax.fori_loop(0, back.shape[0], one, 0, unroll=2)
+    del after
+    add_by_goal(back, goals, sums)
     lane = lax.broadcasted_iota(i32, (1, PART), 1)
 
     def cell(c, _):
-        both = near[c] + far[c]
-        raw = W_SCALE * (jnp.sum(both[0:3], axis=0, keepdims=True) + sums[c])
+        raw = W_SCALE * (near[c] + far[c] + sum(part[c] for part in sums))
         here = lane < counts[c]
         density[pl.ds(c, 1), :] = jnp.where(here, raw, 0.0)
         fluid[c] = jnp.concatenate(
@@ -414,13 +453,13 @@
         )
         return 0
 
-    lax.fori_loop(0, CELLS, cell, 0)
+    lax.fori_loop(0, CELLS, cell, 0, unroll=4)
 
     def send(s, _):
         answer[s] = fluid[jnp.maximum(goals[s], 0)]
         return 0
 
-    lax.fori_loop(0, answer.shape[0], send, 0, unroll=4)
+    lax.fori_loop(0, answer.shape[0], send, 0, unroll=8)
 
 
 def slope_weights(r2, s, total_h):
@@ -447,10 +486,6 @@
     return pressure, sound, 4.0 * rho
 
 
-def two_wide(col, row):
-    return jnp.concatenate([col, col], axis=1) + row
-
-
 def put_halves(ws, c, w):
     hi, lo = halves(w)
     ws[c : c + CHUNK, :] = hi
@@ -476,7 +511,7 @@
     return first[:, 0:PART] + first[:, PART:], second
 
 
-def full_force(first, count, counts, pa, po, ps, refs, prepare, acc1, acc2):
+def full_force(first, count, counts, pa, po, refs, prepare, store):
     bd, bs, own_cf, other_cf, at, as_, bh, row, col, dist, appr, ws = refs
 
     def load(p, side):
@@ -500,9 +535,6 @@
     def combine(p, side):
         return force_combine(own_cf[pa(p)], other_cf[po(p)], ws[side])
 
-    def store(p, sums, valid):
-        keep_sums(acc1, acc2, pa(p), ps(p), sums, valid)
-
     pipeline(first, count, lambda p: counts[pa(p)], prepare, load, combine, store, work)
 
 
@@ -528,10 +560,20 @@
 
 
 def slope_kernel(
-    state_after, blocks, counts, block_own, size, at, as_, bh, out,
-    bd, bs, hj, dist0, dist1, appr0, appr1, buf, sems, *, first,
+    fluid, acc1, blocks, counts, block_own, size, cols, out, far_sums,
+    at, as_, bh, bd, bs, hj, dist0, dist1, appr0, appr1, buf, sems, *, first,
 ):
-    del state_after
+    del fluid
+    expand(cols, at, as_, bh, None)
+    if first == 0:
+
+        def total(c, _):
+            far_sums[c] = column_sums(acc1[c])
+            return 0
+
+        lax.fori_loop(0, CELLS, total, 0, unroll=2)
+    else:
+        far_sums[...] = jnp.zeros_like(far_sums)
     dist, appr = (dist0, dist1), (appr0, appr1)
     count = jnp.clip(size[0] - first, 0, out.shape[0])
     last = first + count - 1
@@ -608,10 +650,11 @@
 
 
 def own_force_kernel(
-    after, state, fluid, counts, pair_first, pair_offset, at, as_, bh, total,
-    acc1, acc2, bd, bs, cf, row, col, dist0, dist1, appr0, appr1, ws0, ws1, pa, po, ps,
+    after, state, fluid, counts, pair_first, pair_offset, cols, total,
+    acc1, acc2, at, as_, bh, bd, bs, cf, row, col, dist0, dist1, appr0, appr1, ws0, ws1, pa, po, ps,
 ):
     del after
+    expand(cols, at, as_, bh, None)
 
     def mine(c, _):
         rows = state[c]
@@ -627,16 +670,16 @@
     ws1[...] = jnp.zeros_like(ws1)
     refs = (bd, bs, cf, cf, at, as_, bh, row, col, (dist0, dist1), (appr0, appr1), (ws0, ws1))
     full_force(
-        0, CELLS + PAIRS, counts, lambda p: pa[p], lambda p: po[p], lambda p: ps[p], refs,
-        lambda p: None, acc1, acc2,
+        0, CELLS + PAIRS, counts, lambda p: pa[p], lambda p: po[p], refs, lambda p: None,
+        lambda p, sums, valid: keep_sums(acc1, acc2, pa[p], ps[p], sums, valid),
     )
     total[...] = acc1[...] + acc2[0:CELLS]
 
 
 def far_force_kernel(
-    state, fluid, blocks, far_fluid, counts, slot, offset, block_own, live, size, at, as_, bh,
+    state, fluid, blocks, far_fluid, counts, slot, offset, block_own, live, size, cols_far,
     ready0, ready1, acc1, ret,
-    acc2, fluids, bd, bs, own_cf, own_row, cf, row, col,
+    acc2, cols, at, as_, bh, fluids, bd, bs, own_cf, own_row, cf, row, col,
     dist0, dist1, appr0, appr1, ws0, ws1, buf, sems,
 ):
     total = size[0]
@@ -695,7 +738,11 @@
         return force_combine(own_cf[block_own[p]], cf[p], ws[side])
 
     def store(p, sums, valid):
-        keep_sums(acc1, acc2, block_own[p], p, sums, valid)
+        first, second = sums
+        if valid is not True:
+            first = first * jnp.where(valid, 1.0, 0.0)
+        acc1[block_own[p]] += first
+        acc2[p] = force_sums(blocks[p], second)
 
     def body(t, _):
         p = 2 * t
@@ -728,6 +775,9 @@
 
     @pl.when(total > 2 * steps)
     def _():
+        pltpu.sync_copy(cols_far, cols)
+        expand(cols, at, as_, bh, None)
+
         def rest(p):
             rows = blocks[p]
             fluid_prepare(p, rows, geometry_prepare(p, rows, bd, bs), fluids[p], cf, row)
@@ -737,40 +787,28 @@
         )
         same = lambda p: p
         full_force(
-            2 * steps, total - 2 * steps, counts, lambda p: block_own[p], same, same, refs,
-            rest, acc1, acc2,
+            2 * steps, total - 2 * steps, counts, lambda p: block_own[p], same, refs, rest, store,
         )
 
-    def turn(t, _):
-        acc2[t, 0:4] = force_sums(blocks[t], acc2[t])
-        return 0
-
-    lax.fori_loop(0, total // 2, lambda t, _: turn(2 * t, 0) + turn(2 * t + 1, 0), 0)
-
     def back(e, _):
-        ret[slot[e]] = unpack(acc2, offset[e])[0:4]
+        ret[slot[e]] = unpack(acc2, offset[e])
         return 0
 
     lax.fori_loop(0, SEND, back, 0, unroll=8)
 
 
 def finish_kernel(
-    back, goals, near, far, state, energy, counts, mig_cell, mig_dest, accel, leave, sums, moved, used
+    back, goals, near, far, state, energy, counts, mig_cell, mig_dest, accel, leave, moved, used, *sums
 ):
-    sums[...] = jnp.zeros_like(sums)
-
-    def one(s, _):
-        goal = goals[s]
-        sums[jnp.where(goal < 0, CELLS, goal)] += back[s]
-        return 0
-
-    lax.fori_loop(0, back.shape[0], one, 0, unroll=2)
+    add_by_goal(back, goals, sums)
     lane = lax.broadcasted_iota(i32, (1, PART), 1)
 
     def cell(c, _):
         rows = state[c]
         here = lane < counts[c]
-        total = jnp.where(here, force_sums(rows, near[c] + far[c]) + sums[c], 0.0)
+        total = jnp.where(
+            here, force_sums(rows, near[c] + far[c]) + sum(part[c] for part in sums), 0.0
+        )
         accel[c] = total
         new_vel = rows[3:6] + STEP * total[0:3]
         new_pos = rows[0:3] + STEP * new_vel
@@ -788,16 +826,25 @@
         used[d] = 0
         return 0
 
-    lax.fori_loop(0, leave.shape[0] // CAPM, clear, 0)
+    lax.fori_loop(0, leave.shape[0], clear, 0)
 
     def entry(e, _):
         d = mig_dest[e]
         k = used[d]
         used[d] = k + 1
-        leave[d * CAPM + k] = moved[mig_cell[e]]
+        full = moved[mig_cell[e]]
+        for r in range(9):
+            leave[d, r, pl.ds(k, 1), :] = full[r : r + 1]
         return 0
 
     lax.fori_loop(0, mig_cell.shape[0], entry, 0)
+
+
+def inbox_kernel(came, out):
+    for d in range(came.shape[0]):
+        full = came[d]
+        for k in range(CAPM):
+            out[d * CAPM + k] = full[:, k, :]
 
 
 def vmem(*dims, dtype=f32):
@@ -812,37 +859,38 @@
 SQUARE = [vmem(PART, PART)] * 2
 
 
-def own_density(state, counts, pair_first, pair_offset):
+def own_density(position, velocity, mass, smoothing, counts, pair_first, pair_offset):
     return kernel_call(
         own_density_kernel,
         (
+            shape(CELLS, 1, PART),
             shape(CELLS, 8, PART),
-            shape(CELLS, PART, 48, dtype=bf16),
-            shape(CELLS, PART, 48, dtype=bf16),
             shape(CELLS, PART, 128),
-            shape(CELLS, 16, PART, dtype=bf16),
         ),
-        [VMEM] + [SMEM] * 3,
-        (VMEM,) * 5,
+        [VMEM] * 4 + [SMEM] * 3,
+        (VMEM,) * 3,
         [
-            vmem(CELLS, 8, PART),
-            vmem(CELLS + 1, 8, PART),
+            vmem(CELLS, PART, 128),
+            vmem(CELLS + 1, 1, PART),
+            vmem(CELLS, PART, 48, dtype=bf16),
+            vmem(CELLS, PART, 128),
+            vmem(CELLS, PART, 128),
             vmem(CELLS, 48, PART, dtype=bf16),
+            vmem(CELLS, 1, PART),
             vmem(CELLS, 1, PART),
         ]
         + SQUARE
-        + WS
         + [smem(CELLS + PAIRS)] * 3,
         flops=32 * PART * PART * 300,
         moved=2**20,
-    )(state, counts, pair_first, pair_offset)
-
-
-def far_density(state, far, counts, slot, proxy_cell, at, bh, own_m):
+    )(position, velocity, mass, smoothing, counts, pair_first, pair_offset)
+
+
+def far_density(far, counts, slot, proxy_cell, cols):
     return kernel_call(
         far_density_kernel,
         (
-            shape(CELLS, 8, PART),
+            shape(CELLS, PART, 128),
             shape(far.shape[0], 1, PART),
             shape(BLOCKS + 1, 8, PART),
             shape(SEND, dtype=i32),
@@ -850,32 +898,37 @@
             shape(SEND, dtype=i32),
             shape(1, dtype=i32),
         ),
-        [VMEM] * 2 + [SMEM] * 3 + [VMEM] * 3,
+        [VMEM] + [SMEM] * 3 + [VMEM],
         (VMEM,) * 3 + (SMEM,) * 4,
         [
-            vmem(BLOCKS + 1, 8, PART),
+            vmem(BLOCKS + 1, 1, PART),
+            vmem(CELLS, PART, 48, dtype=bf16),
+            vmem(CELLS, PART, 128),
+            vmem(CELLS, PART, 128),
             vmem(BLOCKS, 48, PART, dtype=bf16),
-            vmem(BLOCKS, 16, PART, dtype=bf16),
+            vmem(BLOCKS, 1, PART),
             vmem(BLOCKS, 1, PART),
         ]
         + SQUARE
-        + WS
         + [smem(CELLS)],
         flops=128 * PART * PART * 300,
         moved=2**20,
-    )(state, far, counts, slot, proxy_cell, at, bh, own_m)
-
-
-def slopes(after, first, count, blocks, counts, block_own, size, at, as_, bh):
+    )(far, counts, slot, proxy_cell, cols)
+
+
+def slopes(fluid, acc1, first, count, blocks, counts, block_own, size, cols):
     def body(*refs):
         slope_kernel(*refs, first=first)
 
     return kernel_call(
         body,
-        shape(count, 2, PART, PART),
-        [ANY, VMEM] + [SMEM] * 3 + [VMEM] * 3,
-        ANY,
+        (shape(count, 2, PART, PART), shape(CELLS, 1, PART)),
+        [ANY, VMEM if first == 0 else ANY, VMEM] + [SMEM] * 3 + [VMEM],
+        (ANY, VMEM),
         [
+            vmem(CELLS, PART, 48, dtype=bf16),
+            vmem(CELLS, PART, 48, dtype=bf16),
+            vmem(CELLS, PART, 128),
             vmem(count, 48, PART, dtype=bf16),
             vmem(count, 48, PART, dtype=bf16),
             vmem(count, 1, PART),
@@ -884,20 +937,24 @@
         + [vmem(DEPTH, 2, 2, PART, PART), pltpu.SemaphoreType.DMA((DEPTH,))],
         flops=count * PART * PART * 400,
         moved=count * 2**19,
-    )(after, blocks, counts, block_own, size, at, as_, bh)
+    )(fluid, acc1, blocks, counts, block_own, size, cols)
 
 
 def far_force(
-    state, fluid, far_fluid, counts, slot, blocks, offset, block_own, live, size, at, as_, bh,
+    state, fluid, far_fluid, counts, slot, blocks, offset, block_own, live, size, cols,
     ready0, ready1,
 ):
     return kernel_call(
         far_force_kernel,
         (shape(CELLS, 8, PART), shape(far_fluid.shape[0], 4, PART)),
-        [VMEM] * 4 + [SMEM] * 6 + [VMEM] * 3 + [ANY] * 2,
+        [VMEM] * 4 + [SMEM] * 6 + [ANY] * 3,
         (VMEM, VMEM),
         [
-            vmem(BLOCKS + 1, 8, PART),
+            vmem(BLOCKS + 1, 4, PART),
+            vmem(CELLS, PART, 128),
+            vmem(CELLS, PART, 48, dtype=bf16),
+            vmem(CELLS, PART, 48, dtype=bf16),
+            vmem(CELLS, PART, 128),
             vmem(BLOCKS + 1, 2, PART),
             vmem(BLOCKS, 48, PART, dtype=bf16),
             vmem(BLOCKS, 48, PART, dtype=bf16),
@@ -914,19 +971,22 @@
         moved=2**20,
     )(
         state, fluid, blocks, far_fluid, counts, slot, offset, block_own, live, size,
-        at, as_, bh, ready0, ready1,
-    )
-
-
-def own_force(after, state, fluid, counts, pair_first, pair_offset, at, as_, bh):
+        cols, ready0, ready1,
+    )
+
+
+def own_force(after, state, fluid, counts, pair_first, pair_offset, cols):
     return kernel_call(
         own_force_kernel,
         shape(CELLS, 8, PART),
-        [ANY] + [VMEM] * 2 + [SMEM] * 3 + [VMEM] * 3,
+        [ANY] + [VMEM] * 2 + [SMEM] * 3 + [VMEM],
         VMEM,
         [
             vmem(CELLS, 8, PART),
             vmem(CELLS + 1, 8, PART),
+            vmem(CELLS, PART, 48, dtype=bf16),
+            vmem(CELLS, PART, 48, dtype=bf16),
+            vmem(CELLS, PART, 128),
             vmem(CELLS, 48, PART, dtype=bf16),
             vmem(CELLS, 48, PART, dtype=bf16),
             vmem(CELLS, 24, PART, dtype=bf16),
@@ -938,7 +998,7 @@
         + [smem(CELLS + PAIRS)] * 3,
         flops=32 * PART * PART * 600,
         moved=2**20,
-    )(after, state, fluid, counts, pair_first, pair_offset, at, as_, bh)
+    )(after, state, fluid, counts, pair_first, pair_offset, cols)
 
 
 def exchange(x, axes):
@@ -953,54 +1013,57 @@
     col_count = lax.axis_size("cols")
     slots = devices * CAP
     both = ("rows", "cols")
-    state, req, slot = kernel_call(
+    req, slot = kernel_call(
         request_kernel,
-        (shape(CELLS, 8, PART), shape(devices, 1, 128, dtype=i32), shape(SEND, dtype=i32)),
-        [VMEM] * 4 + [SMEM] * 3,
-        (VMEM, VMEM, SMEM),
-        [pltpu.SMEM((devices,), i32)],
+        (shape(devices, 1, 128, dtype=i32), shape(SEND, dtype=i32)),
+        [SMEM] * 2,
+        (VMEM, SMEM),
+        [smem(devices)],
         moved=2**20,
-    )(position, velocity, mass, smoothing, counts, proxy_dest[:, 0], proxy_target)
+    )(proxy_dest[:, 0], proxy_target)
     goals = exchange(req, both)[:, 0, 0:CAP].reshape(slots)
-    near, at, as_, bh, own_m = own_density(state, counts, pair_first, pair_offset)
+    near, state, cols = own_density(
+        position, velocity, mass, smoothing, counts, pair_first, pair_offset
+    )
     answer = kernel_call(
         respond_kernel, shape(slots, 8, PART), [VMEM, SMEM], VMEM, moved=4 * 2**20
     )(state, goals)
     far = exchange(answer, both)
-    far_sums, ret, *plan = far_density(state, far, counts, slot, proxy_cell, at, bh, own_m)
+    acc1, ret, *plan = far_density(far, counts, slot, proxy_cell, cols)
     blocks, offset, block_own, live, size = plan
-    ready0 = slopes(far_sums, 0, EARLY, blocks, counts, block_own, size, at, as_, bh)
+    ready0, far_sums = slopes(near, acc1, 0, EARLY, blocks, counts, block_own, size, cols)
     back = exchange(ret, both)
     density, fluid, answer2 = kernel_call(
         combine_density_kernel,
         (shape(CELLS, PART), shape(CELLS, 2, PART), shape(slots, 2, PART)),
-        [VMEM, SMEM] + [VMEM] * 3 + [SMEM],
+        [ANY, VMEM, SMEM] + [VMEM] * 3 + [SMEM],
         (VMEM, VMEM, VMEM),
-        [pltpu.VMEM((CELLS + 1, 1, PART), f32)],
+        [vmem(CELLS + 1, 1, PART)] * 4,
         moved=2**20,
-    )(back, goals, near, far_sums, energy, counts)
+    )(ready0, back, goals, near, far_sums, energy, counts)
     far_fluid = exchange(answer2, both)
-    ready1 = slopes(fluid, EARLY, LATE, blocks, counts, block_own, size, at, as_, bh)
+    ready1, _ = slopes(fluid, acc1, EARLY, LATE, blocks, counts, block_own, size, cols)
     far_force_sums, ret4 = far_force(
-        state, fluid, far_fluid, counts, slot, *plan, at, as_, bh, ready0, ready1
+        state, fluid, far_fluid, counts, slot, *plan, cols, ready0, ready1
     )
     near_force = own_force(
-        far_force_sums, state, fluid, counts, pair_first, pair_offset, at, as_, bh
+        far_force_sums, state, fluid, counts, pair_first, pair_offset, cols
     )
     back4 = exchange(ret4, both)
     accel, leave = kernel_call(
         finish_kernel,
-        (shape(CELLS, 4, PART), shape(col_count * CAPM, 9, PART)),
+        (shape(CELLS, 4, PART), shape(col_count, 9, CAPM, PART)),
         [VMEM, SMEM] + [VMEM] * 4 + [SMEM] * 3,
         (VMEM, VMEM),
-        [
-            pltpu.VMEM((CELLS + 1, 4, PART), f32),
-            pltpu.VMEM((CELLS, 9, PART), f32),
-            pltpu.SMEM((col_count,), i32),
-        ],
+        [vmem(CELLS, 9, PART), smem(col_count)] + [vmem(CELLS + 1, 4, PART)] * 4,
         moved=2**20,
-    )(back4, goals, near_force, far_force_sums, state, energy, counts, mig_cell, mig_dest[:, 0])
-    arrived = exchange(leave, "cols")
+    )(
+        back4, goals, near_force, far_force_sums, state, energy, counts, mig_cell,
+        mig_dest[:, 0],
+    )
+    arrived = kernel_call(
+        inbox_kernel, shape(col_count * CAPM, 9, PART), [VMEM], VMEM, moved=2**20
+    )(exchange(leave, "cols"))
     return (density, accel, arrived)
 
 

time: 254 us -> 260 us (1.024)
  starting transfers between devices: 20.5 us -> 48.2 us
  waiting for transfers between devices: 16.1 us -> 0.01 us
  Pallas kernels: 152 us -> 145 us
    all_to_all x3 -> x4, starting transfers between devices: 20.5 us -> 48.2 us  [exchange(): return lax.all_to_all(x, axes, split_axis=0, concat_axis=0, tiled=True)]
    all_to_all x3 -> x4, waiting for transfers between devices: 16.1 us -> 0.01 us  [exchange(): return lax.all_to_all(x, axes, split_axis=0, concat_axis=0, tiled=True)]
    pallas_call x1, Pallas kernels: 37.3 us -> 32.1 us  [far_force(): kernel_call(far_force_kernel, (shape(CELLS, 8, PART), shape(far_fluid.sha...]
    all_to_all x3 -> x2, blocking collectives: 55.5 us -> 56.8 us  [exchange(): return lax.all_to_all(x, axes, split_axis=0, concat_axis=0, tiled=True)]
    pallas_call x6 -> x7, Pallas kernels: 87.9 us -> 87.9 us  [the longest x2 35.3 us: slopes(): kernel_call(body, (shape(count, 2, PART, PART), shape(CELLS, 1, PART)), [...]
  transfers between devices with their start and end apart: 3 -> 4, of which waited for: 1 -> 0; matrix products, arithmetic and copies ran while one was open for 0% -> 1% of each run, Pallas kernels for 26% -> 26%
where the time goes in v4:
time: 260 us; the launch traced here: 259 us
  Pallas kernels  145 us (56%)
  blocking collectives  56.8 us (22%)
  starting transfers between devices  48.2 us (19%)
  local copies, waits for them, and re-layouts  8.17 us (3%)
    all_to_all x2, blocking collectives, exchange(): return lax.all_to_all(x, axes, split_axis=0, concat_axis=0, tiled=True)  56.8 us
    all_to_all x4, starting transfers between devices, exchange(): return lax.all_to_all(x, axes, split_axis=0, concat_axis=0, tiled=True)  48.2 us
    pallas_call x2, Pallas kernels, slopes(): kernel_call(body, (shape(count, 2, PART, PART), shape(CELLS, 1, PART)), [...  35.3 us
    pallas_call x1, Pallas kernels, far_force(): kernel_call(far_force_kernel, (shape(CELLS, 8, PART), shape(far_fluid.sha...  32.1 us
    pallas_call x1, Pallas kernels, far_density(): kernel_call(far_density_kernel, (shape(CELLS, PART, 128), shape(far.shape...  31.3 us
    pallas_call x1, Pallas kernels, own_force(): kernel_call(own_force_kernel, shape(CELLS, 8, PART), [ANY] + [VMEM] * 2 +...  19.2 us
    pallas_call x1, Pallas kernels, own_density(): kernel_call(own_density_kernel, (shape(CELLS, 1, PART), shape(CELLS, 8, P...  13.5 us
    unnamed x9, local copies, waits for them, and re-layouts  7.33 us
  transfers between devices with their start and end apart: 4, of which 0 were waited for; matrix products, arithmetic and copies ran while one was open for 1% of the time, Pallas kernels for 26%

profile of v4, /device:TPU:0, one launch (start us, length us, event | category | flops | bytes accessed | tf_op | source)
XLA Modules:
  0.0 259.2 jit_solution(457104329671064839)
XLA Ops:
  0.6 2.2 shard_map.149
  2.8 11.1 %all-to-all-start = ((s32[128,1,128]{2,1,0:T(1,128)}), s32[128,1,128]{2,1,0:T(1,128)S(1)}, u32[]{:S(2)}, u32[]{:S(2)}) async-start(s32[128,1,128]{2,1,0:T(1,128)} %get-tuple-element.27), calls=%async_computation | async-start | bytes 131072 | tf_op jit(solution)/shard_map/all_to_all | solution.py:1005
  14.0 1.5 copy.19.pos
  15.5 1.5 copy.20.vel
  16.9 13.5 %shard_map.148 = (f32[16,1,256]{2,1,0:T(1,128)}, f32[16,8,256]{2,1,0:T(8,128)}, f32[16,256,128]{2,1,0:T(8,128)}) custom-call(f32[16,3,256]{2,1,0:T(4,128)} %copy.19.pos, f32[16,3,256]{2,1,0:T(4,128)} %copy.20.vel, f32[16,256]{1,0:T(8,128)} %mass.1, f32[16,256]{1,0:T(8,128)} %smooth.1, s32[16]{0:T(128)} %counts.11, s32[16]{0:T(128)} %pair_first.3, s32[16]{0:T(128)} %pair_offset.3), custom_call_target="tpu_custom_call" | custom-call | flops 629145600 | bytes 1048576 | tf_op jit(solution)/shard_map/pallas_call | solution.py:863
  30.4 0.0 all-to-all-done
  30.4 0.2 slice_reduce_fusion
  30.6 0.7 reshape_squeeze.3.goals
  31.2 3.0 %shard_map.150 = f32[256,8,256]{2,1,0:T(8,128)} custom-call(f32[16,8,256]{2,1,0:T(8,128)} %get-tuple-element.26.state, s32[256]{0:T(256)} %reshape_squeeze.3.goals), custom_call_target="tpu_custom_call" | custom-call | bytes 4194304 | tf_op jit(solution)/shard_map/pallas_call | solution.py:1028
  34.2 40.3 %all_to_all.30.far = f32[256,8,256]{2,1,0:T(8,128)} all-to-all(f32[256,8,256]{2,1,0:T(8,128)} %shard_map.150), channel_id=1, replica_groups=mesh['rows'=8,'cols'=16] {'rows','cols'}, dimensions={0} | all-to-all | bytes 4194304 | tf_op jit(solution)/shard_map/all_to_all | solution.py:1005
  74.5 31.3 %shard_map.151 = (f32[16,256,128]{2,1,0:T(8,128)}, f32[256,1,256]{2,1,0:T(1,128)}, f32[145,8,256]{2,1,0:T(8,128)}, s32[128]{0:T(128)}, s32[144]{0:T(256)}, /*index=5*/s32[128]{0:T(128)}, s32[1]{0:T(128)}) custom-call(f32[256,8,256]{2,1,0:T(8,128)} %all_to_all.30.far, s32[16]{0:T(128)} %counts.11, s32[128]{0:T(128)} %get-tuple-element.28.slot, ...), custom_call_target="tpu_custom_call" | custom-call | flops 2516582400 | bytes 1048576 | tf_op jit(solution)/shard_map/pallas_call | solution.py:890
  105.9 8.6 %all-to-all-start.2 = ((f32[256,1,256]{2,1,0:T(1,128)}), f32[256,1,256]{2,1,0:T(1,128)S(1)}, u32[]{:S(2)}, u32[]{:S(2)}) async-start(f32[256,1,256]{2,1,0:T(1,128)} %get-tuple-element.35), calls=%async_computation.2 | async-start | bytes 524288 | tf_op jit(solution)/shard_map/all_to_all | solution.py:1005
  114.5 17.2 %shard_map.152 = (f32[42,2,256,256]{3,2,1,0:T(8,128)}, f32[16,1,256]{2,1,0:T(1,128)}) custom-call(f32[16,1,256]{2,1,0:T(1,128)} %get-tuple-element.25.refs_0_.near, f32[16,256,128]{2,1,0:T(8,128)} %get-tuple-element.30.refs_1_, f32[145,8,256]{2,1,0:T(8,128)} %get-tuple-element.31.refs_2_.blocks, s32[16]{0:T(128)} %counts.11, ...), custom_call_target="tpu_custom_call" | custom-call | flops 1101004800 | bytes 22020096 | tf_op jit(solution)/shard_map/pallas_call | solution.py:923
  131.7 0.0 all-to-all-done.2.back
  131.7 0.0 copy-start.2
  131.7 0.7 copy-done.2
  132.4 3.1 %shard_map.153 = (f32[16,256]{1,0:T(8,128)}, f32[16,2,256]{2,1,0:T(2,128)}, f32[256,2,256]{2,1,0:T(2,128)}) custom-call(f32[42,2,256,256]{3,2,1,0:T(8,128)} %get-tuple-element.34.after.ready0, f32[256,1,256]{2,1,0:T(1,128)} %copy-done.2, s32[256]{0:T(256)} %reshape_squeeze.3.goals, f32[16,1,256]{2,1,0:T(1,128)} %get-tuple-element.25.refs_0_.near, ...), custom_call_target="tpu_custom_call" | custom-call | bytes 1048576 | tf_op jit(solution)/shard_map/pallas_call | solution.py:1036
  135.4 11.3 %all-to-all-start.3 = ((f32[256,2,256]{2,1,0:T(2,128)}), f32[256,2,256]{2,1,0:T(2,128)S(1)}, u32[]{:S(2)}, u32[]{:S(2)}) async-start(f32[256,2,256]{2,1,0:T(2,128)} %get-tuple-element.39), calls=%async_computation.3 | async-start | bytes 1048576 | tf_op jit(solution)/shard_map/all_to_all | solution.py:1005
  146.7 18.2 %shard_map.154 = (f32[50,2,256,256]{3,2,1,0:T(8,128)}, f32[16,1,256]{2,1,0:T(1,128)}) custom-call(f32[16,2,256]{2,1,0:T(2,128)} %get-tuple-element.38.refs_0_.fluid, f32[16,256,128]{2,1,0:T(8,128)} %get-tuple-element.30.refs_1_, f32[145,8,256]{2,1,0:T(8,128)} %get-tuple-element.31.refs_2_.blocks, s32[16]{0:T(128)} %counts.11, ...), custom_call_target="tpu_custom_call" | custom-call | flops 1310720000 | bytes 26214400 | tf_op jit(solution)/shard_map/pallas_call | solution.py:923
  164.9 0.0 all-to-all-done.3.far_fluid
  164.9 0.0 copy-start.1
  164.9 0.8 copy-done.1
  165.7 32.1 %shard_map.155 = (f32[16,8,256]{2,1,0:T(8,128)}, f32[256,4,256]{2,1,0:T(4,128)}) custom-call(f32[16,8,256]{2,1,0:T(8,128)} %get-tuple-element.26.state, f32[16,2,256]{2,1,0:T(2,128)} %get-tuple-element.38.refs_0_.fluid, f32[145,8,256]{2,1,0:T(8,128)} %get-tuple-element.31.refs_2_.blocks, f32[256,2,256]{2,1,0:T(2,128)} %copy-done.1, s32[16]{0:T(128)} %counts.11, ...), custom_call_target="tpu_custom_call" | custom-call | flops 2516582400 | bytes 1048576 | tf_op jit(solution)/shard_map/pallas_call | solution.py:947
  197.8 17.1 %all-to-all-start.4 = ((f32[256,4,256]{2,1,0:T(4,128)}), f32[256,4,256]{2,1,0:T(4,128)S(1)}, u32[]{:S(2)}, u32[]{:S(2)}) async-start(f32[256,4,256]{2,1,0:T(4,128)} %get-tuple-element.43), calls=%async_computation.4 | async-start | bytes 2097152 | tf_op jit(solution)/shard_map/all_to_all | solution.py:1005
  214.9 19.2 %shard_map.156.near = f32[16,8,256]{2,1,0:T(8,128)} custom-call(f32[16,8,256]{2,1,0:T(8,128)} %get-tuple-element.44.after.far, f32[16,8,256]{2,1,0:T(8,128)} %get-tuple-element.26.state, f32[16,2,256]{2,1,0:T(2,128)} %get-tuple-element.38.refs_0_.fluid, s32[16]{0:T(128)} %counts.11, s32[16]{0:T(128)} %pair_first.3, s32[16]{0:T(128)} %pair_offset.3, ...), custom_call_target="tpu_custom_call" | custom-call | flops 1258291200 | bytes 1048576 | tf_op jit(solution)/shard_map/pallas_call | solution.py:979
  234.2 0.0 all-to-all-done.4.back
  234.2 0.0 copy-start
  234.2 1.0 copy-done
  235.2 3.7 %shard_map.157 = (f32[16,4,256]{2,1,0:T(4,128)}, f32[16,9,2,256]{3,2,1,0:T(2,128)}) custom-call(f32[256,4,256]{2,1,0:T(4,128)} %copy-done, s32[256]{0:T(256)} %reshape_squeeze.3.goals, f32[16,8,256]{2,1,0:T(8,128)} %shard_map.156.near, f32[16,8,256]{2,1,0:T(8,128)} %get-tuple-element.44.after.far, f32[16,8,256]{2,1,0:T(8,128)} %get-tuple-element.26.state, ...), custom_call_target="tpu_custom_call" | custom-call | bytes 1048576 | tf_op jit(solution)/shard_map/pallas_call | solution.py:1053
  238.8 16.6 %all_to_all.31.came = f32[16,9,2,256]{3,2,1,0:T(2,128)} all-to-all(f32[16,9,2,256]{3,2,1,0:T(2,128)} %get-tuple-element.46), channel_id=1, replica_groups=mesh['rows'=8,'cols'=16] {'cols'}, dimensions={0} | all-to-all | bytes 589824 | tf_op jit(solution)/shard_map/all_to_all | solution.py:1005
  255.4 1.9 shard_map.158
  257.3 1.9 copy.21
Async XLA Ops:
  2.8 27.5 %all-to-all-start = ((s32[128,1,128]{2,1,0:T(1,128)}), s32[128,1,128]{2,1,0:T(1,128)S(1)}, u32[]{:S(2)}, u32[]{:S(2)}) async-start(s32[128,1,128]{2,1,0:T(1,128)} %get-tuple-element.27), calls=%async_computation | async-start | bytes 131072 | tf_op jit(solution)/shard_map/all_to_all | solution.py:1005
  105.9 25.8 %all-to-all-start.2 = ((f32[256,1,256]{2,1,0:T(1,128)}), f32[256,1,256]{2,1,0:T(1,128)S(1)}, u32[]{:S(2)}, u32[]{:S(2)}) async-start(f32[256,1,256]{2,1,0:T(1,128)} %get-tuple-element.35), calls=%async_computation.2 | async-start | bytes 524288 | tf_op jit(solution)/shard_map/all_to_all | solution.py:1005
  131.7 0.7 copy-start.2
  135.4 29.5 %all-to-all-start.3 = ((f32[256,2,256]{2,1,0:T(2,128)}), f32[256,2,256]{2,1,0:T(2,128)S(1)}, u32[]{:S(2)}, u32[]{:S(2)}) async-start(f32[256,2,256]{2,1,0:T(2,128)} %get-tuple-element.39), calls=%async_computation.3 | async-start | bytes 1048576 | tf_op jit(solution)/shard_map/all_to_all | solution.py:1005
  164.9 0.8 copy-start.1
  197.8 36.4 %all-to-all-start.4 = ((f32[256,4,256]{2,1,0:T(4,128)}), f32[256,4,256]{2,1,0:T(4,128)S(1)}, u32[]{:S(2)}, u32[]{:S(2)}) async-start(f32[256,4,256]{2,1,0:T(4,128)} %get-tuple-element.43), calls=%async_computation.4 | async-start | bytes 2097152 | tf_op jit(solution)/shard_map/all_to_all | solution.py:1005
  234.2 1.0 copy-start

commit v5 on v4

--- a/solution.py
+++ b/solution.py
@@ -21,8 +21,9 @@
 CHUNK = 32
 ROWS = (128, 160, 192, 224, 256)
 BLOCKS = SEND + CELLS
-EARLY, LATE = 42, 50
+EARLY, LATE = 32, 60
 DEPTH = 4
+RING = 8
 
 f32, bf16, i32 = jnp.float32, jnp.bfloat16, jnp.int32
 VMEM = pl.BlockSpec(memory_space=pltpu.VMEM)
@@ -284,10 +285,10 @@
 
 
 def density_pairs(count, counts, pa, po, ps, refs, prepare, acc1, acc2):
-    bf, hj, mj, at, bh, bm, dist = refs
+    bf, hj, mj, cols, bh, bm, dist = refs
 
     def load(p, side):
-        dist[side][...] = nn(at[pa(p)], bf[po(p)])
+        dist[side][...] = nn(cols[pa(p)], bf[lax.rem(po(p), bf.shape[0])])
 
     def work(p, side, rows):
         a, o = pa(p), po(p)
@@ -334,52 +335,81 @@
     return jnp.sum(x.T, axis=0, keepdims=True)
 
 
-def expand(cols, at, as_, bh, bm):
+def spreader(lanes):
+    row = lax.broadcasted_iota(i32, (128, 128 * len(lanes)), 0)
+    block = lax.broadcasted_iota(i32, (128, 128 * len(lanes)), 1) // 128
+    hit = row < 0
+    for n, k in enumerate(lanes):
+        hit |= (block == n) & ((row == k) | (row == k + 8) | (row == k + 16))
+    return jnp.where(hit, 1.0, 0.0).astype(bf16)
+
+
+def expand(cols, bh, bm=None):
+    matrix = spreader((102,) if bm is None else (102, 103))
+
     def one(c, _):
-        t = cols[c]
-        at[c] = t[:, 0:48].astype(bf16)
-        if as_ is not None:
-            as_[c] = t[:, 56:104].astype(bf16)
-        bh[c] = jnp.broadcast_to(t[:, 54:55], (PART, 128))
+        wide = nn(cols[c], matrix)
+        bh[c] = wide[:, 0:128]
         if bm is not None:
-            bm[c] = jnp.broadcast_to(t[:, 55:56], (PART, 128))
-        return 0
-
-    lax.fori_loop(0, CELLS, one, 0, unroll=2)
+            bm[c] = wide[:, 128:256]
+        return 0
+
+    lax.fori_loop(0, CELLS, one, 0, unroll=4)
+
+
+def put_right(ref, o, start, parts):
+    ref[lax.rem(o, ref.shape[0]), start : start + 48, :] = stack16(right_parts(parts))
 
 
 def density_prepare(o, rows, bf, hj, mj):
     full, norm, cross = basis(rows)
-    bf[o] = stack16(right_parts(right_distance(full, norm)))
+    put_right(bf, o, 0, right_distance(full, norm))
     hj[o] = rows[6:7]
     mj[o] = rows[7:8]
     return full, norm, cross
 
 
-def own_density_kernel(
-    pos, vel, mass, smooth, counts, pair_first, pair_offset, near, state, cols,
-    acc1, acc2, at, bh, bm, bf, hj, mj, dist0, dist1, pa, po, ps,
-):
+def state_kernel(pos, vel, mass, smooth, counts, state, cols):
     lane = lax.broadcasted_iota(i32, (1, PART), 1)
 
     def mine(c, _):
-        live = jnp.where(lane < counts[c], mass[pl.ds(c, 1), :], 0.0)
-        rows = jnp.concatenate([pos[c], vel[c], smooth[pl.ds(c, 1), :], live], axis=0)
+        one = pl.ds(c, 1)
+        live = jnp.where(lane < counts[c], mass[one, :], 0.0)
+        rows = jnp.concatenate(
+            [pos[k, one, :] for k in range(3)]
+            + [vel[k, one, :] for k in range(3)]
+            + [smooth[one, :], live],
+            axis=0,
+        )
         state[c] = rows
-        full, norm, cross = density_prepare(c, rows, bf, hj, mj)
+        full, norm, cross = basis(rows)
         cols[c] = columns(
             left_parts(left_distance(full, norm))
-            + [rows]
             + left_parts(left_approach(full, cross))
-        )
+            + list(split3(rows))
+        ).astype(bf16)
+        return 0
+
+    lax.fori_loop(0, CELLS, mine, 0, unroll=4)
+
+
+def own_density_kernel(
+    after, state, cols, counts, pair_first, pair_offset, near,
+    acc1, acc2, bh, bm, bf, hj, mj, dist0, dist1, pa, po, ps,
+):
+    del after
+    expand(cols, bh, bm)
+    bf[...] = jnp.zeros_like(bf)
+
+    def mine(c, _):
+        density_prepare(c, state[c], bf, hj, mj)
         return 0
 
     lax.fori_loop(0, CELLS, mine, 0, unroll=2)
-    expand(cols, at, None, bh, bm)
     own_lists(pair_first, pair_offset, pa, po, ps, CELLS)
     acc1[...] = jnp.zeros_like(acc1)
     acc2[...] = jnp.zeros_like(acc2)
-    refs = (bf, hj, mj, at, bh, bm, (dist0, dist1))
+    refs = (bf, hj, mj, cols, bh, bm, (dist0, dist1))
     density_pairs(
         CELLS + PAIRS, counts, lambda p: pa[p], lambda p: po[p], lambda p: ps[p], refs,
         lambda p: None, acc1, acc2,
@@ -393,13 +423,15 @@
 
 
 def far_density_kernel(
-    far, counts, slot, proxy_cell, cols,
+    near, far, counts, slot, proxy_cell, cols,
     acc1, ret, blocks, offset, block_own, live, size,
-    acc2, at, bh, bm, bf, hj, mj, dist0, dist1, filled,
+    acc2, bh, bm, bf, hj, mj, dist0, dist1, filled,
 ):
+    del near
     total = pack_plan(far, slot, proxy_cell, offset, block_own, live, filled)
     size[0] = total
-    expand(cols, at, None, bh, bm)
+    expand(cols, bh, bm)
+    bf[...] = jnp.zeros_like(bf)
     blocks[...] = jnp.zeros_like(blocks)
 
     def fill(e, _):
@@ -409,7 +441,7 @@
     lax.fori_loop(0, SEND, fill, 0, unroll=8)
     acc2[...] = jnp.zeros_like(acc2)
     acc1[...] = jnp.zeros_like(acc1)
-    refs = (bf, hj, mj, at, bh, bm, (dist0, dist1))
+    refs = (bf, hj, mj, cols, bh, bm, (dist0, dist1))
     same = lambda p: p
     density_pairs(
         total, counts, lambda p: block_own[p], same, same, refs,
@@ -512,12 +544,12 @@
 
 
 def full_force(first, count, counts, pa, po, refs, prepare, store):
-    bd, bs, own_cf, other_cf, at, as_, bh, row, col, dist, appr, ws = refs
+    bd, bs, own_cf, other_cf, cols, bh, row, col, dist, appr, ws = refs
 
     def load(p, side):
-        a, o = pa(p), po(p)
-        dist[side][...] = nn(at[a], bd[o])
-        appr[side][...] = nn(as_[a], bs[o])
+        a, o = pa(p), lax.rem(po(p), bd.shape[0])
+        dist[side][...] = nn(cols[a], bd[o])
+        appr[side][...] = nn(cols[a], bs[o])
 
     def work(p, side, rows):
         a = pa(p)
@@ -540,8 +572,8 @@
 
 def geometry_prepare(o, rows, bd, bs):
     full, norm, cross = basis(rows)
-    bd[o] = stack16(right_parts(right_distance(full, norm)))
-    bs[o] = stack16(right_parts(full))
+    put_right(bd, o, 0, right_distance(full, norm))
+    put_right(bs, o, 48, full)
     return full
 
 
@@ -553,18 +585,20 @@
     )
 
 
-def own_fluid_columns(c, row, col):
-    t = columns([row[c]])
+def own_fluid_columns(c, row, col, matrix):
+    wide = nn(columns(list(split3(row[c]))).astype(bf16), matrix)
     for k in range(3):
-        col[c, k] = jnp.broadcast_to(t[:, k + 1 : k + 2], (PART, 128))
+        col[c, k] = wide[:, 128 * k : 128 * (k + 1)]
 
 
 def slope_kernel(
     fluid, acc1, blocks, counts, block_own, size, cols, out, far_sums,
-    at, as_, bh, bd, bs, hj, dist0, dist1, appr0, appr1, buf, sems, *, first,
+    bh, bd, bs, hj, dist0, dist1, appr0, appr1, buf, sems, *, first,
 ):
     del fluid
-    expand(cols, at, as_, bh, None)
+    expand(cols, bh)
+    bd[...] = jnp.zeros_like(bd)
+    bs[...] = jnp.zeros_like(bs)
     if first == 0:
 
         def total(c, _):
@@ -583,17 +617,29 @@
 
     def prepare(p):
         rows = blocks[p]
-        geometry_prepare(p - first, rows, bd, bs)
+        geometry_prepare(p, rows, bd, bs)
         hj[p - first] = rows[6:7]
 
     def load(p, side):
         a = block_own[p]
-        dist[side][...] = nn(at[a], bd[p - first])
-        appr[side][...] = nn(as_[a], bs[p - first])
-
-    def copy(t):
+        o = lax.rem(p, RING)
+        dist[side][...] = nn(cols[a], bd[o])
+        appr[side][...] = nn(cols[a], bs[o])
+
+    def copy(t, rows):
         k = lax.rem(t, DEPTH)
-        return pltpu.make_async_copy(buf.at[k], out.at[pl.ds(2 * t, 2)], sems.at[k])
+        return pltpu.make_async_copy(
+            buf.at[k, :, :, pl.ds(0, rows), :],
+            out.at[pl.ds(2 * t, 2), :, pl.ds(0, rows), :],
+            sems.at[k],
+        )
+
+    def need(t):
+        p = first + 2 * t
+        return jnp.maximum(counts[block_own[p]], counts[block_own[p + 1]])
+
+    def wait(t):
+        by_rows(need(t), lambda rows: copy(t, rows).wait())
 
     def work(p, side, rows, k):
         a = block_own[p]
@@ -616,7 +662,7 @@
     def body(t, _):
         p = first + 2 * t
         k = lax.rem(t, DEPTH)
-        pl.when(t >= DEPTH)(lambda: copy(t - DEPTH).wait())
+        pl.when(t >= DEPTH)(lambda: wait(t - DEPTH))
 
         def step(rows):
             load(p + 1, 1)
@@ -625,16 +671,16 @@
             load(clamp(p + 2), 0)
             prepare(clamp(p + 3))
             prepare(clamp(p + 4))
-
-        by_rows(jnp.maximum(counts[block_own[p]], counts[block_own[p + 1]]), step)
-        copy(t).start()
+            copy(t, rows).start()
+
+        by_rows(need(t), step)
         return 0
 
     steps = count // 2
     lax.fori_loop(0, steps, body, 0)
 
     def drain(t, _):
-        copy(t).wait()
+        wait(t)
         return 0
 
     lax.fori_loop(jnp.maximum(steps - DEPTH, 0), steps, drain, 0)
@@ -651,15 +697,18 @@
 
 def own_force_kernel(
     after, state, fluid, counts, pair_first, pair_offset, cols, total,
-    acc1, acc2, at, as_, bh, bd, bs, cf, row, col, dist0, dist1, appr0, appr1, ws0, ws1, pa, po, ps,
+    acc1, acc2, bh, bd, bs, cf, row, col, dist0, dist1, appr0, appr1, ws0, ws1, pa, po, ps,
 ):
     del after
-    expand(cols, at, as_, bh, None)
+    expand(cols, bh)
+    bd[...] = jnp.zeros_like(bd)
+    bs[...] = jnp.zeros_like(bs)
+    matrix = spreader((1, 2, 3))
 
     def mine(c, _):
         rows = state[c]
         fluid_prepare(c, rows, geometry_prepare(c, rows, bd, bs), fluid[c], cf, row)
-        own_fluid_columns(c, row, col)
+        own_fluid_columns(c, row, col, matrix)
         return 0
 
     lax.fori_loop(0, CELLS, mine, 0, unroll=2)
@@ -668,7 +717,7 @@
     acc2[...] = jnp.zeros_like(acc2)
     ws0[...] = jnp.zeros_like(ws0)
     ws1[...] = jnp.zeros_like(ws1)
-    refs = (bd, bs, cf, cf, at, as_, bh, row, col, (dist0, dist1), (appr0, appr1), (ws0, ws1))
+    refs = (bd, bs, cf, cf, cols, bh, row, col, (dist0, dist1), (appr0, appr1), (ws0, ws1))
     full_force(
         0, CELLS + PAIRS, counts, lambda p: pa[p], lambda p: po[p], refs, lambda p: None,
         lambda p, sums, valid: keep_sums(acc1, acc2, pa[p], ps[p], sums, valid),
@@ -679,37 +728,43 @@
 def far_force_kernel(
     state, fluid, blocks, far_fluid, counts, slot, offset, block_own, live, size, cols_far,
     ready0, ready1, acc1, ret,
-    acc2, cols, at, as_, bh, fluids, bd, bs, own_cf, own_row, cf, row, col,
+    acc2, cols, bh, fluids, bd, bs, own_cf, own_row, cf, row, col,
     dist0, dist1, appr0, appr1, ws0, ws1, buf, sems,
 ):
     total = size[0]
     half = ready0.shape[0] // 2
     steps = jnp.minimum(total, ready0.shape[0] + ready1.shape[0]) // 2
 
+    def need(t):
+        return jnp.maximum(counts[block_own[2 * t]], counts[block_own[2 * t + 1]])
+
+    def copy(ready, t, k, rows):
+        return pltpu.make_async_copy(
+            ready.at[pl.ds(2 * t, 2), :, pl.ds(0, rows), :],
+            buf.at[k, :, :, pl.ds(0, rows), :],
+            sems.at[k],
+        )
+
     def start(t):
         k = lax.rem(t, DEPTH)
 
         @pl.when(t < half)
         def _():
-            pltpu.make_async_copy(ready0.at[pl.ds(2 * t, 2)], buf.at[k], sems.at[k]).start()
+            by_rows(need(t), lambda rows: copy(ready0, t, k, rows).start())
 
         @pl.when(t >= half)
         def _():
-            pltpu.make_async_copy(
-                ready1.at[pl.ds(2 * (t - half), 2)], buf.at[k], sems.at[k]
-            ).start()
-
-    def wait(t):
-        k = lax.rem(t, DEPTH)
-        pltpu.make_async_copy(ready0.at[pl.ds(0, 2)], buf.at[k], sems.at[k]).wait()
+            by_rows(need(t), lambda rows: copy(ready1, t - half, k, rows).start())
 
     for t in range(DEPTH - 1):
         pl.when(t < steps)(lambda t=t: start(t))
+
+    matrix = spreader((1, 2, 3))
 
     def mine(c, _):
         rows = state[c]
         fluid_prepare(c, rows, basis(rows)[0], fluid[c], own_cf, own_row)
-        own_fluid_columns(c, own_row, col)
+        own_fluid_columns(c, own_row, col, matrix)
         return 0
 
     lax.fori_loop(0, CELLS, mine, 0, unroll=2)
@@ -748,7 +803,6 @@
         p = 2 * t
         k = lax.rem(t, DEPTH)
         pl.when(t + DEPTH - 1 < steps)(lambda: start(t + DEPTH - 1))
-        wait(t)
 
         def work(p, side, rows):
             def grads(c):
@@ -757,6 +811,7 @@
             fluid_work(ws[side], col, row[p], block_own[p], rows, grads)
 
         def step(rows):
+            copy(ready0, 0, k, rows).wait()
             before = jnp.maximum(p - 1, 0)
             sums = combine(before, 1)
             work(p, 0, rows)
@@ -767,7 +822,7 @@
             prepare(jnp.minimum(p + 2, last))
             prepare(jnp.minimum(p + 3, last))
 
-        by_rows(jnp.maximum(counts[block_own[p]], counts[block_own[p + 1]]), step)
+        by_rows(need(t), step)
         return 0
 
     lax.fori_loop(0, steps, body, 0)
@@ -776,14 +831,16 @@
     @pl.when(total > 2 * steps)
     def _():
         pltpu.sync_copy(cols_far, cols)
-        expand(cols, at, as_, bh, None)
+        expand(cols, bh)
+        bd[...] = jnp.zeros_like(bd)
+        bs[...] = jnp.zeros_like(bs)
 
         def rest(p):
             rows = blocks[p]
             fluid_prepare(p, rows, geometry_prepare(p, rows, bd, bs), fluids[p], cf, row)
 
         refs = (
-            bd, bs, own_cf, cf, at, as_, bh, row, col, (dist0, dist1), (appr0, appr1), ws,
+            bd, bs, own_cf, cf, cols, bh, row, col, (dist0, dist1), (appr0, appr1), ws,
         )
         same = lambda p: p
         full_force(
@@ -842,9 +899,8 @@
 
 def inbox_kernel(came, out):
     for d in range(came.shape[0]):
-        full = came[d]
-        for k in range(CAPM):
-            out[d * CAPM + k] = full[:, k, :]
+        for r in range(came.shape[1]):
+            out[r, d * CAPM : (d + 1) * CAPM, :] = came[d, r]
 
 
 def vmem(*dims, dtype=f32):
@@ -859,23 +915,29 @@
 SQUARE = [vmem(PART, PART)] * 2
 
 
-def own_density(position, velocity, mass, smoothing, counts, pair_first, pair_offset):
+def cell_state(position, velocity, mass, smoothing, counts):
+    return kernel_call(
+        state_kernel,
+        (shape(CELLS, 8, PART), shape(CELLS, PART, 128, dtype=bf16)),
+        [VMEM] * 4 + [SMEM],
+        (VMEM, VMEM),
+        flops=2**20,
+        moved=2**22,
+    )(position, velocity, mass, smoothing, counts)
+
+
+def own_density(after, state, cols, counts, pair_first, pair_offset):
     return kernel_call(
         own_density_kernel,
-        (
-            shape(CELLS, 1, PART),
-            shape(CELLS, 8, PART),
-            shape(CELLS, PART, 128),
-        ),
-        [VMEM] * 4 + [SMEM] * 3,
-        (VMEM,) * 3,
+        shape(CELLS, 1, PART),
+        [ANY] + [VMEM] * 2 + [SMEM] * 3,
+        VMEM,
         [
             vmem(CELLS, PART, 128),
             vmem(CELLS + 1, 1, PART),
-            vmem(CELLS, PART, 48, dtype=bf16),
             vmem(CELLS, PART, 128),
             vmem(CELLS, PART, 128),
-            vmem(CELLS, 48, PART, dtype=bf16),
+            vmem(CELLS, 128, PART, dtype=bf16),
             vmem(CELLS, 1, PART),
             vmem(CELLS, 1, PART),
         ]
@@ -883,10 +945,10 @@
         + [smem(CELLS + PAIRS)] * 3,
         flops=32 * PART * PART * 300,
         moved=2**20,
-    )(position, velocity, mass, smoothing, counts, pair_first, pair_offset)
-
-
-def far_density(far, counts, slot, proxy_cell, cols):
+    )(after, state, cols, counts, pair_first, pair_offset)
+
+
+def far_density(near, far, counts, slot, proxy_cell, cols):
     return kernel_call(
         far_density_kernel,
         (
@@ -898,14 +960,13 @@
             shape(SEND, dtype=i32),
             shape(1, dtype=i32),
         ),
-        [VMEM] + [SMEM] * 3 + [VMEM],
+        [ANY, VMEM] + [SMEM] * 3 + [VMEM],
         (VMEM,) * 3 + (SMEM,) * 4,
         [
             vmem(BLOCKS + 1, 1, PART),
-            vmem(CELLS, PART, 48, dtype=bf16),
             vmem(CELLS, PART, 128),
             vmem(CELLS, PART, 128),
-            vmem(BLOCKS, 48, PART, dtype=bf16),
+            vmem(RING, 128, PART, dtype=bf16),
             vmem(BLOCKS, 1, PART),
             vmem(BLOCKS, 1, PART),
         ]
@@ -913,7 +974,7 @@
         + [smem(CELLS)],
         flops=128 * PART * PART * 300,
         moved=2**20,
-    )(far, counts, slot, proxy_cell, cols)
+    )(near, far, counts, slot, proxy_cell, cols)
 
 
 def slopes(fluid, acc1, first, count, blocks, counts, block_own, size, cols):
@@ -926,11 +987,9 @@
         [ANY, VMEM if first == 0 else ANY, VMEM] + [SMEM] * 3 + [VMEM],
         (ANY, VMEM),
         [
-            vmem(CELLS, PART, 48, dtype=bf16),
-            vmem(CELLS, PART, 48, dtype=bf16),
             vmem(CELLS, PART, 128),
-            vmem(count, 48, PART, dtype=bf16),
-            vmem(count, 48, PART, dtype=bf16),
+            vmem(RING, 128, PART, dtype=bf16),
+            vmem(RING, 128, PART, dtype=bf16),
             vmem(count, 1, PART),
         ]
         + SQUARE * 2
@@ -951,13 +1010,11 @@
         (VMEM, VMEM),
         [
             vmem(BLOCKS + 1, 4, PART),
-            vmem(CELLS, PART, 128),
-            vmem(CELLS, PART, 48, dtype=bf16),
-            vmem(CELLS, PART, 48, dtype=bf16),
+            vmem(CELLS, PART, 128, dtype=bf16),
             vmem(CELLS, PART, 128),
             vmem(BLOCKS + 1, 2, PART),
-            vmem(BLOCKS, 48, PART, dtype=bf16),
-            vmem(BLOCKS, 48, PART, dtype=bf16),
+            vmem(RING, 128, PART, dtype=bf16),
+            vmem(RING, 128, PART, dtype=bf16),
             vmem(CELLS, 24, PART, dtype=bf16),
             vmem(CELLS, 8, PART),
             vmem(BLOCKS, 24, PART, dtype=bf16),
@@ -984,11 +1041,9 @@
         [
             vmem(CELLS, 8, PART),
             vmem(CELLS + 1, 8, PART),
-            vmem(CELLS, PART, 48, dtype=bf16),
-            vmem(CELLS, PART, 48, dtype=bf16),
             vmem(CELLS, PART, 128),
-            vmem(CELLS, 48, PART, dtype=bf16),
-            vmem(CELLS, 48, PART, dtype=bf16),
+            vmem(CELLS, 128, PART, dtype=bf16),
+            vmem(CELLS, 128, PART, dtype=bf16),
             vmem(CELLS, 24, PART, dtype=bf16),
             vmem(CELLS, 8, PART),
             vmem(CELLS, 3, PART, 128),
@@ -1022,14 +1077,15 @@
         moved=2**20,
     )(proxy_dest[:, 0], proxy_target)
     goals = exchange(req, both)[:, 0, 0:CAP].reshape(slots)
-    near, state, cols = own_density(
-        position, velocity, mass, smoothing, counts, pair_first, pair_offset
+    state, cols = cell_state(
+        position.transpose(1, 0, 2), velocity.transpose(1, 0, 2), mass, smoothing, counts
     )
     answer = kernel_call(
         respond_kernel, shape(slots, 8, PART), [VMEM, SMEM], VMEM, moved=4 * 2**20
     )(state, goals)
     far = exchange(answer, both)
-    acc1, ret, *plan = far_density(far, counts, slot, proxy_cell, cols)
+    near = own_density(answer, state, cols, counts, pair_first, pair_offset)
+    acc1, ret, *plan = far_density(near, far, counts, slot, proxy_cell, cols)
     blocks, offset, block_own, live, size = plan
     ready0, far_sums = slopes(near, acc1, 0, EARLY, blocks, counts, block_own, size, cols)
     back = exchange(ret, both)
@@ -1062,9 +1118,9 @@
         mig_dest[:, 0],
     )
     arrived = kernel_call(
-        inbox_kernel, shape(col_count * CAPM, 9, PART), [VMEM], VMEM, moved=2**20
+        inbox_kernel, shape(9, col_count * CAPM, PART), [VMEM], VMEM, moved=2**20
     )(exchange(leave, "cols"))
-    return (density, accel, arrived)
+    return (density, accel, arrived.transpose(1, 0, 2))
 
 
 def solution(mesh):

time: 260 us -> 244 us (0.938)
  blocking collectives: 56.8 us -> 14.8 us
  waiting for transfers between devices: 0.01 us -> 25.2 us
  Pallas kernels: 145 us -> 151 us
  local copies, waits for them, and re-layouts: 8.17 us -> 4.76 us
    all_to_all x2 -> x1, blocking collectives: 56.8 us -> 14.8 us  [exchange(): return lax.all_to_all(x, axes, split_axis=0, concat_axis=0, tiled=True)]
    all_to_all x4 -> x5, waiting for transfers between devices: 0.01 us -> 25.2 us  [exchange(): return lax.all_to_all(x, axes, split_axis=0, concat_axis=0, tiled=True)]
    pallas_call x1, Pallas kernels: 32.1 us -> 36.2 us  [far_force(): kernel_call(far_force_kernel, (shape(CELLS, 8, PART), shape(far_fluid.sha...]
    unnamed x9 -> x8, local copies, waits for them, and re-layouts: 7.33 us -> 3.87 us
    all_to_all x4 -> x5, starting transfers between devices: 48.2 us -> 45.9 us  [exchange(): return lax.all_to_all(x, axes, split_axis=0, concat_axis=0, tiled=True)]
    pallas_call x2 -> x3, Pallas kernels: 15.3 us -> 16.7 us  [the longest x1 12.4 us: own_density(): kernel_call(own_density_kernel, shape(CELLS, 1, PART), [ANY] + [VMEM] * 2...]
  transfers between devices with their start and end apart: 4 -> 5, of which waited for: 0 -> 3; matrix products, arithmetic and copies ran while one was open for 1% -> 0% of each run, Pallas kernels for 26% -> 28%
where the time goes in v5:
time: 244 us; the launch traced here: 243 us
  Pallas kernels  151 us (62%)
  starting transfers between devices  45.9 us (19%)
  waiting for transfers between devices  25.2 us (10%)
  blocking collectives  14.8 us (6%)
  local copies, waits for them, and re-layouts  4.76 us (2%)
    all_to_all x5, starting transfers between devices, exchange(): return lax.all_to_all(x, axes, split_axis=0, concat_axis=0, tiled=True)  45.9 us
    pallas_call x1, Pallas kernels, far_force(): kernel_call(far_force_kernel, (shape(CELLS, 8, PART), shape(far_fluid.sha...  36.2 us
    pallas_call x2, Pallas kernels, slopes(): kernel_call(body, (shape(count, 2, PART, PART), shape(CELLS, 1, PART)), [...  35.9 us
    pallas_call x1, Pallas kernels, far_density(): kernel_call(far_density_kernel, (shape(CELLS, PART, 128), shape(far.shape...  32.6 us
    all_to_all x5, waiting for transfers between devices, exchange(): return lax.all_to_all(x, axes, split_axis=0, concat_axis=0, tiled=True)  25.2 us
    pallas_call x1, Pallas kernels, own_force(): kernel_call(own_force_kernel, shape(CELLS, 8, PART), [ANY] + [VMEM] * 2 +...  17.8 us
    all_to_all x1, blocking collectives, exchange(): return lax.all_to_all(x, axes, split_axis=0, concat_axis=0, tiled=True)  14.8 us
    pallas_call x1, Pallas kernels, own_density(): kernel_call(own_density_kernel, shape(CELLS, 1, PART), [ANY] + [VMEM] * 2...  12.4 us
  transfers between devices with their start and end apart: 5, of which 3 were waited for; matrix products, arithmetic and copies ran while one was open for 0% of the time, Pallas kernels for 28%

profile of v5, /device:TPU:0, one launch (start us, length us, event | category | flops | bytes accessed | tf_op | source)
XLA Modules:
  0.0 242.6 jit_solution(8937316721964681042)
XLA Ops:
  0.6 2.2 shard_map.149
  2.9 11.1 %all-to-all-start = ((s32[128,1,128]{2,1,0:T(1,128)}), s32[128,1,128]{2,1,0:T(1,128)S(1)}, u32[]{:S(2)}, u32[]{:S(2)}) async-start(s32[128,1,128]{2,1,0:T(1,128)} %get-tuple-element.25), calls=%async_computation | async-start | bytes 131072 | tf_op jit(solution)/shard_map/all_to_all | solution.py:1060
  14.0 2.5 %shard_map.148 = (f32[16,8,256]{2,1,0:T(8,128)}, bf16[16,256,128]{2,1,0:T(8,128)(2,1)}) custom-call(f32[3,16,256]{2,1,0:T(8,128)} %bitcast.6, f32[3,16,256]{2,1,0:T(8,128)} %bitcast.7, f32[16,256]{1,0:T(8,128)} %mass.1, f32[16,256]{1,0:T(8,128)} %smooth.1, s32[16]{0:T(128)} %counts.13), custom_call_target="tpu_custom_call" | custom-call | flops 1048576 | bytes 4194304 | tf_op jit(solution)/shard_map/pallas_call | solution.py:919
  16.6 6.9 %all-to-all-done = s32[128,1,128]{2,1,0:T(1,128)S(1)} async-done(((s32[128,1,128]{2,1,0:T(1,128)}), s32[128,1,128]{2,1,0:T(1,128)S(1)}, u32[]{:S(2)}, u32[]{:S(2)}) %all-to-all-start) | async-done | bytes 65568 | tf_op jit(solution)/shard_map/all_to_all | solution.py:1060
  23.4 0.2 slice_reduce_fusion
  23.6 0.7 reshape_squeeze.3.goals
  24.3 3.0 %shard_map.150.after = f32[256,8,256]{2,1,0:T(8,128)} custom-call(f32[16,8,256]{2,1,0:T(8,128)} %get-tuple-element.24.state, s32[256]{0:T(256)} %reshape_squeeze.3.goals), custom_call_target="tpu_custom_call" | custom-call | bytes 4194304 | tf_op jit(solution)/shard_map/pallas_call | solution.py:1083
  27.3 4.6 %all-to-all-start.1 = ((f32[256,8,256]{2,1,0:T(8,128)}), f32[256,8,256]{2,1,0:T(8,128)S(1)}, u32[]{:S(2)}, u32[]{:S(2)}) async-start(f32[256,8,256]{2,1,0:T(8,128)} %shard_map.150.after), calls=%async_computation.1 | async-start | bytes 4194304 | tf_op jit(solution)/shard_map/all_to_all | solution.py:1060
  32.0 12.4 %shard_map.151.near.refs_0_ = f32[16,1,256]{2,1,0:T(1,128)} custom-call(f32[256,8,256]{2,1,0:T(8,128)} %shard_map.150.after, f32[16,8,256]{2,1,0:T(8,128)} %get-tuple-element.24.state, bf16[16,256,128]{2,1,0:T(8,128)(2,1)} %get-tuple-element.26.cols.refs_6_.cols_far, s32[16]{0:T(128)} %counts.13, s32[16]{0:T(128)} %pair_first.3, s32[16]{0:T(128)} %pair_offset.3), custom_call_target="tpu_custom_call" | custom-call | flops 629145600 | bytes 1048576 | tf_op jit(solution)/shard_map/pallas_call | solution.py:930
  44.3 17.4 %all-to-all-done.1.far = f32[256,8,256]{2,1,0:T(8,128)S(1)} async-done(((f32[256,8,256]{2,1,0:T(8,128)}), f32[256,8,256]{2,1,0:T(8,128)S(1)}, u32[]{:S(2)}, u32[]{:S(2)}) %all-to-all-start.1) | async-done | bytes 2097184 | tf_op jit(solution)/shard_map/all_to_all | solution.py:1060
  61.7 0.0 copy-start.2
  61.7 1.3 copy-done.2
  63.0 32.6 %shard_map.152 = (f32[16,256,128]{2,1,0:T(8,128)}, f32[256,1,256]{2,1,0:T(1,128)}, f32[145,8,256]{2,1,0:T(8,128)}, s32[128]{0:T(128)}, s32[144]{0:T(256)}, /*index=5*/s32[128]{0:T(128)}, s32[1]{0:T(128)}) custom-call(f32[16,1,256]{2,1,0:T(1,128)} %shard_map.151.near.refs_0_, f32[256,8,256]{2,1,0:T(8,128)} %copy-done.2, s32[16]{0:T(128)} %counts.13, ...), custom_call_target="tpu_custom_call" | custom-call | flops 2516582400 | bytes 1048576 | tf_op jit(solution)/shard_map/pallas_call | solution.py:952
  95.6 7.0 %all-to-all-start.2 = ((f32[256,1,256]{2,1,0:T(1,128)}), f32[256,1,256]{2,1,0:T(1,128)S(1)}, u32[]{:S(2)}, u32[]{:S(2)}) async-start(f32[256,1,256]{2,1,0:T(1,128)} %get-tuple-element.33), calls=%async_computation.2 | async-start | bytes 524288 | tf_op jit(solution)/shard_map/all_to_all | solution.py:1060
  102.7 15.3 %shard_map.153 = (f32[32,2,256,256]{3,2,1,0:T(8,128)}, f32[16,1,256]{2,1,0:T(1,128)}) custom-call(f32[16,1,256]{2,1,0:T(1,128)} %shard_map.151.near.refs_0_, f32[16,256,128]{2,1,0:T(8,128)} %get-tuple-element.28.refs_1_, f32[145,8,256]{2,1,0:T(8,128)} %get-tuple-element.29.refs_2_.blocks, s32[16]{0:T(128)} %counts.13, ...), custom_call_target="tpu_custom_call" | custom-call | flops 838860800 | bytes 16777216 | tf_op jit(solution)/shard_map/pallas_call | solution.py:984
  118.0 0.0 all-to-all-done.2.back
  118.0 0.0 copy-start.3
  118.0 0.7 copy-done.3
  118.7 3.0 %shard_map.154 = (f32[16,256]{1,0:T(8,128)}, f32[16,2,256]{2,1,0:T(2,128)}, f32[256,2,256]{2,1,0:T(2,128)}) custom-call(f32[32,2,256,256]{3,2,1,0:T(8,128)} %get-tuple-element.32.after.ready0, f32[256,1,256]{2,1,0:T(1,128)} %copy-done.3, s32[256]{0:T(256)} %reshape_squeeze.3.goals, f32[16,1,256]{2,1,0:T(1,128)} %shard_map.151.near.refs_0_, ...), custom_call_target="tpu_custom_call" | custom-call | bytes 1048576 | tf_op jit(solution)/shard_map/pallas_call | solution.py:1092
  121.7 10.1 %all-to-all-start.3 = ((f32[256,2,256]{2,1,0:T(2,128)}), f32[256,2,256]{2,1,0:T(2,128)S(1)}, u32[]{:S(2)}, u32[]{:S(2)}) async-start(f32[256,2,256]{2,1,0:T(2,128)} %get-tuple-element.37), calls=%async_computation.3 | async-start | bytes 1048576 | tf_op jit(solution)/shard_map/all_to_all | solution.py:1060
  131.8 20.6 %shard_map.155 = (f32[60,2,256,256]{3,2,1,0:T(8,128)}, f32[16,1,256]{2,1,0:T(1,128)}) custom-call(f32[16,2,256]{2,1,0:T(2,128)} %get-tuple-element.36.refs_0_.fluid, f32[16,256,128]{2,1,0:T(8,128)} %get-tuple-element.28.refs_1_, f32[145,8,256]{2,1,0:T(8,128)} %get-tuple-element.29.refs_2_.blocks, s32[16]{0:T(128)} %counts.13, ...), custom_call_target="tpu_custom_call" | custom-call | flops 1572864000 | bytes 31457280 | tf_op jit(solution)/shard_map/pallas_call | solution.py:984
  152.4 0.0 all-to-all-done.3.far_fluid
  152.4 0.0 copy-start.1
  152.4 0.8 copy-done.1
  153.3 36.2 %shard_map.156 = (f32[16,8,256]{2,1,0:T(8,128)}, f32[256,4,256]{2,1,0:T(4,128)}) custom-call(f32[16,8,256]{2,1,0:T(8,128)} %get-tuple-element.24.state, f32[16,2,256]{2,1,0:T(2,128)} %get-tuple-element.36.refs_0_.fluid, f32[145,8,256]{2,1,0:T(8,128)} %get-tuple-element.29.refs_2_.blocks, f32[256,2,256]{2,1,0:T(2,128)} %copy-done.1, s32[16]{0:T(128)} %counts.13, ...), custom_call_target="tpu_custom_call" | custom-call | flops 2516582400 | bytes 1048576 | tf_op jit(solution)/shard_map/pallas_call | solution.py:1006
  189.5 12.9 %all-to-all-start.4 = ((f32[256,4,256]{2,1,0:T(4,128)}), f32[256,4,256]{2,1,0:T(4,128)S(1)}, u32[]{:S(2)}, u32[]{:S(2)}) async-start(f32[256,4,256]{2,1,0:T(4,128)} %get-tuple-element.41), calls=%async_computation.4 | async-start | bytes 2097152 | tf_op jit(solution)/shard_map/all_to_all | solution.py:1060
  202.5 17.8 %shard_map.157.near = f32[16,8,256]{2,1,0:T(8,128)} custom-call(f32[16,8,256]{2,1,0:T(8,128)} %get-tuple-element.42.after.far, f32[16,8,256]{2,1,0:T(8,128)} %get-tuple-element.24.state, f32[16,2,256]{2,1,0:T(2,128)} %get-tuple-element.36.refs_0_.fluid, s32[16]{0:T(128)} %counts.13, s32[16]{0:T(128)} %pair_first.3, s32[16]{0:T(128)} %pair_offset.3, ...), custom_call_target="tpu_custom_call" | custom-call | flops 1258291200 | bytes 1048576 | tf_op jit(solution)/shard_map/pallas_call | solution.py:1036
  220.3 1.0 all-to-all-done.4.back
  221.3 1.0 copy-done
  222.3 3.7 %shard_map.158 = (f32[16,4,256]{2,1,0:T(4,128)}, f32[16,9,2,256]{3,2,1,0:T(2,128)}) custom-call(f32[256,4,256]{2,1,0:T(4,128)} %copy-done, s32[256]{0:T(256)} %reshape_squeeze.3.goals, f32[16,8,256]{2,1,0:T(8,128)} %shard_map.157.near, f32[16,8,256]{2,1,0:T(8,128)} %get-tuple-element.42.after.far, f32[16,8,256]{2,1,0:T(8,128)} %get-tuple-element.24.state, ...), custom_call_target="tpu_custom_call" | custom-call | bytes 1048576 | tf_op jit(solution)/shard_map/pallas_call | solution.py:1109
  226.0 14.8 %all_to_all.30.came = f32[16,9,2,256]{3,2,1,0:T(2,128)} all-to-all(f32[16,9,2,256]{3,2,1,0:T(2,128)} %get-tuple-element.44), channel_id=1, replica_groups=mesh['rows'=8,'cols'=16] {'cols'}, dimensions={0} | all-to-all | bytes 589824 | tf_op jit(solution)/shard_map/all_to_all | solution.py:1060
  240.8 1.8 shard_map.159
  (1 shorter events, 0.0 us)
Async XLA Ops:
  2.9 20.6 %all-to-all-start = ((s32[128,1,128]{2,1,0:T(1,128)}), s32[128,1,128]{2,1,0:T(1,128)S(1)}, u32[]{:S(2)}, u32[]{:S(2)}) async-start(s32[128,1,128]{2,1,0:T(1,128)} %get-tuple-element.25), calls=%async_computation | async-start | bytes 131072 | tf_op jit(solution)/shard_map/all_to_all | solution.py:1060
  27.3 34.4 %all-to-all-start.1 = ((f32[256,8,256]{2,1,0:T(8,128)}), f32[256,8,256]{2,1,0:T(8,128)S(1)}, u32[]{:S(2)}, u32[]{:S(2)}) async-start(f32[256,8,256]{2,1,0:T(8,128)} %shard_map.150.after), calls=%async_computation.1 | async-start | bytes 4194304 | tf_op jit(solution)/shard_map/all_to_all | solution.py:1060
  61.7 1.3 copy-start.2
  95.6 22.4 %all-to-all-start.2 = ((f32[256,1,256]{2,1,0:T(1,128)}), f32[256,1,256]{2,1,0:T(1,128)S(1)}, u32[]{:S(2)}, u32[]{:S(2)}) async-start(f32[256,1,256]{2,1,0:T(1,128)} %get-tuple-element.33), calls=%async_computation.2 | async-start | bytes 524288 | tf_op jit(solution)/shard_map/all_to_all | solution.py:1060
  118.0 0.7 copy-start.3
  121.7 30.7 %all-to-all-start.3 = ((f32[256,2,256]{2,1,0:T(2,128)}), f32[256,2,256]{2,1,0:T(2,128)S(1)}, u32[]{:S(2)}, u32[]{:S(2)}) async-start(f32[256,2,256]{2,1,0:T(2,128)} %get-tuple-element.37), calls=%async_computation.3 | async-start | bytes 1048576 | tf_op jit(solution)/shard_map/all_to_all | solution.py:1060
  152.4 0.9 copy-start.1
  189.5 31.8 %all-to-all-start.4 = ((f32[256,4,256]{2,1,0:T(4,128)}), f32[256,4,256]{2,1,0:T(4,128)S(1)}, u32[]{:S(2)}, u32[]{:S(2)}) async-start(f32[256,4,256]{2,1,0:T(4,128)} %get-tuple-element.41), calls=%async_computation.4 | async-start | bytes 2097152 | tf_op jit(solution)/shard_map/all_to_all | solution.py:1060
  221.3 1.0 copy-start

commit v6 on v5

--- a/solution.py
+++ b/solution.py
@@ -21,8 +21,6 @@
 CHUNK = 32
 ROWS = (128, 160, 192, 224, 256)
 BLOCKS = SEND + CELLS
-EARLY, LATE = 32, 60
-DEPTH = 4
 RING = 8
 
 f32, bf16, i32 = jnp.float32, jnp.bfloat16, jnp.int32
@@ -470,9 +468,8 @@
 
 
 def combine_density_kernel(
-    after, back, goals, near, far, energy, counts, density, fluid, answer, *sums
+    back, goals, near, far, energy, counts, density, fluid, answer, *sums
 ):
-    del after
     add_by_goal(back, goals, sums)
     lane = lax.broadcasted_iota(i32, (1, PART), 1)
 
@@ -591,99 +588,12 @@
         col[c, k] = wide[:, 128 * k : 128 * (k + 1)]
 
 
-def slope_kernel(
-    fluid, acc1, blocks, counts, block_own, size, cols, out, far_sums,
-    bh, bd, bs, hj, dist0, dist1, appr0, appr1, buf, sems, *, first,
-):
-    del fluid
-    expand(cols, bh)
-    bd[...] = jnp.zeros_like(bd)
-    bs[...] = jnp.zeros_like(bs)
-    if first == 0:
-
-        def total(c, _):
-            far_sums[c] = column_sums(acc1[c])
-            return 0
-
-        lax.fori_loop(0, CELLS, total, 0, unroll=2)
-    else:
-        far_sums[...] = jnp.zeros_like(far_sums)
-    dist, appr = (dist0, dist1), (appr0, appr1)
-    count = jnp.clip(size[0] - first, 0, out.shape[0])
-    last = first + count - 1
-
-    def clamp(p):
-        return jnp.minimum(p, last)
-
-    def prepare(p):
-        rows = blocks[p]
-        geometry_prepare(p, rows, bd, bs)
-        hj[p - first] = rows[6:7]
-
-    def load(p, side):
-        a = block_own[p]
-        o = lax.rem(p, RING)
-        dist[side][...] = nn(cols[a], bd[o])
-        appr[side][...] = nn(cols[a], bs[o])
-
-    def copy(t, rows):
-        k = lax.rem(t, DEPTH)
-        return pltpu.make_async_copy(
-            buf.at[k, :, :, pl.ds(0, rows), :],
-            out.at[pl.ds(2 * t, 2), :, pl.ds(0, rows), :],
-            sems.at[k],
-        )
-
-    def need(t):
-        p = first + 2 * t
-        return jnp.maximum(counts[block_own[p]], counts[block_own[p + 1]])
-
-    def wait(t):
-        by_rows(need(t), lambda rows: copy(t, rows).wait())
-
-    def work(p, side, rows, k):
-        a = block_own[p]
-        h_j = hj[p - first]
-        for c in range(0, rows, CHUNK):
-            grad, m = slope_weights(
-                dist[side][c : c + CHUNK, :],
-                appr[side][c : c + CHUNK, :],
-                two_wide(bh[a, c : c + CHUNK, :], h_j),
-            )
-            buf[k, side, 0, c : c + CHUNK, :] = grad
-            buf[k, side, 1, c : c + CHUNK, :] = m
-
-    @pl.when(count > 0)
-    def _():
-        for k in range(3):
-            prepare(clamp(first + k))
-        load(first, 0)
-
-    def body(t, _):
-        p = first + 2 * t
-        k = lax.rem(t, DEPTH)
-        pl.when(t >= DEPTH)(lambda: wait(t - DEPTH))
-
-        def step(rows):
-            load(p + 1, 1)
-            work(p, 0, rows, k)
-            work(p + 1, 1, rows, k)
-            load(clamp(p + 2), 0)
-            prepare(clamp(p + 3))
-            prepare(clamp(p + 4))
-            copy(t, rows).start()
-
-        by_rows(need(t), step)
-        return 0
-
-    steps = count // 2
-    lax.fori_loop(0, steps, body, 0)
-
-    def drain(t, _):
-        wait(t)
-        return 0
-
-    lax.fori_loop(jnp.maximum(steps - DEPTH, 0), steps, drain, 0)
+def sums_kernel(acc1, out):
+    def total(c, _):
+        out[c] = column_sums(acc1[c])
+        return 0
+
+    lax.fori_loop(0, CELLS, total, 0, unroll=4)
 
 
 def force_sums(rows, sums):
@@ -696,10 +606,9 @@
 
 
 def own_force_kernel(
-    after, state, fluid, counts, pair_first, pair_offset, cols, total,
+    state, fluid, counts, pair_first, pair_offset, cols, total,
     acc1, acc2, bh, bd, bs, cf, row, col, dist0, dist1, appr0, appr1, ws0, ws1, pa, po, ps,
 ):
-    del after
     expand(cols, bh)
     bd[...] = jnp.zeros_like(bd)
     bs[...] = jnp.zeros_like(bs)
@@ -726,39 +635,12 @@
 
 
 def far_force_kernel(
-    state, fluid, blocks, far_fluid, counts, slot, offset, block_own, live, size, cols_far,
-    ready0, ready1, acc1, ret,
-    acc2, cols, bh, fluids, bd, bs, own_cf, own_row, cf, row, col,
-    dist0, dist1, appr0, appr1, ws0, ws1, buf, sems,
+    near, state, fluid, blocks, far_fluid, counts, slot, offset, block_own, live, size, cols,
+    acc1, ret,
+    acc2, bh, fluids, bd, bs, own_cf, own_row, cf, row, col, dist0, dist1, appr0, appr1, ws0, ws1,
 ):
+    del near
     total = size[0]
-    half = ready0.shape[0] // 2
-    steps = jnp.minimum(total, ready0.shape[0] + ready1.shape[0]) // 2
-
-    def need(t):
-        return jnp.maximum(counts[block_own[2 * t]], counts[block_own[2 * t + 1]])
-
-    def copy(ready, t, k, rows):
-        return pltpu.make_async_copy(
-            ready.at[pl.ds(2 * t, 2), :, pl.ds(0, rows), :],
-            buf.at[k, :, :, pl.ds(0, rows), :],
-            sems.at[k],
-        )
-
-    def start(t):
-        k = lax.rem(t, DEPTH)
-
-        @pl.when(t < half)
-        def _():
-            by_rows(need(t), lambda rows: copy(ready0, t, k, rows).start())
-
-        @pl.when(t >= half)
-        def _():
-            by_rows(need(t), lambda rows: copy(ready1, t - half, k, rows).start())
-
-    for t in range(DEPTH - 1):
-        pl.when(t < steps)(lambda t=t: start(t))
-
     matrix = spreader((1, 2, 3))
 
     def mine(c, _):
@@ -768,6 +650,9 @@
         return 0
 
     lax.fori_loop(0, CELLS, mine, 0, unroll=2)
+    expand(cols, bh)
+    bd[...] = jnp.zeros_like(bd)
+    bs[...] = jnp.zeros_like(bs)
     fluids[...] = jnp.ones_like(fluids)
 
     def fill(e, _):
@@ -776,21 +661,12 @@
 
     lax.fori_loop(0, SEND, fill, 0, unroll=8)
     acc1[...] = jnp.zeros_like(acc1)
-    acc2[...] = jnp.zeros_like(acc2)
     ws0[...] = jnp.zeros_like(ws0)
     ws1[...] = jnp.zeros_like(ws1)
-    ws = (ws0, ws1)
 
     def prepare(p):
         rows = blocks[p]
-        fluid_prepare(p, rows, basis(rows)[0], fluids[p], cf, row)
-
-    last = 2 * steps - 1
-    for k in range(2):
-        prepare(jnp.int32(k))
-
-    def combine(p, side):
-        return force_combine(own_cf[block_own[p]], cf[p], ws[side])
+        fluid_prepare(p, rows, geometry_prepare(p, rows, bd, bs), fluids[p], cf, row)
 
     def store(p, sums, valid):
         first, second = sums
@@ -799,53 +675,11 @@
         acc1[block_own[p]] += first
         acc2[p] = force_sums(blocks[p], second)
 
-    def body(t, _):
-        p = 2 * t
-        k = lax.rem(t, DEPTH)
-        pl.when(t + DEPTH - 1 < steps)(lambda: start(t + DEPTH - 1))
-
-        def work(p, side, rows):
-            def grads(c):
-                return buf[k, side, 0, c : c + CHUNK, :], buf[k, side, 1, c : c + CHUNK, :]
-
-            fluid_work(ws[side], col, row[p], block_own[p], rows, grads)
-
-        def step(rows):
-            copy(ready0, 0, k, rows).wait()
-            before = jnp.maximum(p - 1, 0)
-            sums = combine(before, 1)
-            work(p, 0, rows)
-            sums0 = combine(p, 0)
-            work(p + 1, 1, rows)
-            store(before, sums, t > 0)
-            store(p, sums0, True)
-            prepare(jnp.minimum(p + 2, last))
-            prepare(jnp.minimum(p + 3, last))
-
-        by_rows(need(t), step)
-        return 0
-
-    lax.fori_loop(0, steps, body, 0)
-    store(last, combine(last, 1), True)
-
-    @pl.when(total > 2 * steps)
-    def _():
-        pltpu.sync_copy(cols_far, cols)
-        expand(cols, bh)
-        bd[...] = jnp.zeros_like(bd)
-        bs[...] = jnp.zeros_like(bs)
-
-        def rest(p):
-            rows = blocks[p]
-            fluid_prepare(p, rows, geometry_prepare(p, rows, bd, bs), fluids[p], cf, row)
-
-        refs = (
-            bd, bs, own_cf, cf, cols, bh, row, col, (dist0, dist1), (appr0, appr1), ws,
-        )
-        same = lambda p: p
-        full_force(
-            2 * steps, total - 2 * steps, counts, lambda p: block_own[p], same, refs, rest, store,
-        )
+    refs = (
+        bd, bs, own_cf, cf, cols, bh, row, col, (dist0, dist1), (appr0, appr1), (ws0, ws1),
+    )
+    same = lambda p: p
+    full_force(0, total, counts, lambda p: block_own[p], same, refs, prepare, store)
 
     def back(e, _):
         ret[slot[e]] = unpack(acc2, offset[e])
@@ -977,40 +811,16 @@
     )(near, far, counts, slot, proxy_cell, cols)
 
 
-def slopes(fluid, acc1, first, count, blocks, counts, block_own, size, cols):
-    def body(*refs):
-        slope_kernel(*refs, first=first)
-
-    return kernel_call(
-        body,
-        (shape(count, 2, PART, PART), shape(CELLS, 1, PART)),
-        [ANY, VMEM if first == 0 else ANY, VMEM] + [SMEM] * 3 + [VMEM],
-        (ANY, VMEM),
-        [
-            vmem(CELLS, PART, 128),
-            vmem(RING, 128, PART, dtype=bf16),
-            vmem(RING, 128, PART, dtype=bf16),
-            vmem(count, 1, PART),
-        ]
-        + SQUARE * 2
-        + [vmem(DEPTH, 2, 2, PART, PART), pltpu.SemaphoreType.DMA((DEPTH,))],
-        flops=count * PART * PART * 400,
-        moved=count * 2**19,
-    )(fluid, acc1, blocks, counts, block_own, size, cols)
-
-
 def far_force(
-    state, fluid, far_fluid, counts, slot, blocks, offset, block_own, live, size, cols,
-    ready0, ready1,
+    near, state, fluid, far_fluid, counts, slot, blocks, offset, block_own, live, size, cols
 ):
     return kernel_call(
         far_force_kernel,
         (shape(CELLS, 8, PART), shape(far_fluid.shape[0], 4, PART)),
-        [VMEM] * 4 + [SMEM] * 6 + [ANY] * 3,
+        [ANY] + [VMEM] * 4 + [SMEM] * 6 + [VMEM],
         (VMEM, VMEM),
         [
             vmem(BLOCKS + 1, 4, PART),
-            vmem(CELLS, PART, 128, dtype=bf16),
             vmem(CELLS, PART, 128),
             vmem(BLOCKS + 1, 2, PART),
             vmem(RING, 128, PART, dtype=bf16),
@@ -1022,21 +832,20 @@
             vmem(CELLS, 3, PART, 128),
         ]
         + SQUARE * 2
-        + WS
-        + [vmem(DEPTH, 2, 2, PART, PART), pltpu.SemaphoreType.DMA((DEPTH,))],
-        flops=128 * PART * PART * 300,
+        + WS,
+        flops=128 * PART * PART * 600,
         moved=2**20,
     )(
-        state, fluid, blocks, far_fluid, counts, slot, offset, block_own, live, size,
-        cols, ready0, ready1,
-    )
-
-
-def own_force(after, state, fluid, counts, pair_first, pair_offset, cols):
+        near, state, fluid, blocks, far_fluid, counts, slot, offset, block_own, live, size,
+        cols,
+    )
+
+
+def own_force(state, fluid, counts, pair_first, pair_offset, cols):
     return kernel_call(
         own_force_kernel,
         shape(CELLS, 8, PART),
-        [ANY] + [VMEM] * 2 + [SMEM] * 3 + [VMEM],
+        [VMEM] * 2 + [SMEM] * 3 + [VMEM],
         VMEM,
         [
             vmem(CELLS, 8, PART),
@@ -1053,7 +862,7 @@
         + [smem(CELLS + PAIRS)] * 3,
         flops=32 * PART * PART * 600,
         moved=2**20,
-    )(after, state, fluid, counts, pair_first, pair_offset, cols)
+    )(state, fluid, counts, pair_first, pair_offset, cols)
 
 
 def exchange(x, axes):
@@ -1086,24 +895,22 @@
     far = exchange(answer, both)
     near = own_density(answer, state, cols, counts, pair_first, pair_offset)
     acc1, ret, *plan = far_density(near, far, counts, slot, proxy_cell, cols)
-    blocks, offset, block_own, live, size = plan
-    ready0, far_sums = slopes(near, acc1, 0, EARLY, blocks, counts, block_own, size, cols)
+    far_sums = kernel_call(
+        sums_kernel, shape(CELLS, 1, PART), [VMEM], VMEM, flops=2**20, moved=2**21
+    )(acc1)
     back = exchange(ret, both)
     density, fluid, answer2 = kernel_call(
         combine_density_kernel,
         (shape(CELLS, PART), shape(CELLS, 2, PART), shape(slots, 2, PART)),
-        [ANY, VMEM, SMEM] + [VMEM] * 3 + [SMEM],
+        [VMEM, SMEM] + [VMEM] * 3 + [SMEM],
         (VMEM, VMEM, VMEM),
         [vmem(CELLS + 1, 1, PART)] * 4,
         moved=2**20,
-    )(ready0, back, goals, near, far_sums, energy, counts)
+    )(back, goals, near, far_sums, energy, counts)
     far_fluid = exchange(answer2, both)
-    ready1, _ = slopes(fluid, acc1, EARLY, LATE, blocks, counts, block_own, size, cols)
+    near_force = own_force(state, fluid, counts, pair_first, pair_offset, cols)
     far_force_sums, ret4 = far_force(
-        state, fluid, far_fluid, counts, slot, *plan, cols, ready0, ready1
-    )
-    near_force = own_force(
-        far_force_sums, state, fluid, counts, pair_first, pair_offset, cols
+        near_force, state, fluid, far_fluid, counts, slot, *plan, cols
     )
     back4 = exchange(ret4, both)
     accel, leave = kernel_call(

time: 244 us -> 237 us (0.971)
  blocking collectives: 14.8 us -> 46.6 us
  Pallas kernels: 151 us -> 125 us
  starting transfers between devices: 45.9 us -> 28.9 us
  waiting for transfers between devices: 25.2 us -> 32.6 us
    pallas_call x3 -> x2, Pallas kernels: 53.7 us -> 20.4 us  [the longest x1 17.3 us: own_force(): kernel_call(own_force_kernel, shape(CELLS, 8, PART), [VMEM] * 2 + [SMEM]...]
    all_to_all x1 -> x2, blocking collectives: 14.8 us -> 46.6 us  [exchange(): return lax.all_to_all(x, axes, split_axis=0, concat_axis=0, tiled=True)]
    all_to_all x5 -> x4, starting transfers between devices: 45.9 us -> 28.9 us  [exchange(): return lax.all_to_all(x, axes, split_axis=0, concat_axis=0, tiled=True)]
    pallas_call x1, Pallas kernels: 36.2 us -> 44.8 us  [far_force(): kernel_call(far_force_kernel, (shape(CELLS, 8, PART), shape(far_fluid.sha...]
    all_to_all x5 -> x4, waiting for transfers between devices: 25.2 us -> 32.6 us  [exchange(): return lax.all_to_all(x, axes, split_axis=0, concat_axis=0, tiled=True)]
  transfers between devices with their start and end apart: 5 -> 4, of which waited for: 3 -> 3; matrix products, arithmetic and copies ran while one was open for 0% -> 0% of each run, Pallas kernels for 28% -> 15%
where the time goes in v6:
time: 237 us; the launch traced here: 238 us
  Pallas kernels  125 us (53%)
  blocking collectives  46.6 us (20%)
  waiting for transfers between devices  32.6 us (14%)
  starting transfers between devices  28.9 us (12%)
  local copies, waits for them, and re-layouts  3.74 us (2%)
    all_to_all x2, blocking collectives, exchange(): return lax.all_to_all(x, axes, split_axis=0, concat_axis=0, tiled=True)  46.6 us
    pallas_call x1, Pallas kernels, far_force(): kernel_call(far_force_kernel, (shape(CELLS, 8, PART), shape(far_fluid.sha...  44.8 us
    all_to_all x4, waiting for transfers between devices, exchange(): return lax.all_to_all(x, axes, split_axis=0, concat_axis=0, tiled=True)  32.6 us
    pallas_call x1, Pallas kernels, far_density(): kernel_call(far_density_kernel, (shape(CELLS, PART, 128), shape(far.shape...  31.9 us
    all_to_all x4, starting transfers between devices, exchange(): return lax.all_to_all(x, axes, split_axis=0, concat_axis=0, tiled=True)  28.9 us
    pallas_call x1, Pallas kernels, own_force(): kernel_call(own_force_kernel, shape(CELLS, 8, PART), [VMEM] * 2 + [SMEM]...  17.3 us
    pallas_call x1, Pallas kernels, own_density(): kernel_call(own_density_kernel, shape(CELLS, 1, PART), [ANY] + [VMEM] * 2...  11.9 us
  transfers between devices with their start and end apart: 4, of which 3 were waited for; matrix products, arithmetic and copies ran while one was open for 0% of the time, Pallas kernels for 15%

profile of v6, /device:TPU:0, one launch (start us, length us, event | category | flops | bytes accessed | tf_op | source)
XLA Modules:
  0.0 237.6 jit_solution(8527369566740537655)
XLA Ops:
  0.6 2.2 shard_map.149
  2.9 11.1 %all-to-all-start = ((s32[128,1,128]{2,1,0:T(1,128)}), s32[128,1,128]{2,1,0:T(1,128)S(1)}, u32[]{:S(2)}, u32[]{:S(2)}) async-start(s32[128,1,128]{2,1,0:T(1,128)} %get-tuple-element.22), calls=%async_computation | async-start | bytes 131072 | tf_op jit(solution)/shard_map/all_to_all | solution.py:869
  14.0 2.5 %shard_map.148 = (f32[16,8,256]{2,1,0:T(8,128)}, bf16[16,256,128]{2,1,0:T(8,128)(2,1)}) custom-call(f32[3,16,256]{2,1,0:T(8,128)} %bitcast.6, f32[3,16,256]{2,1,0:T(8,128)} %bitcast.7, f32[16,256]{1,0:T(8,128)} %mass.1, f32[16,256]{1,0:T(8,128)} %smooth.1, s32[16]{0:T(128)} %counts.13), custom_call_target="tpu_custom_call" | custom-call | flops 1048576 | bytes 4194304 | tf_op jit(solution)/shard_map/pallas_call | solution.py:753
  16.6 6.9 %all-to-all-done = s32[128,1,128]{2,1,0:T(1,128)S(1)} async-done(((s32[128,1,128]{2,1,0:T(1,128)}), s32[128,1,128]{2,1,0:T(1,128)S(1)}, u32[]{:S(2)}, u32[]{:S(2)}) %all-to-all-start) | async-done | bytes 65568 | tf_op jit(solution)/shard_map/all_to_all | solution.py:869
  23.4 0.2 slice_reduce_fusion
  23.6 0.7 reshape_squeeze.3.goals
  24.3 3.0 %shard_map.150.after = f32[256,8,256]{2,1,0:T(8,128)} custom-call(f32[16,8,256]{2,1,0:T(8,128)} %get-tuple-element.21.state, s32[256]{0:T(256)} %reshape_squeeze.3.goals), custom_call_target="tpu_custom_call" | custom-call | bytes 4194304 | tf_op jit(solution)/shard_map/pallas_call | solution.py:892
  27.3 4.6 %all-to-all-start.1 = ((f32[256,8,256]{2,1,0:T(8,128)}), f32[256,8,256]{2,1,0:T(8,128)S(1)}, u32[]{:S(2)}, u32[]{:S(2)}) async-start(f32[256,8,256]{2,1,0:T(8,128)} %shard_map.150.after), calls=%async_computation.1 | async-start | bytes 4194304 | tf_op jit(solution)/shard_map/all_to_all | solution.py:869
  32.0 11.9 %shard_map.151.near = f32[16,1,256]{2,1,0:T(1,128)} custom-call(f32[256,8,256]{2,1,0:T(8,128)} %shard_map.150.after, f32[16,8,256]{2,1,0:T(8,128)} %get-tuple-element.21.state, bf16[16,256,128]{2,1,0:T(8,128)(2,1)} %get-tuple-element.23.cols, s32[16]{0:T(128)} %counts.13, s32[16]{0:T(128)} %pair_first.3, s32[16]{0:T(128)} %pair_offset.3), custom_call_target="tpu_custom_call" | custom-call | flops 629145600 | bytes 1048576 | tf_op jit(solution)/shard_map/pallas_call | solution.py:764
  43.8 17.8 %all-to-all-done.1.far = f32[256,8,256]{2,1,0:T(8,128)S(1)} async-done(((f32[256,8,256]{2,1,0:T(8,128)}), f32[256,8,256]{2,1,0:T(8,128)S(1)}, u32[]{:S(2)}, u32[]{:S(2)}) %all-to-all-start.1) | async-done | bytes 2097184 | tf_op jit(solution)/shard_map/all_to_all | solution.py:869
  61.7 0.0 copy-start
  61.7 1.3 copy-done
  63.0 31.9 %shard_map.152 = (f32[16,256,128]{2,1,0:T(8,128)}, f32[256,1,256]{2,1,0:T(1,128)}, f32[145,8,256]{2,1,0:T(8,128)}, s32[128]{0:T(128)}, s32[144]{0:T(256)}, /*index=5*/s32[128]{0:T(128)}, s32[1]{0:T(128)}) custom-call(f32[16,1,256]{2,1,0:T(1,128)} %shard_map.151.near, f32[256,8,256]{2,1,0:T(8,128)} %copy-done, s32[16]{0:T(128)} %counts.13, ...), custom_call_target="tpu_custom_call" | custom-call | flops 2516582400 | bytes 1048576 | tf_op jit(solution)/shard_map/pallas_call | solution.py:786
  94.9 8.3 %all-to-all-start.2 = ((f32[256,1,256]{2,1,0:T(1,128)}), f32[256,1,256]{2,1,0:T(1,128)S(1)}, u32[]{:S(2)}, u32[]{:S(2)}) async-start(f32[256,1,256]{2,1,0:T(1,128)} %get-tuple-element.25), calls=%async_computation.2 | async-start | bytes 524288 | tf_op jit(solution)/shard_map/all_to_all | solution.py:869
  103.2 3.0 %shard_map.153.far = f32[16,1,256]{2,1,0:T(1,128)} custom-call(f32[16,256,128]{2,1,0:T(8,128)} %get-tuple-element.26.acc1), custom_call_target="tpu_custom_call" | custom-call | flops 1048576 | bytes 2097152 | tf_op jit(solution)/shard_map/pallas_call | solution.py:898
  106.2 7.8 %all-to-all-done.2.back = f32[256,1,256]{2,1,0:T(1,128)S(1)} async-done(((f32[256,1,256]{2,1,0:T(1,128)}), f32[256,1,256]{2,1,0:T(1,128)S(1)}, u32[]{:S(2)}, u32[]{:S(2)}) %all-to-all-start.2) | async-done | bytes 262176 | tf_op jit(solution)/shard_map/all_to_all | solution.py:869
  114.1 0.0 copy-start.1
  114.1 0.7 copy-done.1
  114.8 3.0 %shard_map.154 = (f32[16,256]{1,0:T(8,128)}, f32[16,2,256]{2,1,0:T(2,128)}, f32[256,2,256]{2,1,0:T(2,128)}) custom-call(f32[256,1,256]{2,1,0:T(1,128)} %copy-done.1, s32[256]{0:T(256)} %reshape_squeeze.3.goals, f32[16,1,256]{2,1,0:T(1,128)} %shard_map.151.near, f32[16,1,256]{2,1,0:T(1,128)} %shard_map.153.far, f32[16,256]{1,0:T(8,128)} %energy.3, s32[16]{0:T(128)} %counts.13), custom_call_target="tpu_custom_call" | custom-call | bytes 1048576 | tf_op jit(solution)/shard_map/pallas_call | solution.py:902
  117.8 4.8 %all-to-all-start.3 = ((f32[256,2,256]{2,1,0:T(2,128)}), f32[256,2,256]{2,1,0:T(2,128)S(1)}, u32[]{:S(2)}, u32[]{:S(2)}) async-start(f32[256,2,256]{2,1,0:T(2,128)} %get-tuple-element.30), calls=%async_computation.3 | async-start | bytes 1048576 | tf_op jit(solution)/shard_map/all_to_all | solution.py:869
  122.6 17.3 %shard_map.155.near = f32[16,8,256]{2,1,0:T(8,128)} custom-call(f32[16,8,256]{2,1,0:T(8,128)} %get-tuple-element.21.state, f32[16,2,256]{2,1,0:T(2,128)} %get-tuple-element.28.fluid, s32[16]{0:T(128)} %counts.13, s32[16]{0:T(128)} %pair_first.3, s32[16]{0:T(128)} %pair_offset.3, bf16[16,256,128]{2,1,0:T(8,128)(2,1)} %get-tuple-element.23.cols), custom_call_target="tpu_custom_call" | custom-call | flops 1258291200 | bytes 1048576 | tf_op jit(solution)/shard_map/pallas_call | solution.py:845
  139.9 0.0 all-to-all-done.3.far_fluid
  139.9 0.0 copy-start.2
  139.9 0.8 copy-done.2
  140.8 44.8 %shard_map.156 = (f32[16,8,256]{2,1,0:T(8,128)}, f32[256,4,256]{2,1,0:T(4,128)}) custom-call(f32[16,8,256]{2,1,0:T(8,128)} %shard_map.155.near, f32[16,8,256]{2,1,0:T(8,128)} %get-tuple-element.21.state, f32[16,2,256]{2,1,0:T(2,128)} %get-tuple-element.28.fluid, f32[145,8,256]{2,1,0:T(8,128)} %get-tuple-element.29.blocks, f32[256,2,256]{2,1,0:T(2,128)} %copy-done.2, ...), custom_call_target="tpu_custom_call" | custom-call | flops 5033164800 | bytes 1048576 | tf_op jit(solution)/shard_map/pallas_call | solution.py:817
  185.5 33.7 %all_to_all.30.back = f32[256,4,256]{2,1,0:T(4,128)} all-to-all(f32[256,4,256]{2,1,0:T(4,128)} %get-tuple-element.35), channel_id=1, replica_groups=mesh['rows'=8,'cols'=16] {'rows','cols'}, dimensions={0} | all-to-all | bytes 2097152 | tf_op jit(solution)/shard_map/all_to_all | solution.py:869
  219.3 3.7 %shard_map.157 = (f32[16,4,256]{2,1,0:T(4,128)}, f32[16,9,2,256]{3,2,1,0:T(2,128)}) custom-call(f32[256,4,256]{2,1,0:T(4,128)} %all_to_all.30.back, s32[256]{0:T(256)} %reshape_squeeze.3.goals, f32[16,8,256]{2,1,0:T(8,128)} %shard_map.155.near, f32[16,8,256]{2,1,0:T(8,128)} %get-tuple-element.36.far, f32[16,8,256]{2,1,0:T(8,128)} %get-tuple-element.21.state, ...), custom_call_target="tpu_custom_call" | custom-call | bytes 1048576 | tf_op jit(solution)/shard_map/pallas_call | solution.py:916
  223.0 12.8 %all_to_all.31.came = f32[16,9,2,256]{3,2,1,0:T(2,128)} all-to-all(f32[16,9,2,256]{3,2,1,0:T(2,128)} %get-tuple-element.38), channel_id=1, replica_groups=mesh['rows'=8,'cols'=16] {'cols'}, dimensions={0} | all-to-all | bytes 589824 | tf_op jit(solution)/shard_map/all_to_all | solution.py:869
  235.8 1.8 shard_map.158
Async XLA Ops:
  2.9 20.6 %all-to-all-start = ((s32[128,1,128]{2,1,0:T(1,128)}), s32[128,1,128]{2,1,0:T(1,128)S(1)}, u32[]{:S(2)}, u32[]{:S(2)}) async-start(s32[128,1,128]{2,1,0:T(1,128)} %get-tuple-element.22), calls=%async_computation | async-start | bytes 131072 | tf_op jit(solution)/shard_map/all_to_all | solution.py:869
  27.3 34.4 %all-to-all-start.1 = ((f32[256,8,256]{2,1,0:T(8,128)}), f32[256,8,256]{2,1,0:T(8,128)S(1)}, u32[]{:S(2)}, u32[]{:S(2)}) async-start(f32[256,8,256]{2,1,0:T(8,128)} %shard_map.150.after), calls=%async_computation.1 | async-start | bytes 4194304 | tf_op jit(solution)/shard_map/all_to_all | solution.py:869
  61.7 1.3 copy-start
  94.9 19.2 %all-to-all-start.2 = ((f32[256,1,256]{2,1,0:T(1,128)}), f32[256,1,256]{2,1,0:T(1,128)S(1)}, u32[]{:S(2)}, u32[]{:S(2)}) async-start(f32[256,1,256]{2,1,0:T(1,128)} %get-tuple-element.25), calls=%async_computation.2 | async-start | bytes 524288 | tf_op jit(solution)/shard_map/all_to_all | solution.py:869
  114.1 0.7 copy-start.1
  117.8 22.1 %all-to-all-start.3 = ((f32[256,2,256]{2,1,0:T(2,128)}), f32[256,2,256]{2,1,0:T(2,128)S(1)}, u32[]{:S(2)}, u32[]{:S(2)}) async-start(f32[256,2,256]{2,1,0:T(2,128)} %get-tuple-element.30), calls=%async_computation.3 | async-start | bytes 1048576 | tf_op jit(solution)/shard_map/all_to_all | solution.py:869
  139.9 0.8 copy-start.2

commit v7 on v6

--- a/solution.py
+++ b/solution.py
@@ -605,22 +605,32 @@
     return jnp.concatenate([accel, heat], axis=0)
 
 
+def fluid_kernel(state, fluid, cols, own_cf, own_row, col, bh):
+    matrix = spreader((1, 2, 3))
+    expand(cols, bh)
+
+    def mine(c, _):
+        rows = state[c]
+        fluid_prepare(c, rows, basis(rows)[0], fluid[c], own_cf, own_row)
+        own_fluid_columns(c, own_row, col, matrix)
+        return 0
+
+    lax.fori_loop(0, CELLS, mine, 0, unroll=4)
+
+
 def own_force_kernel(
-    state, fluid, counts, pair_first, pair_offset, cols, total,
-    acc1, acc2, bh, bd, bs, cf, row, col, dist0, dist1, appr0, appr1, ws0, ws1, pa, po, ps,
+    after, state, counts, pair_first, pair_offset, cols, cf, row, col, bh, total,
+    acc1, acc2, bd, bs, dist0, dist1, appr0, appr1, ws0, ws1, pa, po, ps,
 ):
-    expand(cols, bh)
+    del after
     bd[...] = jnp.zeros_like(bd)
     bs[...] = jnp.zeros_like(bs)
-    matrix = spreader((1, 2, 3))
 
     def mine(c, _):
-        rows = state[c]
-        fluid_prepare(c, rows, geometry_prepare(c, rows, bd, bs), fluid[c], cf, row)
-        own_fluid_columns(c, row, col, matrix)
-        return 0
-
-    lax.fori_loop(0, CELLS, mine, 0, unroll=2)
+        geometry_prepare(c, state[c], bd, bs)
+        return 0
+
+    lax.fori_loop(0, CELLS, mine, 0, unroll=4)
     own_lists(pair_first, pair_offset, pa, po, ps, CELLS)
     acc1[...] = jnp.zeros_like(acc1)
     acc2[...] = jnp.zeros_like(acc2)
@@ -635,22 +645,11 @@
 
 
 def far_force_kernel(
-    near, state, fluid, blocks, far_fluid, counts, slot, offset, block_own, live, size, cols,
+    blocks, far_fluid, counts, slot, offset, block_own, live, size, cols, own_cf, col, bh,
     acc1, ret,
-    acc2, bh, fluids, bd, bs, own_cf, own_row, cf, row, col, dist0, dist1, appr0, appr1, ws0, ws1,
+    acc2, fluids, bd, bs, cf, row, dist0, dist1, appr0, appr1, ws0, ws1,
 ):
-    del near
     total = size[0]
-    matrix = spreader((1, 2, 3))
-
-    def mine(c, _):
-        rows = state[c]
-        fluid_prepare(c, rows, basis(rows)[0], fluid[c], own_cf, own_row)
-        own_fluid_columns(c, own_row, col, matrix)
-        return 0
-
-    lax.fori_loop(0, CELLS, mine, 0, unroll=2)
-    expand(cols, bh)
     bd[...] = jnp.zeros_like(bd)
     bs[...] = jnp.zeros_like(bs)
     fluids[...] = jnp.ones_like(fluids)
@@ -811,58 +810,63 @@
     )(near, far, counts, slot, proxy_cell, cols)
 
 
+def own_fluid(state, fluid, cols):
+    return kernel_call(
+        fluid_kernel,
+        (
+            shape(CELLS, 24, PART, dtype=bf16),
+            shape(CELLS, 8, PART),
+            shape(CELLS, 3, PART, 128),
+            shape(CELLS, PART, 128),
+        ),
+        [VMEM] * 3,
+        (VMEM,) * 4,
+        flops=2**22,
+        moved=2**24,
+    )(state, fluid, cols)
+
+
 def far_force(
-    near, state, fluid, far_fluid, counts, slot, blocks, offset, block_own, live, size, cols
+    far_fluid, counts, slot, blocks, offset, block_own, live, size, cols, own_cf, col, bh
 ):
     return kernel_call(
         far_force_kernel,
         (shape(CELLS, 8, PART), shape(far_fluid.shape[0], 4, PART)),
-        [ANY] + [VMEM] * 4 + [SMEM] * 6 + [VMEM],
+        [VMEM] * 2 + [SMEM] * 6 + [VMEM] * 4,
         (VMEM, VMEM),
         [
             vmem(BLOCKS + 1, 4, PART),
-            vmem(CELLS, PART, 128),
             vmem(BLOCKS + 1, 2, PART),
             vmem(RING, 128, PART, dtype=bf16),
             vmem(RING, 128, PART, dtype=bf16),
-            vmem(CELLS, 24, PART, dtype=bf16),
-            vmem(CELLS, 8, PART),
             vmem(BLOCKS, 24, PART, dtype=bf16),
             vmem(BLOCKS, 8, PART),
-            vmem(CELLS, 3, PART, 128),
         ]
         + SQUARE * 2
         + WS,
         flops=128 * PART * PART * 600,
         moved=2**20,
-    )(
-        near, state, fluid, blocks, far_fluid, counts, slot, offset, block_own, live, size,
-        cols,
-    )
-
-
-def own_force(state, fluid, counts, pair_first, pair_offset, cols):
+    )(blocks, far_fluid, counts, slot, offset, block_own, live, size, cols, own_cf, col, bh)
+
+
+def own_force(after, state, counts, pair_first, pair_offset, cols, cf, row, col, bh):
     return kernel_call(
         own_force_kernel,
         shape(CELLS, 8, PART),
-        [VMEM] * 2 + [SMEM] * 3 + [VMEM],
+        [ANY, VMEM] + [SMEM] * 3 + [VMEM] * 5,
         VMEM,
         [
             vmem(CELLS, 8, PART),
             vmem(CELLS + 1, 8, PART),
-            vmem(CELLS, PART, 128),
             vmem(CELLS, 128, PART, dtype=bf16),
             vmem(CELLS, 128, PART, dtype=bf16),
-            vmem(CELLS, 24, PART, dtype=bf16),
-            vmem(CELLS, 8, PART),
-            vmem(CELLS, 3, PART, 128),
         ]
         + SQUARE * 2
         + WS
         + [smem(CELLS + PAIRS)] * 3,
         flops=32 * PART * PART * 600,
         moved=2**20,
-    )(state, fluid, counts, pair_first, pair_offset, cols)
+    )(after, state, counts, pair_first, pair_offset, cols, cf, row, col, bh)
 
 
 def exchange(x, axes):
@@ -908,9 +912,10 @@
         moved=2**20,
     )(back, goals, near, far_sums, energy, counts)
     far_fluid = exchange(answer2, both)
-    near_force = own_force(state, fluid, counts, pair_first, pair_offset, cols)
-    far_force_sums, ret4 = far_force(
-        near_force, state, fluid, far_fluid, counts, slot, *plan, cols
+    own_cf, own_row, col, bh = own_fluid(state, fluid, cols)
+    far_force_sums, ret4 = far_force(far_fluid, counts, slot, *plan, cols, own_cf, col, bh)
+    near_force = own_force(
+        far_force_sums, state, counts, pair_first, pair_offset, cols, own_cf, own_row, col, bh
     )
     back4 = exchange(ret4, both)
     accel, leave = kernel_call(

time: 237 us -> 228 us (0.962)
  blocking collectives: 46.6 us -> 14 us
  waiting for transfers between devices: 32.6 us -> 40.4 us
  Pallas kernels: 125 us -> 132 us
  starting transfers between devices: 28.9 us -> 35.8 us
    all_to_all x2 -> x1, blocking collectives: 46.6 us -> 14 us  [exchange(): return lax.all_to_all(x, axes, split_axis=0, concat_axis=0, tiled=True)]
    all_to_all x4 -> x5, waiting for transfers between devices: 32.6 us -> 40.4 us  [exchange(): return lax.all_to_all(x, axes, split_axis=0, concat_axis=0, tiled=True)]
    all_to_all x4 -> x5, starting transfers between devices: 28.9 us -> 35.8 us  [exchange(): return lax.all_to_all(x, axes, split_axis=0, concat_axis=0, tiled=True)]
    pallas_call x1 -> x2, Pallas kernels: 17.3 us -> 24.2 us  [the longest x1 17.2 us: own_force(): kernel_call(own_force_kernel, shape(CELLS, 8, PART), [ANY, VMEM] + [SMEM]...]
  transfers between devices with their start and end apart: 4 -> 5, of which waited for: 3 -> 5; matrix products, arithmetic and copies ran while one was open for 0% -> 0% of each run, Pallas kernels for 15% -> 19%
where the time goes in v7:
time: 228 us
  Pallas kernels  132 us (58%)
  waiting for transfers between devices  40.4 us (18%)
  starting transfers between devices  35.8 us (16%)
  blocking collectives  14 us (6%)
  local copies, waits for them, and re-layouts  4.7 us (2%)
    pallas_call x1, Pallas kernels, far_force(): kernel_call(far_force_kernel, (shape(CELLS, 8, PART), shape(far_fluid.sha...  43.7 us
    all_to_all x5, waiting for transfers between devices, exchange(): return lax.all_to_all(x, axes, split_axis=0, concat_axis=0, tiled=True)  40.4 us
    all_to_all x5, starting transfers between devices, exchange(): return lax.all_to_all(x, axes, split_axis=0, concat_axis=0, tiled=True)  35.8 us
    pallas_call x1, Pallas kernels, far_density(): kernel_call(far_density_kernel, (shape(CELLS, PART, 128), shape(far.shape...  32.6 us
    pallas_call x1, Pallas kernels, own_force(): kernel_call(own_force_kernel, shape(CELLS, 8, PART), [ANY, VMEM] + [SMEM]...  17.2 us
    all_to_all x1, blocking collectives, exchange(): return lax.all_to_all(x, axes, split_axis=0, concat_axis=0, tiled=True)  14 us
    pallas_call x1, Pallas kernels, own_density(): kernel_call(own_density_kernel, shape(CELLS, 1, PART), [ANY] + [VMEM] * 2...  12.5 us
    pallas_call x1, Pallas kernels, own_fluid(): kernel_call(fluid_kernel, (shape(CELLS, 24, PART, dtype=bf16), shape(CELL...  7.04 us
  transfers between devices with their start and end apart: 5, of which 5 were waited for; matrix products, arithmetic and copies ran while one was open for 0% of the time, Pallas kernels for 19%

profile of v7, /device:TPU:0, one launch (start us, length us, event | category | flops | bytes accessed | tf_op | source)
XLA Modules:
  0.0 227.9 jit_solution(3784224342008888012)
XLA Ops:
  0.6 2.2 shard_map.149
  2.9 11.1 %all-to-all-start = ((s32[128,1,128]{2,1,0:T(1,128)}), s32[128,1,128]{2,1,0:T(1,128)S(1)}, u32[]{:S(2)}, u32[]{:S(2)}) async-start(s32[128,1,128]{2,1,0:T(1,128)} %get-tuple-element.26), calls=%async_computation | async-start | bytes 131072 | tf_op jit(solution)/shard_map/all_to_all | solution.py:873
  14.0 2.5 %shard_map.148 = (f32[16,8,256]{2,1,0:T(8,128)}, bf16[16,256,128]{2,1,0:T(8,128)(2,1)}) custom-call(f32[3,16,256]{2,1,0:T(8,128)} %bitcast.6, f32[3,16,256]{2,1,0:T(8,128)} %bitcast.7, f32[16,256]{1,0:T(8,128)} %mass.1, f32[16,256]{1,0:T(8,128)} %smooth.1, s32[16]{0:T(128)} %counts.13), custom_call_target="tpu_custom_call" | custom-call | flops 1048576 | bytes 4194304 | tf_op jit(solution)/shard_map/pallas_call | solution.py:752
  16.6 6.9 %all-to-all-done = s32[128,1,128]{2,1,0:T(1,128)S(1)} async-done(((s32[128,1,128]{2,1,0:T(1,128)}), s32[128,1,128]{2,1,0:T(1,128)S(1)}, u32[]{:S(2)}, u32[]{:S(2)}) %all-to-all-start) | async-done | bytes 65568 | tf_op jit(solution)/shard_map/all_to_all | solution.py:873
  23.4 0.2 slice_reduce_fusion
  23.6 0.7 reshape_squeeze.3.goals
  24.3 3.0 %shard_map.150.after = f32[256,8,256]{2,1,0:T(8,128)} custom-call(f32[16,8,256]{2,1,0:T(8,128)} %get-tuple-element.25.state, s32[256]{0:T(256)} %reshape_squeeze.3.goals), custom_call_target="tpu_custom_call" | custom-call | bytes 4194304 | tf_op jit(solution)/shard_map/pallas_call | solution.py:896
  27.3 4.6 %all-to-all-start.1 = ((f32[256,8,256]{2,1,0:T(8,128)}), f32[256,8,256]{2,1,0:T(8,128)S(1)}, u32[]{:S(2)}, u32[]{:S(2)}) async-start(f32[256,8,256]{2,1,0:T(8,128)} %shard_map.150.after), calls=%async_computation.1 | async-start | bytes 4194304 | tf_op jit(solution)/shard_map/all_to_all | solution.py:873
  32.0 12.5 %shard_map.151.near = f32[16,1,256]{2,1,0:T(1,128)} custom-call(f32[256,8,256]{2,1,0:T(8,128)} %shard_map.150.after, f32[16,8,256]{2,1,0:T(8,128)} %get-tuple-element.25.state, bf16[16,256,128]{2,1,0:T(8,128)(2,1)} %get-tuple-element.27.cols, s32[16]{0:T(128)} %counts.13, s32[16]{0:T(128)} %pair_first.3, s32[16]{0:T(128)} %pair_offset.3), custom_call_target="tpu_custom_call" | custom-call | flops 629145600 | bytes 1048576 | tf_op jit(solution)/shard_map/pallas_call | solution.py:763
  44.4 17.3 %all-to-all-done.1.far = f32[256,8,256]{2,1,0:T(8,128)S(1)} async-done(((f32[256,8,256]{2,1,0:T(8,128)}), f32[256,8,256]{2,1,0:T(8,128)S(1)}, u32[]{:S(2)}, u32[]{:S(2)}) %all-to-all-start.1) | async-done | bytes 2097184 | tf_op jit(solution)/shard_map/all_to_all | solution.py:873
  61.7 0.0 copy-start.1
  61.7 1.3 copy-done.1
  63.0 32.6 %shard_map.152 = (f32[16,256,128]{2,1,0:T(8,128)}, f32[256,1,256]{2,1,0:T(1,128)}, f32[145,8,256]{2,1,0:T(8,128)}, s32[128]{0:T(128)}, s32[144]{0:T(256)}, /*index=5*/s32[128]{0:T(128)}, s32[1]{0:T(128)}) custom-call(f32[16,1,256]{2,1,0:T(1,128)} %shard_map.151.near, f32[256,8,256]{2,1,0:T(8,128)} %copy-done.1, s32[16]{0:T(128)} %counts.13, ...), custom_call_target="tpu_custom_call" | custom-call | flops 2516582400 | bytes 1048576 | tf_op jit(solution)/shard_map/pallas_call | solution.py:785
  95.6 7.4 %all-to-all-start.2 = ((f32[256,1,256]{2,1,0:T(1,128)}), f32[256,1,256]{2,1,0:T(1,128)S(1)}, u32[]{:S(2)}, u32[]{:S(2)}) async-start(f32[256,1,256]{2,1,0:T(1,128)} %get-tuple-element.29), calls=%async_computation.2 | async-start | bytes 524288 | tf_op jit(solution)/shard_map/all_to_all | solution.py:873
  103.0 3.0 %shard_map.153.far = f32[16,1,256]{2,1,0:T(1,128)} custom-call(f32[16,256,128]{2,1,0:T(8,128)} %get-tuple-element.30.acc1), custom_call_target="tpu_custom_call" | custom-call | flops 1048576 | bytes 2097152 | tf_op jit(solution)/shard_map/pallas_call | solution.py:902
  106.0 7.8 %all-to-all-done.2.back = f32[256,1,256]{2,1,0:T(1,128)S(1)} async-done(((f32[256,1,256]{2,1,0:T(1,128)}), f32[256,1,256]{2,1,0:T(1,128)S(1)}, u32[]{:S(2)}, u32[]{:S(2)}) %all-to-all-start.2) | async-done | bytes 262176 | tf_op jit(solution)/shard_map/all_to_all | solution.py:873
  113.9 0.0 copy-start.2
  113.9 0.7 copy-done.2
  114.6 3.0 %shard_map.154 = (f32[16,256]{1,0:T(8,128)}, f32[16,2,256]{2,1,0:T(2,128)}, f32[256,2,256]{2,1,0:T(2,128)}) custom-call(f32[256,1,256]{2,1,0:T(1,128)} %copy-done.2, s32[256]{0:T(256)} %reshape_squeeze.3.goals, f32[16,1,256]{2,1,0:T(1,128)} %shard_map.151.near, f32[16,1,256]{2,1,0:T(1,128)} %shard_map.153.far, f32[16,256]{1,0:T(8,128)} %energy.3, s32[16]{0:T(128)} %counts.13), custom_call_target="tpu_custom_call" | custom-call | bytes 1048576 | tf_op jit(solution)/shard_map/pallas_call | solution.py:906
  117.6 4.6 %all-to-all-start.3 = ((f32[256,2,256]{2,1,0:T(2,128)}), f32[256,2,256]{2,1,0:T(2,128)S(1)}, u32[]{:S(2)}, u32[]{:S(2)}) async-start(f32[256,2,256]{2,1,0:T(2,128)} %get-tuple-element.33), calls=%async_computation.3 | async-start | bytes 1048576 | tf_op jit(solution)/shard_map/all_to_all | solution.py:873
  122.2 7.0 %shard_map.155 = (bf16[16,24,256]{2,1,0:T(8,128)(2,1)}, f32[16,8,256]{2,1,0:T(8,128)}, f32[16,3,256,128]{3,2,1,0:T(8,128)}, f32[16,256,128]{2,1,0:T(8,128)}) custom-call(f32[16,8,256]{2,1,0:T(8,128)} %get-tuple-element.25.state, f32[16,2,256]{2,1,0:T(2,128)} %get-tuple-element.38.fluid, bf16[16,256,128]{2,1,0:T(8,128)(2,1)} %get-tuple-element.27.cols), custom_call_target="tpu_custom_call" | custom-call | flops 4194304 | bytes 16777216 | tf_op jit(solution)/shard_map/pallas_call | solution.py:814
  129.3 6.6 %all-to-all-done.3.far_fluid = f32[256,2,256]{2,1,0:T(2,128)S(1)} async-done(((f32[256,2,256]{2,1,0:T(2,128)}), f32[256,2,256]{2,1,0:T(2,128)S(1)}, u32[]{:S(2)}, u32[]{:S(2)}) %all-to-all-start.3) | async-done | bytes 524320 | tf_op jit(solution)/shard_map/all_to_all | solution.py:873
  135.9 0.0 copy-start.3
  135.9 0.8 copy-done.3
  136.6 43.7 %shard_map.156 = (f32[16,8,256]{2,1,0:T(8,128)}, f32[256,4,256]{2,1,0:T(4,128)}) custom-call(f32[145,8,256]{2,1,0:T(8,128)} %get-tuple-element.32.blocks, f32[256,2,256]{2,1,0:T(2,128)} %copy-done.3, s32[16]{0:T(128)} %counts.13, s32[128]{0:T(128)} %get-tuple-element.28.slot, s32[128]{0:T(128)} %get-tuple-element.34.offset, s32[144]{0:T(256)} %get-tuple-element.35.block_own, ...), custom_call_target="tpu_custom_call" | custom-call | flops 5033164800 | bytes 1048576 | tf_op jit(solution)/shard_map/pallas_call | solution.py:832
  180.3 8.1 %all-to-all-start.4 = ((f32[256,4,256]{2,1,0:T(4,128)}), f32[256,4,256]{2,1,0:T(4,128)S(1)}, u32[]{:S(2)}, u32[]{:S(2)}) async-start(f32[256,4,256]{2,1,0:T(4,128)} %get-tuple-element.42), calls=%async_computation.4 | async-start | bytes 2097152 | tf_op jit(solution)/shard_map/all_to_all | solution.py:873
  188.4 17.2 %shard_map.157.near = f32[16,8,256]{2,1,0:T(8,128)} custom-call(f32[16,8,256]{2,1,0:T(8,128)} %get-tuple-element.43.after.far, f32[16,8,256]{2,1,0:T(8,128)} %get-tuple-element.25.state, s32[16]{0:T(128)} %counts.13, s32[16]{0:T(128)} %pair_first.3, s32[16]{0:T(128)} %pair_offset.3, bf16[16,256,128]{2,1,0:T(8,128)(2,1)} %get-tuple-element.27.cols, ...), custom_call_target="tpu_custom_call" | custom-call | flops 1258291200 | bytes 1048576 | tf_op jit(solution)/shard_map/pallas_call | solution.py:853
  205.6 1.9 all-to-all-done.4.back
  207.4 1.0 copy-done
  208.4 3.7 %shard_map.158 = (f32[16,4,256]{2,1,0:T(4,128)}, f32[16,9,2,256]{3,2,1,0:T(2,128)}) custom-call(f32[256,4,256]{2,1,0:T(4,128)} %copy-done, s32[256]{0:T(256)} %reshape_squeeze.3.goals, f32[16,8,256]{2,1,0:T(8,128)} %shard_map.157.near, f32[16,8,256]{2,1,0:T(8,128)} %get-tuple-element.43.after.far, f32[16,8,256]{2,1,0:T(8,128)} %get-tuple-element.25.state, ...), custom_call_target="tpu_custom_call" | custom-call | bytes 1048576 | tf_op jit(solution)/shard_map/pallas_call | solution.py:921
  212.1 14.0 %all_to_all.30.came = f32[16,9,2,256]{3,2,1,0:T(2,128)} all-to-all(f32[16,9,2,256]{3,2,1,0:T(2,128)} %get-tuple-element.46), channel_id=1, replica_groups=mesh['rows'=8,'cols'=16] {'cols'}, dimensions={0} | all-to-all | bytes 589824 | tf_op jit(solution)/shard_map/all_to_all | solution.py:873
  226.1 1.8 shard_map.159
  (1 shorter events, 0.0 us)
Async XLA Ops:
  2.9 20.6 %all-to-all-start = ((s32[128,1,128]{2,1,0:T(1,128)}), s32[128,1,128]{2,1,0:T(1,128)S(1)}, u32[]{:S(2)}, u32[]{:S(2)}) async-start(s32[128,1,128]{2,1,0:T(1,128)} %get-tuple-element.26), calls=%async_computation | async-start | bytes 131072 | tf_op jit(solution)/shard_map/all_to_all | solution.py:873
  27.3 34.4 %all-to-all-start.1 = ((f32[256,8,256]{2,1,0:T(8,128)}), f32[256,8,256]{2,1,0:T(8,128)S(1)}, u32[]{:S(2)}, u32[]{:S(2)}) async-start(f32[256,8,256]{2,1,0:T(8,128)} %shard_map.150.after), calls=%async_computation.1 | async-start | bytes 4194304 | tf_op jit(solution)/shard_map/all_to_all | solution.py:873
  61.7 1.3 copy-start.1
  95.6 18.3 %all-to-all-start.2 = ((f32[256,1,256]{2,1,0:T(1,128)}), f32[256,1,256]{2,1,0:T(1,128)S(1)}, u32[]{:S(2)}, u32[]{:S(2)}) async-start(f32[256,1,256]{2,1,0:T(1,128)} %get-tuple-element.29), calls=%async_computation.2 | async-start | bytes 524288 | tf_op jit(solution)/shard_map/all_to_all | solution.py:873
  113.9 0.7 copy-start.2
  117.6 18.2 %all-to-all-start.3 = ((f32[256,2,256]{2,1,0:T(2,128)}), f32[256,2,256]{2,1,0:T(2,128)S(1)}, u32[]{:S(2)}, u32[]{:S(2)}) async-start(f32[256,2,256]{2,1,0:T(2,128)} %get-tuple-element.33), calls=%async_computation.3 | async-start | bytes 1048576 | tf_op jit(solution)/shard_map/all_to_all | solution.py:873
  135.9 0.8 copy-start.3
  180.3 27.1 %all-to-all-start.4 = ((f32[256,4,256]{2,1,0:T(4,128)}), f32[256,4,256]{2,1,0:T(4,128)S(1)}, u32[]{:S(2)}, u32[]{:S(2)}) async-start(f32[256,4,256]{2,1,0:T(4,128)} %get-tuple-element.42), calls=%async_computation.4 | async-start | bytes 2097152 | tf_op jit(solution)/shard_map/all_to_all | solution.py:873
  207.4 1.0 copy-start

commit v8 on v7

--- a/solution.py
+++ b/solution.py
@@ -21,7 +21,8 @@
 CHUNK = 32
 ROWS = (128, 160, 192, 224, 256)
 BLOCKS = SEND + CELLS
-RING = 8
+WIDE = 4
+RING = 4 * WIDE
 
 f32, bf16, i32 = jnp.float32, jnp.bfloat16, jnp.int32
 VMEM = pl.BlockSpec(memory_space=pltpu.VMEM)
@@ -147,37 +148,44 @@
         low = rows
 
 
-def pipeline(first, count, rows_of, prepare, load, combine, store, work):
-    last = first + count - 1
+def pipeline(count, rows_of, prepare, load, work, combine=None, store=None):
+    last = count - 1
 
     def clamp(p):
         return jnp.minimum(p, last)
 
-    for k in range(3):
-        prepare(clamp(first + k))
-    load(first, 0)
+    for k in range(2 * WIDE):
+        prepare(clamp(k))
+    for k in range(WIDE):
+        load(clamp(k), k)
 
     def body(t, _):
-        p = first + 2 * t
+        p = WIDE * t
+        need = rows_of(p)
+        for k in range(1, WIDE):
+            need = jnp.maximum(need, rows_of(p + k))
 
         def step(rows):
-            before = jnp.maximum(p - 1, first)
-            sums = combine(before, 1)
-            work(p, 0, rows)
-            load(p + 1, 1)
-            sums0 = combine(p, 0)
-            work(p + 1, 1, rows)
-            load(clamp(p + 2), 0)
-            store(before, sums, t > 0)
-            store(p, sums0, True)
-            prepare(clamp(p + 3))
-            prepare(clamp(p + 4))
-
-        by_rows(jnp.maximum(rows_of(p), rows_of(p + 1)), step)
-        return 0
-
-    lax.fori_loop(0, count // 2, body, 0)
-    store(last, combine(last, 1), True)
+            before = jnp.maximum(p - 1, 0)
+            done = []
+            if combine is not None:
+                done.append((before, combine(before, WIDE - 1), t > 0))
+            for k in range(WIDE):
+                work(p + k, k, rows)
+                load(clamp(p + WIDE + k), k)
+                if combine is not None and k < WIDE - 1:
+                    done.append((p + k, combine(p + k, k), True))
+            for item in done:
+                store(*item)
+            for k in range(WIDE):
+                prepare(clamp(p + 2 * WIDE + k))
+
+        by_rows(need, step)
+        return 0
+
+    lax.fori_loop(0, count // WIDE, body, 0)
+    if combine is not None:
+        store(last, combine(last, WIDE - 1), True)
 
 
 def keep_sums(acc1, acc2, a, s, sums, valid):
@@ -224,8 +232,9 @@
         return 0
 
     lax.fori_loop(0, SEND, shift, 0, unroll=8)
-    block_own[total] = block_own[total - 1]
-    return total + lax.rem(total, 2)
+    for k in range(WIDE - 1):
+        block_own[jnp.minimum(total + k, BLOCKS - 1)] = block_own[total - 1]
+    return (total + WIDE - 1) // WIDE * WIDE
 
 
 def pack(target, rows, offset, n):
@@ -303,30 +312,7 @@
             second += jnp.sum(other.reshape(CHUNK // 8, 8, PART), axis=0)
         acc2[ps(p)] += jnp.sum(second, axis=0, keepdims=True)
 
-    last = count - 1
-
-    def clamp(p):
-        return jnp.minimum(p, last)
-
-    for k in range(3):
-        prepare(clamp(k))
-    load(0, 0)
-
-    def body(t, _):
-        p = 2 * t
-
-        def step(rows):
-            load(p + 1, 1)
-            work(p, 0, rows)
-            work(p + 1, 1, rows)
-            load(clamp(p + 2), 0)
-            prepare(clamp(p + 3))
-            prepare(clamp(p + 4))
-
-        by_rows(jnp.maximum(counts[pa(p)], counts[pa(p + 1)]), step)
-        return 0
-
-    lax.fori_loop(0, count // 2, body, 0)
+    pipeline(count, lambda p: counts[pa(p)], prepare, load, work)
 
 
 def column_sums(x):
@@ -393,7 +379,7 @@
 
 def own_density_kernel(
     after, state, cols, counts, pair_first, pair_offset, near,
-    acc1, acc2, bh, bm, bf, hj, mj, dist0, dist1, pa, po, ps,
+    acc1, acc2, bh, bm, bf, hj, mj, pa, po, ps, *dist,
 ):
     del after
     expand(cols, bh, bm)
@@ -407,7 +393,7 @@
     own_lists(pair_first, pair_offset, pa, po, ps, CELLS)
     acc1[...] = jnp.zeros_like(acc1)
     acc2[...] = jnp.zeros_like(acc2)
-    refs = (bf, hj, mj, cols, bh, bm, (dist0, dist1))
+    refs = (bf, hj, mj, cols, bh, bm, dist)
     density_pairs(
         CELLS + PAIRS, counts, lambda p: pa[p], lambda p: po[p], lambda p: ps[p], refs,
         lambda p: None, acc1, acc2,
@@ -423,7 +409,7 @@
 def far_density_kernel(
     near, far, counts, slot, proxy_cell, cols,
     acc1, ret, blocks, offset, block_own, live, size,
-    acc2, bh, bm, bf, hj, mj, dist0, dist1, filled,
+    acc2, bh, bm, bf, hj, mj, filled, *dist,
 ):
     del near
     total = pack_plan(far, slot, proxy_cell, offset, block_own, live, filled)
@@ -439,7 +425,7 @@
     lax.fori_loop(0, SEND, fill, 0, unroll=8)
     acc2[...] = jnp.zeros_like(acc2)
     acc1[...] = jnp.zeros_like(acc1)
-    refs = (bf, hj, mj, cols, bh, bm, (dist0, dist1))
+    refs = (bf, hj, mj, cols, bh, bm, dist)
     same = lambda p: p
     density_pairs(
         total, counts, lambda p: block_own[p], same, same, refs,
@@ -540,7 +526,7 @@
     return first[:, 0:PART] + first[:, PART:], second
 
 
-def full_force(first, count, counts, pa, po, refs, prepare, store):
+def full_force(count, counts, pa, po, refs, prepare, store):
     bd, bs, own_cf, other_cf, cols, bh, row, col, dist, appr, ws = refs
 
     def load(p, side):
@@ -564,7 +550,7 @@
     def combine(p, side):
         return force_combine(own_cf[pa(p)], other_cf[po(p)], ws[side])
 
-    pipeline(first, count, lambda p: counts[pa(p)], prepare, load, combine, store, work)
+    pipeline(count, lambda p: counts[pa(p)], prepare, load, work, combine, store)
 
 
 def geometry_prepare(o, rows, bd, bs):
@@ -620,7 +606,7 @@
 
 def own_force_kernel(
     after, state, counts, pair_first, pair_offset, cols, cf, row, col, bh, total,
-    acc1, acc2, bd, bs, dist0, dist1, appr0, appr1, ws0, ws1, pa, po, ps,
+    acc1, acc2, bd, bs, pa, po, ps, *wide,
 ):
     del after
     bd[...] = jnp.zeros_like(bd)
@@ -634,22 +620,29 @@
     own_lists(pair_first, pair_offset, pa, po, ps, CELLS)
     acc1[...] = jnp.zeros_like(acc1)
     acc2[...] = jnp.zeros_like(acc2)
-    ws0[...] = jnp.zeros_like(ws0)
-    ws1[...] = jnp.zeros_like(ws1)
-    refs = (bd, bs, cf, cf, cols, bh, row, col, (dist0, dist1), (appr0, appr1), (ws0, ws1))
+    dist, appr, ws = wide[:WIDE], wide[WIDE : 2 * WIDE], wide[2 * WIDE :]
+    for part in ws:
+        part[...] = jnp.zeros_like(part)
+    refs = (bd, bs, cf, cf, cols, bh, row, col, dist, appr, ws)
     full_force(
-        0, CELLS + PAIRS, counts, lambda p: pa[p], lambda p: po[p], refs, lambda p: None,
+        CELLS + PAIRS, counts, lambda p: pa[p], lambda p: po[p], refs, lambda p: None,
         lambda p, sums, valid: keep_sums(acc1, acc2, pa[p], ps[p], sums, valid),
     )
     total[...] = acc1[...] + acc2[0:CELLS]
 
 
 def far_force_kernel(
-    blocks, far_fluid, counts, slot, offset, block_own, live, size, cols, own_cf, col, bh,
+    blocks, far_fluid, counts, slot, offset, block_own, live, size, cols, own_cf, col_far, bh_far,
     acc1, ret,
-    acc2, fluids, bd, bs, cf, row, dist0, dist1, appr0, appr1, ws0, ws1,
+    acc2, fluids, bd, bs, cf, row, col, bh, sems, *wide,
 ):
     total = size[0]
+    copies = [
+        pltpu.make_async_copy(col_far, col, sems.at[0]),
+        pltpu.make_async_copy(bh_far, bh, sems.at[1]),
+    ]
+    for copy in copies:
+        copy.start()
     bd[...] = jnp.zeros_like(bd)
     bs[...] = jnp.zeros_like(bs)
     fluids[...] = jnp.ones_like(fluids)
@@ -660,8 +653,9 @@
 
     lax.fori_loop(0, SEND, fill, 0, unroll=8)
     acc1[...] = jnp.zeros_like(acc1)
-    ws0[...] = jnp.zeros_like(ws0)
-    ws1[...] = jnp.zeros_like(ws1)
+    dist, appr, ws = wide[:WIDE], wide[WIDE : 2 * WIDE], wide[2 * WIDE :]
+    for part in ws:
+        part[...] = jnp.zeros_like(part)
 
     def prepare(p):
         rows = blocks[p]
@@ -675,10 +669,12 @@
         acc2[p] = force_sums(blocks[p], second)
 
     refs = (
-        bd, bs, own_cf, cf, cols, bh, row, col, (dist0, dist1), (appr0, appr1), (ws0, ws1),
-    )
+        bd, bs, own_cf, cf, cols, bh, row, col, dist, appr, ws,
+    )
+    for copy in copies:
+        copy.wait()
     same = lambda p: p
-    full_force(0, total, counts, lambda p: block_own[p], same, refs, prepare, store)
+    full_force(total, counts, lambda p: block_own[p], same, refs, prepare, store)
 
     def back(e, _):
         ret[slot[e]] = unpack(acc2, offset[e])
@@ -744,8 +740,8 @@
     return pltpu.SMEM(dims, i32)
 
 
-WS = [vmem(2 * PART, PART, dtype=bf16)] * 2
-SQUARE = [vmem(PART, PART)] * 2
+WS = [vmem(2 * PART, PART, dtype=bf16)] * WIDE
+SQUARE = [vmem(PART, PART)] * WIDE
 
 
 def cell_state(position, velocity, mass, smoothing, counts):
@@ -774,8 +770,8 @@
             vmem(CELLS, 1, PART),
             vmem(CELLS, 1, PART),
         ]
-        + SQUARE
-        + [smem(CELLS + PAIRS)] * 3,
+        + [smem(CELLS + PAIRS)] * 3
+        + SQUARE,
         flops=32 * PART * PART * 300,
         moved=2**20,
     )(after, state, cols, counts, pair_first, pair_offset)
@@ -803,8 +799,8 @@
             vmem(BLOCKS, 1, PART),
             vmem(BLOCKS, 1, PART),
         ]
-        + SQUARE
-        + [smem(CELLS)],
+        + [smem(CELLS)]
+        + SQUARE,
         flops=128 * PART * PART * 300,
         moved=2**20,
     )(near, far, counts, slot, proxy_cell, cols)
@@ -832,7 +828,7 @@
     return kernel_call(
         far_force_kernel,
         (shape(CELLS, 8, PART), shape(far_fluid.shape[0], 4, PART)),
-        [VMEM] * 2 + [SMEM] * 6 + [VMEM] * 4,
+        [VMEM] * 2 + [SMEM] * 6 + [VMEM] * 2 + [ANY] * 2,
         (VMEM, VMEM),
         [
             vmem(BLOCKS + 1, 4, PART),
@@ -841,6 +837,9 @@
             vmem(RING, 128, PART, dtype=bf16),
             vmem(BLOCKS, 24, PART, dtype=bf16),
             vmem(BLOCKS, 8, PART),
+            vmem(CELLS, 3, PART, 128),
+            vmem(CELLS, PART, 128),
+            pltpu.SemaphoreType.DMA((2,)),
         ]
         + SQUARE * 2
         + WS,
@@ -861,9 +860,9 @@
             vmem(CELLS, 128, PART, dtype=bf16),
             vmem(CELLS, 128, PART, dtype=bf16),
         ]
+        + [smem(CELLS + PAIRS)] * 3
         + SQUARE * 2
-        + WS
-        + [smem(CELLS + PAIRS)] * 3,
+        + WS,
         flops=32 * PART * PART * 600,
         moved=2**20,
     )(after, state, counts, pair_first, pair_offset, cols, cf, row, col, bh)

time: 228 us -> 224 us (0.982)
  starting transfers between devices: 35.8 us -> 32.7 us
    all_to_all x5, starting transfers between devices: 35.8 us -> 32.7 us  [exchange(): return lax.all_to_all(x, axes, split_axis=0, concat_axis=0, tiled=True)]
where the time goes in v8:
time: 224 us; the launch traced here: 223 us
  Pallas kernels  131 us (58%)
  waiting for transfers between devices  39.9 us (18%)
  starting transfers between devices  32.7 us (15%)
  blocking collectives  14.4 us (6%)
  local copies, waits for them, and re-layouts  4.7 us (2%)
    pallas_call x1, Pallas kernels, far_force(): kernel_call(far_force_kernel, (shape(CELLS, 8, PART), shape(far_fluid.sha...  43.2 us
    all_to_all x5, waiting for transfers between devices, exchange(): return lax.all_to_all(x, axes, split_axis=0, concat_axis=0, tiled=True)  39.9 us
    all_to_all x5, starting transfers between devices, exchange(): return lax.all_to_all(x, axes, split_axis=0, concat_axis=0, tiled=True)  32.7 us
    pallas_call x1, Pallas kernels, far_density(): kernel_call(far_density_kernel, (shape(CELLS, PART, 128), shape(far.shape...  31.4 us
    pallas_call x1, Pallas kernels, own_force(): kernel_call(own_force_kernel, shape(CELLS, 8, PART), [ANY, VMEM] + [SMEM]...  17.9 us
    all_to_all x1, blocking collectives, exchange(): return lax.all_to_all(x, axes, split_axis=0, concat_axis=0, tiled=True)  14.4 us
    pallas_call x1, Pallas kernels, own_density(): kernel_call(own_density_kernel, shape(CELLS, 1, PART), [ANY] + [VMEM] * 2...  12 us
    pallas_call x1, Pallas kernels, own_fluid(): kernel_call(fluid_kernel, (shape(CELLS, 24, PART, dtype=bf16), shape(CELL...  7.04 us
  transfers between devices with their start and end apart: 5, of which 5 were waited for; matrix products, arithmetic and copies ran while one was open for 0% of the time, Pallas kernels for 19%

profile of v8, /device:TPU:0, one launch (start us, length us, event | category | flops | bytes accessed | tf_op | source)
XLA Modules:
  0.0 223.2 jit_solution(1765456853460751827)
XLA Ops:
  0.6 2.2 shard_map.149
  2.9 11.1 %all-to-all-start = ((s32[128,1,128]{2,1,0:T(1,128)}), s32[128,1,128]{2,1,0:T(1,128)S(1)}, u32[]{:S(2)}, u32[]{:S(2)}) async-start(s32[128,1,128]{2,1,0:T(1,128)} %get-tuple-element.26), calls=%async_computation | async-start | bytes 131072 | tf_op jit(solution)/shard_map/all_to_all | solution.py:872
  14.0 2.5 %shard_map.148 = (f32[16,8,256]{2,1,0:T(8,128)}, bf16[16,256,128]{2,1,0:T(8,128)(2,1)}) custom-call(f32[3,16,256]{2,1,0:T(8,128)} %bitcast.6, f32[3,16,256]{2,1,0:T(8,128)} %bitcast.7, f32[16,256]{1,0:T(8,128)} %mass.1, f32[16,256]{1,0:T(8,128)} %smooth.1, s32[16]{0:T(128)} %counts.13), custom_call_target="tpu_custom_call" | custom-call | flops 1048576 | bytes 4194304 | tf_op jit(solution)/shard_map/pallas_call | solution.py:748
  16.6 6.9 %all-to-all-done = s32[128,1,128]{2,1,0:T(1,128)S(1)} async-done(((s32[128,1,128]{2,1,0:T(1,128)}), s32[128,1,128]{2,1,0:T(1,128)S(1)}, u32[]{:S(2)}, u32[]{:S(2)}) %all-to-all-start) | async-done | bytes 65568 | tf_op jit(solution)/shard_map/all_to_all | solution.py:872
  23.4 0.2 slice_reduce_fusion
  23.6 0.7 reshape_squeeze.3.goals
  24.3 3.0 %shard_map.150.after = f32[256,8,256]{2,1,0:T(8,128)} custom-call(f32[16,8,256]{2,1,0:T(8,128)} %get-tuple-element.25.state, s32[256]{0:T(256)} %reshape_squeeze.3.goals), custom_call_target="tpu_custom_call" | custom-call | bytes 4194304 | tf_op jit(solution)/shard_map/pallas_call | solution.py:895
  27.3 4.6 %all-to-all-start.1 = ((f32[256,8,256]{2,1,0:T(8,128)}), f32[256,8,256]{2,1,0:T(8,128)S(1)}, u32[]{:S(2)}, u32[]{:S(2)}) async-start(f32[256,8,256]{2,1,0:T(8,128)} %shard_map.150.after), calls=%async_computation.1 | async-start | bytes 4194304 | tf_op jit(solution)/shard_map/all_to_all | solution.py:872
  32.0 12.0 %shard_map.151.near = f32[16,1,256]{2,1,0:T(1,128)} custom-call(f32[256,8,256]{2,1,0:T(8,128)} %shard_map.150.after, f32[16,8,256]{2,1,0:T(8,128)} %get-tuple-element.25.state, bf16[16,256,128]{2,1,0:T(8,128)(2,1)} %get-tuple-element.27.cols, s32[16]{0:T(128)} %counts.13, s32[16]{0:T(128)} %pair_first.3, s32[16]{0:T(128)} %pair_offset.3), custom_call_target="tpu_custom_call" | custom-call | flops 629145600 | bytes 1048576 | tf_op jit(solution)/shard_map/pallas_call | solution.py:759
  44.0 17.7 %all-to-all-done.1.far = f32[256,8,256]{2,1,0:T(8,128)S(1)} async-done(((f32[256,8,256]{2,1,0:T(8,128)}), f32[256,8,256]{2,1,0:T(8,128)S(1)}, u32[]{:S(2)}, u32[]{:S(2)}) %all-to-all-start.1) | async-done | bytes 2097184 | tf_op jit(solution)/shard_map/all_to_all | solution.py:872
  61.7 0.0 copy-start.1
  61.7 1.3 copy-done.1
  63.0 31.4 %shard_map.152 = (f32[16,256,128]{2,1,0:T(8,128)}, f32[256,1,256]{2,1,0:T(1,128)}, f32[145,8,256]{2,1,0:T(8,128)}, s32[128]{0:T(128)}, s32[144]{0:T(256)}, /*index=5*/s32[128]{0:T(128)}, s32[1]{0:T(128)}) custom-call(f32[16,1,256]{2,1,0:T(1,128)} %shard_map.151.near, f32[256,8,256]{2,1,0:T(8,128)} %copy-done.1, s32[16]{0:T(128)} %counts.13, ...), custom_call_target="tpu_custom_call" | custom-call | flops 2516582400 | bytes 1048576 | tf_op jit(solution)/shard_map/pallas_call | solution.py:781
  94.4 5.5 %all-to-all-start.2 = ((f32[256,1,256]{2,1,0:T(1,128)}), f32[256,1,256]{2,1,0:T(1,128)S(1)}, u32[]{:S(2)}, u32[]{:S(2)}) async-start(f32[256,1,256]{2,1,0:T(1,128)} %get-tuple-element.29), calls=%async_computation.2 | async-start | bytes 524288 | tf_op jit(solution)/shard_map/all_to_all | solution.py:872
  99.9 3.0 %shard_map.153.far = f32[16,1,256]{2,1,0:T(1,128)} custom-call(f32[16,256,128]{2,1,0:T(8,128)} %get-tuple-element.30.acc1), custom_call_target="tpu_custom_call" | custom-call | flops 1048576 | bytes 2097152 | tf_op jit(solution)/shard_map/pallas_call | solution.py:901
  102.9 7.8 %all-to-all-done.2.back = f32[256,1,256]{2,1,0:T(1,128)S(1)} async-done(((f32[256,1,256]{2,1,0:T(1,128)}), f32[256,1,256]{2,1,0:T(1,128)S(1)}, u32[]{:S(2)}, u32[]{:S(2)}) %all-to-all-start.2) | async-done | bytes 262176 | tf_op jit(solution)/shard_map/all_to_all | solution.py:872
  110.8 0.0 copy-start.2
  110.8 0.7 copy-done.2
  111.5 3.0 %shard_map.154 = (f32[16,256]{1,0:T(8,128)}, f32[16,2,256]{2,1,0:T(2,128)}, f32[256,2,256]{2,1,0:T(2,128)}) custom-call(f32[256,1,256]{2,1,0:T(1,128)} %copy-done.2, s32[256]{0:T(256)} %reshape_squeeze.3.goals, f32[16,1,256]{2,1,0:T(1,128)} %shard_map.151.near, f32[16,1,256]{2,1,0:T(1,128)} %shard_map.153.far, f32[16,256]{1,0:T(8,128)} %energy.3, s32[16]{0:T(128)} %counts.13), custom_call_target="tpu_custom_call" | custom-call | bytes 1048576 | tf_op jit(solution)/shard_map/pallas_call | solution.py:905
  114.5 4.8 %all-to-all-start.3 = ((f32[256,2,256]{2,1,0:T(2,128)}), f32[256,2,256]{2,1,0:T(2,128)S(1)}, u32[]{:S(2)}, u32[]{:S(2)}) async-start(f32[256,2,256]{2,1,0:T(2,128)} %get-tuple-element.33), calls=%async_computation.3 | async-start | bytes 1048576 | tf_op jit(solution)/shard_map/all_to_all | solution.py:872
  119.3 7.0 %shard_map.155 = (bf16[16,24,256]{2,1,0:T(8,128)(2,1)}, f32[16,8,256]{2,1,0:T(8,128)}, f32[16,3,256,128]{3,2,1,0:T(8,128)}, f32[16,256,128]{2,1,0:T(8,128)}) custom-call(f32[16,8,256]{2,1,0:T(8,128)} %get-tuple-element.25.state, f32[16,2,256]{2,1,0:T(2,128)} %get-tuple-element.38.fluid, bf16[16,256,128]{2,1,0:T(8,128)(2,1)} %get-tuple-element.27.cols), custom_call_target="tpu_custom_call" | custom-call | flops 4194304 | bytes 16777216 | tf_op jit(solution)/shard_map/pallas_call | solution.py:810
  126.4 6.6 %all-to-all-done.3.far_fluid = f32[256,2,256]{2,1,0:T(2,128)S(1)} async-done(((f32[256,2,256]{2,1,0:T(2,128)}), f32[256,2,256]{2,1,0:T(2,128)S(1)}, u32[]{:S(2)}, u32[]{:S(2)}) %all-to-all-start.3) | async-done | bytes 524320 | tf_op jit(solution)/shard_map/all_to_all | solution.py:872
  132.9 0.0 copy-start.3
  132.9 0.8 copy-done.3
  133.7 43.2 %shard_map.156 = (f32[16,8,256]{2,1,0:T(8,128)}, f32[256,4,256]{2,1,0:T(4,128)}) custom-call(f32[145,8,256]{2,1,0:T(8,128)} %get-tuple-element.32.blocks, f32[256,2,256]{2,1,0:T(2,128)} %copy-done.3, s32[16]{0:T(128)} %counts.13, s32[128]{0:T(128)} %get-tuple-element.28.slot, s32[128]{0:T(128)} %get-tuple-element.34.offset, s32[144]{0:T(256)} %get-tuple-element.35.block_own, ...), custom_call_target="tpu_custom_call" | custom-call | flops 5033164800 | bytes 1048576 | tf_op jit(solution)/shard_map/pallas_call | solution.py:828
  176.9 6.6 %all-to-all-start.4 = ((f32[256,4,256]{2,1,0:T(4,128)}), f32[256,4,256]{2,1,0:T(4,128)S(1)}, u32[]{:S(2)}, u32[]{:S(2)}) async-start(f32[256,4,256]{2,1,0:T(4,128)} %get-tuple-element.42), calls=%async_computation.4 | async-start | bytes 2097152 | tf_op jit(solution)/shard_map/all_to_all | solution.py:872
  183.5 17.9 %shard_map.157.near = f32[16,8,256]{2,1,0:T(8,128)} custom-call(f32[16,8,256]{2,1,0:T(8,128)} %get-tuple-element.43.after.far, f32[16,8,256]{2,1,0:T(8,128)} %get-tuple-element.25.state, s32[16]{0:T(128)} %counts.13, s32[16]{0:T(128)} %pair_first.3, s32[16]{0:T(128)} %pair_offset.3, bf16[16,256,128]{2,1,0:T(8,128)(2,1)} %get-tuple-element.27.cols, ...), custom_call_target="tpu_custom_call" | custom-call | flops 1258291200 | bytes 1048576 | tf_op jit(solution)/shard_map/pallas_call | solution.py:852
  201.4 0.9 all-to-all-done.4.back
  202.4 1.0 copy-done
  203.3 3.7 %shard_map.158 = (f32[16,4,256]{2,1,0:T(4,128)}, f32[16,9,2,256]{3,2,1,0:T(2,128)}) custom-call(f32[256,4,256]{2,1,0:T(4,128)} %copy-done, s32[256]{0:T(256)} %reshape_squeeze.3.goals, f32[16,8,256]{2,1,0:T(8,128)} %shard_map.157.near, f32[16,8,256]{2,1,0:T(8,128)} %get-tuple-element.43.after.far, f32[16,8,256]{2,1,0:T(8,128)} %get-tuple-element.25.state, ...), custom_call_target="tpu_custom_call" | custom-call | bytes 1048576 | tf_op jit(solution)/shard_map/pallas_call | solution.py:920
  207.0 14.4 %all_to_all.30.came = f32[16,9,2,256]{3,2,1,0:T(2,128)} all-to-all(f32[16,9,2,256]{3,2,1,0:T(2,128)} %get-tuple-element.46), channel_id=1, replica_groups=mesh['rows'=8,'cols'=16] {'cols'}, dimensions={0} | all-to-all | bytes 589824 | tf_op jit(solution)/shard_map/all_to_all | solution.py:872
  221.5 1.8 shard_map.159
  (1 shorter events, 0.0 us)
Async XLA Ops:
  2.9 20.6 %all-to-all-start = ((s32[128,1,128]{2,1,0:T(1,128)}), s32[128,1,128]{2,1,0:T(1,128)S(1)}, u32[]{:S(2)}, u32[]{:S(2)}) async-start(s32[128,1,128]{2,1,0:T(1,128)} %get-tuple-element.26), calls=%async_computation | async-start | bytes 131072 | tf_op jit(solution)/shard_map/all_to_all | solution.py:872
  27.3 34.4 %all-to-all-start.1 = ((f32[256,8,256]{2,1,0:T(8,128)}), f32[256,8,256]{2,1,0:T(8,128)S(1)}, u32[]{:S(2)}, u32[]{:S(2)}) async-start(f32[256,8,256]{2,1,0:T(8,128)} %shard_map.150.after), calls=%async_computation.1 | async-start | bytes 4194304 | tf_op jit(solution)/shard_map/all_to_all | solution.py:872
  61.7 1.3 copy-start.1
  94.4 16.4 %all-to-all-start.2 = ((f32[256,1,256]{2,1,0:T(1,128)}), f32[256,1,256]{2,1,0:T(1,128)S(1)}, u32[]{:S(2)}, u32[]{:S(2)}) async-start(f32[256,1,256]{2,1,0:T(1,128)} %get-tuple-element.29), calls=%async_computation.2 | async-start | bytes 524288 | tf_op jit(solution)/shard_map/all_to_all | solution.py:872
  110.8 0.7 copy-start.2
  114.5 18.4 %all-to-all-start.3 = ((f32[256,2,256]{2,1,0:T(2,128)}), f32[256,2,256]{2,1,0:T(2,128)S(1)}, u32[]{:S(2)}, u32[]{:S(2)}) async-start(f32[256,2,256]{2,1,0:T(2,128)} %get-tuple-element.33), calls=%async_computation.3 | async-start | bytes 1048576 | tf_op jit(solution)/shard_map/all_to_all | solution.py:872
  132.9 0.8 copy-start.3
  176.9 25.4 %all-to-all-start.4 = ((f32[256,4,256]{2,1,0:T(4,128)}), f32[256,4,256]{2,1,0:T(4,128)S(1)}, u32[]{:S(2)}, u32[]{:S(2)}) async-start(f32[256,4,256]{2,1,0:T(4,128)} %get-tuple-element.42), calls=%async_computation.4 | async-start | bytes 2097152 | tf_op jit(solution)/shard_map/all_to_all | solution.py:872
  202.4 1.0 copy-start

commit v9 on v8

--- a/solution.py
+++ b/solution.py
@@ -138,7 +138,7 @@
         out[s] = state[goal]
         return 0
 
-    lax.fori_loop(0, out.shape[0], one, 0, unroll=4)
+    lax.fori_loop(0, out.shape[0], one, 0, unroll=16)
 
 
 def by_rows(need, step):
@@ -196,7 +196,7 @@
     acc2[s] += sums[1]
 
 
-def pack_plan(far, slot, proxy_cell, offset, block_own, live, filled):
+def pack_plan(far, slot, proxy_cell, order, offset, block_own, live, filled):
     def clear(c, _):
         filled[c] = 0
         return 0
@@ -214,7 +214,8 @@
 
     lax.fori_loop(0, SEND, measure, 0, unroll=16)
 
-    def place(c, total):
+    def place(k, total):
+        c = order[k]
         blocks = (filled[c] + PART - 1) // PART
         filled[c] = total * PART
 
@@ -378,10 +379,22 @@
 
 
 def own_density_kernel(
-    after, state, cols, counts, pair_first, pair_offset, near,
+    after, state, cols, counts, pair_first, pair_offset, near, order,
     acc1, acc2, bh, bm, bf, hj, mj, pa, po, ps, *dist,
 ):
     del after
+
+    def rank(c, _):
+        mine = counts[c]
+
+        def ahead(d, n):
+            other = counts[d]
+            return n + jnp.where((other > mine) | ((other == mine) & (d < c)), 1, 0)
+
+        order[lax.fori_loop(0, CELLS, ahead, 0, unroll=8)] = c
+        return 0
+
+    lax.fori_loop(0, CELLS, rank, 0)
     expand(cols, bh, bm)
     bf[...] = jnp.zeros_like(bf)
 
@@ -407,12 +420,12 @@
 
 
 def far_density_kernel(
-    near, far, counts, slot, proxy_cell, cols,
+    near, far, counts, slot, proxy_cell, order, cols,
     acc1, ret, blocks, offset, block_own, live, size,
     acc2, bh, bm, bf, hj, mj, filled, *dist,
 ):
     del near
-    total = pack_plan(far, slot, proxy_cell, offset, block_own, live, filled)
+    total = pack_plan(far, slot, proxy_cell, order, offset, block_own, live, filled)
     size[0] = total
     expand(cols, bh, bm)
     bf[...] = jnp.zeros_like(bf)
@@ -450,7 +463,7 @@
             part[jnp.where(goal < 0, CELLS, goal)] += back[s]
         return 0
 
-    lax.fori_loop(0, back.shape[0] // len(sums), one, 0, unroll=2)
+    lax.fori_loop(0, back.shape[0] // len(sums), one, 0, unroll=8)
 
 
 def combine_density_kernel(
@@ -758,9 +771,9 @@
 def own_density(after, state, cols, counts, pair_first, pair_offset):
     return kernel_call(
         own_density_kernel,
-        shape(CELLS, 1, PART),
+        (shape(CELLS, 1, PART), shape(CELLS, dtype=i32)),
         [ANY] + [VMEM] * 2 + [SMEM] * 3,
-        VMEM,
+        (VMEM, SMEM),
         [
             vmem(CELLS, PART, 128),
             vmem(CELLS + 1, 1, PART),
@@ -777,7 +790,7 @@
     )(after, state, cols, counts, pair_first, pair_offset)
 
 
-def far_density(near, far, counts, slot, proxy_cell, cols):
+def far_density(near, far, counts, slot, proxy_cell, order, cols):
     return kernel_call(
         far_density_kernel,
         (
@@ -789,7 +802,7 @@
             shape(SEND, dtype=i32),
             shape(1, dtype=i32),
         ),
-        [ANY, VMEM] + [SMEM] * 3 + [VMEM],
+        [ANY, VMEM] + [SMEM] * 4 + [VMEM],
         (VMEM,) * 3 + (SMEM,) * 4,
         [
             vmem(BLOCKS + 1, 1, PART),
@@ -803,7 +816,7 @@
         + SQUARE,
         flops=128 * PART * PART * 300,
         moved=2**20,
-    )(near, far, counts, slot, proxy_cell, cols)
+    )(near, far, counts, slot, proxy_cell, order, cols)
 
 
 def own_fluid(state, fluid, cols):
@@ -896,8 +909,8 @@
         respond_kernel, shape(slots, 8, PART), [VMEM, SMEM], VMEM, moved=4 * 2**20
     )(state, goals)
     far = exchange(answer, both)
-    near = own_density(answer, state, cols, counts, pair_first, pair_offset)
-    acc1, ret, *plan = far_density(near, far, counts, slot, proxy_cell, cols)
+    near, order = own_density(answer, state, cols, counts, pair_first, pair_offset)
+    acc1, ret, *plan = far_density(near, far, counts, slot, proxy_cell, order, cols)
     far_sums = kernel_call(
         sums_kernel, shape(CELLS, 1, PART), [VMEM], VMEM, flops=2**20, moved=2**21
     )(acc1)

time: 224 us -> 222 us (level)
  no operation moved by 1% of the time
where the time goes in v9:
time: 222 us; the launch traced here: 223 us
  Pallas kernels  129 us (58%)
  waiting for transfers between devices  39.2 us (18%)
  starting transfers between devices  33.4 us (15%)
  blocking collectives  15.1 us (7%)
  local copies, waits for them, and re-layouts  4.69 us (2%)
    pallas_call x1, Pallas kernels, far_force(): kernel_call(far_force_kernel, (shape(CELLS, 8, PART), shape(far_fluid.sha...  42.3 us
    all_to_all x5, waiting for transfers between devices, exchange(): return lax.all_to_all(x, axes, split_axis=0, concat_axis=0, tiled=True)  39.2 us
    all_to_all x5, starting transfers between devices, exchange(): return lax.all_to_all(x, axes, split_axis=0, concat_axis=0, tiled=True)  33.4 us
    pallas_call x1, Pallas kernels, far_density(): kernel_call(far_density_kernel, (shape(CELLS, PART, 128), shape(far.shape...  30.8 us
    pallas_call x1, Pallas kernels, own_force(): kernel_call(own_force_kernel, shape(CELLS, 8, PART), [ANY, VMEM] + [SMEM]...  17.7 us
    all_to_all x1, blocking collectives, exchange(): return lax.all_to_all(x, axes, split_axis=0, concat_axis=0, tiled=True)  15.1 us
    pallas_call x1, Pallas kernels, own_density(): kernel_call(own_density_kernel, (shape(CELLS, 1, PART), shape(CELLS, dtyp...  12.9 us
    pallas_call x1, Pallas kernels, own_fluid(): kernel_call(fluid_kernel, (shape(CELLS, 24, PART, dtype=bf16), shape(CELL...  7.01 us
  transfers between devices with their start and end apart: 5, of which 5 were waited for; matrix products, arithmetic and copies ran while one was open for 0% of the time, Pallas kernels for 19%

profile of v9, /device:TPU:0, one launch (start us, length us, event | category | flops | bytes accessed | tf_op | source)
XLA Modules:
  0.0 222.6 jit_solution(6191261736321514877)
XLA Ops:
  0.6 2.2 %shard_map.149 = (s32[128,1,128]{2,1,0:T(1,128)}, s32[128]{0:T(128)}) custom-call(s32[128]{0:T(128)} %bitcast.9, s32[128]{0:T(128)} %target.1), custom_call_target="tpu_custom_call" | custom-call | bytes 1048576 | tf_op jit(solution)/shard_map/pallas_call | solution.py:896
  2.9 11.1 %all-to-all-start = ((s32[128,1,128]{2,1,0:T(1,128)}), s32[128,1,128]{2,1,0:T(1,128)S(1)}, u32[]{:S(2)}, u32[]{:S(2)}) async-start(s32[128,1,128]{2,1,0:T(1,128)} %get-tuple-element.28), calls=%async_computation | async-start | bytes 131072 | tf_op jit(solution)/shard_map/all_to_all | solution.py:885
  14.0 2.5 %shard_map.148 = (f32[16,8,256]{2,1,0:T(8,128)}, bf16[16,256,128]{2,1,0:T(8,128)(2,1)}) custom-call(f32[3,16,256]{2,1,0:T(8,128)} %bitcast.6, f32[3,16,256]{2,1,0:T(8,128)} %bitcast.7, f32[16,256]{1,0:T(8,128)} %mass.1, f32[16,256]{1,0:T(8,128)} %smooth.1, s32[16]{0:T(128)} %counts.13), custom_call_target="tpu_custom_call" | custom-call | flops 1048576 | bytes 4194304 | tf_op jit(solution)/shard_map/pallas_call | solution.py:761
  16.6 6.9 %all-to-all-done = s32[128,1,128]{2,1,0:T(1,128)S(1)} async-done(((s32[128,1,128]{2,1,0:T(1,128)}), s32[128,1,128]{2,1,0:T(1,128)S(1)}, u32[]{:S(2)}, u32[]{:S(2)}) %all-to-all-start) | async-done | bytes 65568 | tf_op jit(solution)/shard_map/all_to_all | solution.py:885
  23.4 0.2 slice_reduce_fusion
  23.6 0.7 reshape_squeeze.3.goals
  24.3 2.7 %shard_map.150.after = f32[256,8,256]{2,1,0:T(8,128)} custom-call(f32[16,8,256]{2,1,0:T(8,128)} %get-tuple-element.27.state, s32[256]{0:T(256)} %reshape_squeeze.3.goals), custom_call_target="tpu_custom_call" | custom-call | bytes 4194304 | tf_op jit(solution)/shard_map/pallas_call | solution.py:908
  27.1 4.6 %all-to-all-start.1 = ((f32[256,8,256]{2,1,0:T(8,128)}), f32[256,8,256]{2,1,0:T(8,128)S(1)}, u32[]{:S(2)}, u32[]{:S(2)}) async-start(f32[256,8,256]{2,1,0:T(8,128)} %shard_map.150.after), calls=%async_computation.1 | async-start | bytes 4194304 | tf_op jit(solution)/shard_map/all_to_all | solution.py:885
  31.7 12.9 %shard_map.151 = (f32[16,1,256]{2,1,0:T(1,128)}, s32[16]{0:T(128)}) custom-call(f32[256,8,256]{2,1,0:T(8,128)} %shard_map.150.after, f32[16,8,256]{2,1,0:T(8,128)} %get-tuple-element.27.state, bf16[16,256,128]{2,1,0:T(8,128)(2,1)} %get-tuple-element.29.cols, s32[16]{0:T(128)} %counts.13, s32[16]{0:T(128)} %pair_first.3, s32[16]{0:T(128)} %pair_offset.3), custom_call_target="tpu_custom_call" | custom-call | flops 629145600 | bytes 1048576 | tf_op jit(solution)/shard_map/pallas_call | solution.py:772
  44.6 16.8 %all-to-all-done.1.far = f32[256,8,256]{2,1,0:T(8,128)S(1)} async-done(((f32[256,8,256]{2,1,0:T(8,128)}), f32[256,8,256]{2,1,0:T(8,128)S(1)}, u32[]{:S(2)}, u32[]{:S(2)}) %all-to-all-start.1) | async-done | bytes 2097184 | tf_op jit(solution)/shard_map/all_to_all | solution.py:885
  61.4 0.0 copy-start.1
  61.4 1.3 copy-done.1
  62.8 30.8 %shard_map.152 = (f32[16,256,128]{2,1,0:T(8,128)}, f32[256,1,256]{2,1,0:T(1,128)}, f32[145,8,256]{2,1,0:T(8,128)}, s32[128]{0:T(128)}, s32[144]{0:T(256)}, /*index=5*/s32[128]{0:T(128)}, s32[1]{0:T(128)}) custom-call(f32[16,1,256]{2,1,0:T(1,128)} %get-tuple-element.30.near, f32[256,8,256]{2,1,0:T(8,128)} %copy-done.1, s32[16]{0:T(128)} %counts.13, ...), custom_call_target="tpu_custom_call" | custom-call | flops 2516582400 | bytes 1048576 | tf_op jit(solution)/shard_map/pallas_call | solution.py:794
  93.5 6.0 %all-to-all-start.2 = ((f32[256,1,256]{2,1,0:T(1,128)}), f32[256,1,256]{2,1,0:T(1,128)S(1)}, u32[]{:S(2)}, u32[]{:S(2)}) async-start(f32[256,1,256]{2,1,0:T(1,128)} %get-tuple-element.33), calls=%async_computation.2 | async-start | bytes 524288 | tf_op jit(solution)/shard_map/all_to_all | solution.py:885
  99.6 3.0 %shard_map.153.far = f32[16,1,256]{2,1,0:T(1,128)} custom-call(f32[16,256,128]{2,1,0:T(8,128)} %get-tuple-element.34.acc1), custom_call_target="tpu_custom_call" | custom-call | flops 1048576 | bytes 2097152 | tf_op jit(solution)/shard_map/pallas_call | solution.py:914
  102.6 7.8 %all-to-all-done.2.back = f32[256,1,256]{2,1,0:T(1,128)S(1)} async-done(((f32[256,1,256]{2,1,0:T(1,128)}), f32[256,1,256]{2,1,0:T(1,128)S(1)}, u32[]{:S(2)}, u32[]{:S(2)}) %all-to-all-start.2) | async-done | bytes 262176 | tf_op jit(solution)/shard_map/all_to_all | solution.py:885
  110.5 0.0 copy-start.2
  110.5 0.7 copy-done.2
  111.2 2.9 %shard_map.154 = (f32[16,256]{1,0:T(8,128)}, f32[16,2,256]{2,1,0:T(2,128)}, f32[256,2,256]{2,1,0:T(2,128)}) custom-call(f32[256,1,256]{2,1,0:T(1,128)} %copy-done.2, s32[256]{0:T(256)} %reshape_squeeze.3.goals, f32[16,1,256]{2,1,0:T(1,128)} %get-tuple-element.30.near, f32[16,1,256]{2,1,0:T(1,128)} %shard_map.153.far, f32[16,256]{1,0:T(8,128)} %energy.3, ...), custom_call_target="tpu_custom_call" | custom-call | bytes 1048576 | tf_op jit(solution)/shard_map/pallas_call | solution.py:918
  114.1 4.8 %all-to-all-start.3 = ((f32[256,2,256]{2,1,0:T(2,128)}), f32[256,2,256]{2,1,0:T(2,128)S(1)}, u32[]{:S(2)}, u32[]{:S(2)}) async-start(f32[256,2,256]{2,1,0:T(2,128)} %get-tuple-element.37), calls=%async_computation.3 | async-start | bytes 1048576 | tf_op jit(solution)/shard_map/all_to_all | solution.py:885
  118.9 7.0 %shard_map.155 = (bf16[16,24,256]{2,1,0:T(8,128)(2,1)}, f32[16,8,256]{2,1,0:T(8,128)}, f32[16,3,256,128]{3,2,1,0:T(8,128)}, f32[16,256,128]{2,1,0:T(8,128)}) custom-call(f32[16,8,256]{2,1,0:T(8,128)} %get-tuple-element.27.state, f32[16,2,256]{2,1,0:T(2,128)} %get-tuple-element.42.fluid, bf16[16,256,128]{2,1,0:T(8,128)(2,1)} %get-tuple-element.29.cols), custom_call_target="tpu_custom_call" | custom-call | flops 4194304 | bytes 16777216 | tf_op jit(solution)/shard_map/pallas_call | solution.py:823
  125.9 6.6 %all-to-all-done.3.far_fluid = f32[256,2,256]{2,1,0:T(2,128)S(1)} async-done(((f32[256,2,256]{2,1,0:T(2,128)}), f32[256,2,256]{2,1,0:T(2,128)S(1)}, u32[]{:S(2)}, u32[]{:S(2)}) %all-to-all-start.3) | async-done | bytes 524320 | tf_op jit(solution)/shard_map/all_to_all | solution.py:885
  132.5 0.0 copy-start.3
  132.5 0.8 copy-done.3
  133.3 42.3 %shard_map.156 = (f32[16,8,256]{2,1,0:T(8,128)}, f32[256,4,256]{2,1,0:T(4,128)}) custom-call(f32[145,8,256]{2,1,0:T(8,128)} %get-tuple-element.36.blocks, f32[256,2,256]{2,1,0:T(2,128)} %copy-done.3, s32[16]{0:T(128)} %counts.13, s32[128]{0:T(128)} %get-tuple-element.31.slot, s32[128]{0:T(128)} %get-tuple-element.38.offset, s32[144]{0:T(256)} %get-tuple-element.39.block_own, ...), custom_call_target="tpu_custom_call" | custom-call | flops 5033164800 | bytes 1048576 | tf_op jit(solution)/shard_map/pallas_call | solution.py:841
  175.6 6.7 %all-to-all-start.4 = ((f32[256,4,256]{2,1,0:T(4,128)}), f32[256,4,256]{2,1,0:T(4,128)S(1)}, u32[]{:S(2)}, u32[]{:S(2)}) async-start(f32[256,4,256]{2,1,0:T(4,128)} %get-tuple-element.46), calls=%async_computation.4 | async-start | bytes 2097152 | tf_op jit(solution)/shard_map/all_to_all | solution.py:885
  182.3 17.7 %shard_map.157.near = f32[16,8,256]{2,1,0:T(8,128)} custom-call(f32[16,8,256]{2,1,0:T(8,128)} %get-tuple-element.47.after.far, f32[16,8,256]{2,1,0:T(8,128)} %get-tuple-element.27.state, s32[16]{0:T(128)} %counts.13, s32[16]{0:T(128)} %pair_first.3, s32[16]{0:T(128)} %pair_offset.3, bf16[16,256,128]{2,1,0:T(8,128)(2,1)} %get-tuple-element.29.cols, ...), custom_call_target="tpu_custom_call" | custom-call | flops 1258291200 | bytes 1048576 | tf_op jit(solution)/shard_map/pallas_call | solution.py:865
  200.0 1.1 all-to-all-done.4.back
  201.1 1.0 copy-done
  202.1 3.6 %shard_map.158 = (f32[16,4,256]{2,1,0:T(4,128)}, f32[16,9,2,256]{3,2,1,0:T(2,128)}) custom-call(f32[256,4,256]{2,1,0:T(4,128)} %copy-done, s32[256]{0:T(256)} %reshape_squeeze.3.goals, f32[16,8,256]{2,1,0:T(8,128)} %shard_map.157.near, f32[16,8,256]{2,1,0:T(8,128)} %get-tuple-element.47.after.far, f32[16,8,256]{2,1,0:T(8,128)} %get-tuple-element.27.state, ...), custom_call_target="tpu_custom_call" | custom-call | bytes 1048576 | tf_op jit(solution)/shard_map/pallas_call | solution.py:933
  205.7 15.1 %all_to_all.30.came = f32[16,9,2,256]{3,2,1,0:T(2,128)} all-to-all(f32[16,9,2,256]{3,2,1,0:T(2,128)} %get-tuple-element.50), channel_id=1, replica_groups=mesh['rows'=8,'cols'=16] {'cols'}, dimensions={0} | all-to-all | bytes 589824 | tf_op jit(solution)/shard_map/all_to_all | solution.py:885
  220.8 1.8 shard_map.159
  (1 shorter events, 0.0 us)
Async XLA Ops:
  2.9 20.6 %all-to-all-start = ((s32[128,1,128]{2,1,0:T(1,128)}), s32[128,1,128]{2,1,0:T(1,128)S(1)}, u32[]{:S(2)}, u32[]{:S(2)}) async-start(s32[128,1,128]{2,1,0:T(1,128)} %get-tuple-element.28), calls=%async_computation | async-start | bytes 131072 | tf_op jit(solution)/shard_map/all_to_all | solution.py:885
  27.1 34.4 %all-to-all-start.1 = ((f32[256,8,256]{2,1,0:T(8,128)}), f32[256,8,256]{2,1,0:T(8,128)S(1)}, u32[]{:S(2)}, u32[]{:S(2)}) async-start(f32[256,8,256]{2,1,0:T(8,128)} %shard_map.150.after), calls=%async_computation.1 | async-start | bytes 4194304 | tf_op jit(solution)/shard_map/all_to_all | solution.py:885
  61.4 1.3 copy-start.1
  93.5 16.9 %all-to-all-start.2 = ((f32[256,1,256]{2,1,0:T(1,128)}), f32[256,1,256]{2,1,0:T(1,128)S(1)}, u32[]{:S(2)}, u32[]{:S(2)}) async-start(f32[256,1,256]{2,1,0:T(1,128)} %get-tuple-element.33), calls=%async_computation.2 | async-start | bytes 524288 | tf_op jit(solution)/shard_map/all_to_all | solution.py:885
  110.5 0.7 copy-start.2
  114.1 18.4 %all-to-all-start.3 = ((f32[256,2,256]{2,1,0:T(2,128)}), f32[256,2,256]{2,1,0:T(2,128)S(1)}, u32[]{:S(2)}, u32[]{:S(2)}) async-start(f32[256,2,256]{2,1,0:T(2,128)} %get-tuple-element.37), calls=%async_computation.3 | async-start | bytes 1048576 | tf_op jit(solution)/shard_map/all_to_all | solution.py:885
  132.5 0.8 copy-start.3
  175.6 25.6 %all-to-all-start.4 = ((f32[256,4,256]{2,1,0:T(4,128)}), f32[256,4,256]{2,1,0:T(4,128)S(1)}, u32[]{:S(2)}, u32[]{:S(2)}) async-start(f32[256,4,256]{2,1,0:T(4,128)} %get-tuple-element.46), calls=%async_computation.4 | async-start | bytes 2097152 | tf_op jit(solution)/shard_map/all_to_all | solution.py:885
  201.1 1.0 copy-start
